TPU v7x, 32 devices: a whole 2x2x4 slice. The times are simulated.
32 devices in a mesh: rep: 2 (over y), ctx: 4 (over z), ch: 2 (over x), sub: 2 (over core).
Axes of the slice: x: 2, y: 2, z: 4, core: 2. Of those that a mesh axis runs over, the one named last changes fastest.
Arguments:
- hyena_query: bfloat16 [3072, 8192], P(('rep', 'ctx'), ('ch', 'sub')), parts along dimension 0, may hold values from -6 to 6
- hyena_key: bfloat16 [3072, 8192], P(('rep', 'ctx'), ('ch', 'sub')), parts along dimension 0, may hold values from -6 to 6
- hyena_value: bfloat16 [3072, 8192], P(('rep', 'ctx'), ('ch', 'sub')), parts along dimension 0, may hold values from -6 to 6
- filters: bfloat16 [512, 128], P(('ch', 'sub')), may hold values from -0.5 to 0.5
- skip_gain: float32 [8192], P(('ch', 'sub')), may hold values from 0.5 to 1.5
- attn_query: bfloat16 [3072, 8192], P(('rep', 'ctx'), ('ch', 'sub')), parts along dimension 0, may hold values from -40 to 40
- attn_key: bfloat16 [3072, 8192], P(('rep', 'ctx'), ('ch', 'sub')), parts along dimension 0, may hold values from -5 to 5
- genome_starts: int32 [8], P('rep'), parts along dimension 0, may hold values from 0 to 1408, as said below
Outputs:
- hyena_mix: bfloat16 [3072, 8192], P(('rep', 'ctx'), ('ch', 'sub')), parts along dimension 0
- attended: bfloat16 [3072, 8192], P(('rep', 'ctx'), ('ch', 'sub')), parts along dimension 0
There are 2 independent parts, one for each index of `rep`. A program takes and returns all parts, laid end to end along the dimension named above; an argument that names none is the same for every part. Nothing has to cross between parts.
Inputs may be any that keep to these rules, and one draw needn't show every extreme that they name: genome_starts[0] is 0; the entries rise, each by 128 or more, and the last genome holds exactly 128 positions.
All inputs are finite; a program needn't handle non-finite values.
Results may differ from a plain program's by a relative error of at most 0.0059.
Values may be sent and summed in bfloat16 or wider, within the bound.
No kernel may reach another device: no remote copies, remote signals or barrier semaphores. Data moves between devices by JAX's collectives and lax.ppermute only.
A program may use at most 128 MiB of HBM per device.

v0:
```python
from functools import partial
import math

import jax
import jax.numpy as jnp
from jax import lax
from jax.experimental import pallas as pl
from jax.experimental.pallas import tpu as pltpu
from jax.sharding import PartitionSpec as P

HEAD_DIM = 128
BLOCK = 128
FAR = -1e30
TO_LOG2 = math.log2(math.e) / math.sqrt(HEAD_DIM)
VMEM_LIMIT = 48 * 1024 * 1024
STAT_ROWS = 32


def begin_of(pos, starts):
    begin = jnp.zeros_like(pos)
    for start in starts:
        begin = jnp.where(pos >= start, start, begin)
    return begin


def compiler_params():
    return pltpu.CompilerParams(vmem_limit_bytes=VMEM_LIMIT)


def rounded_product(key, value):
    return (key.astype(jnp.float32) * value.astype(jnp.float32)).astype(jnp.bfloat16)


def halo_kernel(hk, hv, out):
    out[...] = rounded_product(hk[...], hv[...])


def halo_product(hk, hv):
    rows, channels = hk.shape
    width = min(channels, 512)
    last = pl.BlockSpec((BLOCK, width), lambda j: (rows // BLOCK - 1, j))
    return pl.pallas_call(
        halo_kernel,
        grid=(channels // width,),
        in_specs=[last, last],
        out_specs=pl.BlockSpec((BLOCK, width), lambda j: (0, j)),
        out_shape=jax.ShapeDtypeStruct((BLOCK, channels), jnp.bfloat16),
        compiler_params=compiler_params(),
        cost_estimate=pl.CostEstimate(
            flops=BLOCK * channels, bytes_accessed=6 * BLOCK * channels, transcendentals=0
        ),
        name="halo_product",
    )(hk, hv)


def hyena_kernel(genomes, group, info, hq, hk, hv, halo, filters, gain, out, lines, ext, tall):
    rows, width = out.shape
    blocks = rows // BLOCK
    groups = width // group
    starts = [info[i] for i in range(genomes)]
    step = pl.program_id(0)
    first = lax.axis_index("ctx") * rows

    @pl.when(step == 0)
    def _():
        tap = lax.broadcasted_iota(jnp.int32, (BLOCK, BLOCK), 0)
        col = lax.broadcasted_iota(jnp.int32, (BLOCK, BLOCK), 1)
        turn = jnp.where((tap + col) % BLOCK == 0, 1.0, 0.0).astype(jnp.bfloat16)
        lines[...] = jnp.dot(filters[...], turn, preferred_element_type=jnp.float32)

    ext[:BLOCK] = halo[...]
    ext[BLOCK:] = rounded_product(hk[...], hv[...])
    ours = lines[pl.ds(pl.multiple_of(step * groups, groups), groups), :]
    row = lax.broadcasted_iota(jnp.int32, (BLOCK, BLOCK), 0)
    col = lax.broadcasted_iota(jnp.int32, (BLOCK, BLOCK), 1)
    before = jnp.where(col > row, 1.0, 0.0).astype(jnp.bfloat16)
    within = jnp.where(col <= row, 1.0, 0.0).astype(jnp.bfloat16)
    for g in range(groups):
        line = jnp.broadcast_to(ours[g : g + 1, :], (BLOCK, BLOCK))
        circulant = pltpu.roll(line, 0, 1, stride=1, stride_axis=0).astype(jnp.bfloat16)
        at = slice(g * BLOCK, (g + 1) * BLOCK)
        tall[at, :BLOCK] = circulant * before
        tall[at, BLOCK:] = circulant * within
    lane_group = lax.broadcasted_iota(jnp.int32, (BLOCK, width), 1) // group

    def finish(b, parts):
        filtered = parts[0]
        for g in range(1, groups):
            filtered = jnp.where(lane_group == g, parts[g], filtered)
        at = pl.ds(b * BLOCK, BLOCK)
        direct = ext[(b + 1) * BLOCK : (b + 2) * BLOCK, :].astype(jnp.float32)
        mix = hq[at, :].astype(jnp.float32) * (filtered + gain[...] * direct)
        out[at, :] = mix.astype(jnp.bfloat16)

    for b in range(blocks):
        here = first + b * BLOCK
        window = ext[b * BLOCK : (b + 2) * BLOCK, :]
        cut = begin_of(here + BLOCK - 1, starts) > here - BLOCK

        @pl.when(jnp.logical_not(cut))
        def _():
            finish(
                b,
                [
                    jnp.dot(
                        tall[g * BLOCK : (g + 1) * BLOCK, :],
                        window,
                        preferred_element_type=jnp.float32,
                    )
                    for g in range(groups)
                ],
            )

        @pl.when(cut)
        def _():
            row = here + lax.broadcasted_iota(jnp.int32, (BLOCK, 2 * BLOCK), 0)
            col = here - BLOCK + lax.broadcasted_iota(jnp.int32, (BLOCK, 2 * BLOCK), 1)
            seen = jnp.where(col >= begin_of(row, starts), 1.0, 0.0).astype(jnp.bfloat16)
            finish(
                b,
                [
                    jnp.dot(
                        tall[g * BLOCK : (g + 1) * BLOCK, :] * seen,
                        window,
                        preferred_element_type=jnp.float32,
                    )
                    for g in range(groups)
                ],
            )


def hyena(starts, hq, hk, hv, halo, filters, gain):
    rows, channels = hk.shape
    group = channels // filters.shape[0]
    here = lambda r: pl.BlockSpec((r, BLOCK), lambda j: (0, j))
    return pl.pallas_call(
        partial(hyena_kernel, starts.shape[0], group),
        grid=(channels // BLOCK,),
        in_specs=[
            pl.BlockSpec(memory_space=pltpu.SMEM),
            here(rows),
            here(rows),
            here(rows),
            here(BLOCK),
            pl.BlockSpec(filters.shape, lambda j: (0, 0)),
            here(1),
        ],
        out_specs=here(rows),
        out_shape=jax.ShapeDtypeStruct((rows, channels), jnp.bfloat16),
        scratch_shapes=[
            pltpu.VMEM((filters.shape[0], BLOCK), jnp.float32),
            pltpu.VMEM((rows + BLOCK, BLOCK), jnp.bfloat16),
            pltpu.VMEM((BLOCK // group * BLOCK, 2 * BLOCK), jnp.bfloat16),
        ],
        compiler_params=compiler_params(),
        cost_estimate=pl.CostEstimate(
            flops=2 * rows * channels * 2 * BLOCK * 8,
            bytes_accessed=2 * rows * channels * 4,
            transcendentals=0,
        ),
        name="hyena_mix",
    )(starts, hq, hk, hv, halo, filters, gain)


def one_of(flags, me):
    on = me < 0
    for d, flag in enumerate(flags):
        if flag:
            on = on | (me == d)
    return on


def attend_kernel(genomes, plan, info, q, k, v, *rest):
    rows = q.shape[0]
    me = lax.axis_index("ctx")
    own = me * rows
    rest = list(rest)
    turned, wide = rest[-2:]
    jobs = [(rows, q, own, None)]
    if plan.na:
        jobs.append((plan.na, rest.pop(0), own + rows, one_of(plan.a_to, me)))
    if plan.nb:
        jobs.append((plan.nb, rest.pop(0), own + 2 * rows, one_of(plan.b_to, me)))
    rk, rv = (rest.pop(0), rest.pop(0)) if plan.nk else (None, None)
    out, stats = rest.pop(0), rest.pop(0)
    outs = [out] + rest[: len(jobs) - 1]
    starts = [info[i] for i in range(genomes)]

    turned[:, :rows] = k[...].T
    wide[:rows, :HEAD_DIM] = v[...]
    if plan.nk:
        turned[:, rows:] = rk[...].T
        wide[rows:, :HEAD_DIM] = rv[...]
    wide[:, HEAD_DIM:] = jnp.ones((rows + plan.nk, HEAD_DIM), jnp.bfloat16)

    def seen(row_at, count, col_at, columns):
        row = row_at + lax.broadcasted_iota(jnp.int32, (count, columns), 0)
        col = col_at + lax.broadcasted_iota(jnp.int32, (count, columns), 1)
        begin = begin_of(row_at + lax.broadcasted_iota(jnp.int32, (count, 1), 0), starts)
        return (col <= row) & (col >= begin)

    def piece(queries, out, count, row_at, far, put):
        keys = rows + plan.nk if far else rows
        scores = jnp.dot(queries[...], turned[:, :keys], preferred_element_type=jnp.float32)
        visible = seen(row_at, count, own, rows)
        if far:
            other = seen(row_at, count, own - plan.nk, plan.nk)
            visible = jnp.concatenate([visible, other], axis=1)
        scores = jnp.where(visible, scores, FAR)
        top = jnp.max(scores, axis=1, keepdims=True)
        weights = jnp.exp2((scores - top) * TO_LOG2).astype(jnp.bfloat16)
        mixed = jnp.dot(weights, wide[:keys, :], preferred_element_type=jnp.float32)
        total = mixed[:, HEAD_DIM:]
        out[:count, :] = (mixed[:, :HEAD_DIM] / total).astype(jnp.bfloat16)
        put(as_rows(top * TO_LOG2 + jnp.log2(total)))

    for (count, queries, at, on), out in zip(jobs, outs):
        if on is None:
            put = partial(stats.__setitem__, ...)
        else:
            put = partial(carry, out, count)

        begin = begin_of(at, starts)
        on = True if on is None else on & (begin < own + rows)
        near_only = on
        if plan.nk:
            far = on & (begin < own) & one_of(plan.k_to, me)
            near_only = on & jnp.logical_not(far)

            @pl.when(far)
            def _():
                piece(queries, out, count, at, True, put)

        if near_only is True:
            piece(queries, out, count, at, False, put)
        else:

            @pl.when(near_only)
            def _():
                piece(queries, out, count, at, False, put)

        if on is not True:

            @pl.when(jnp.logical_not(on))
            def _():
                out[:count, :] = jnp.zeros((count, HEAD_DIM), jnp.bfloat16)
                put(jnp.full((8, BLOCK), FAR, jnp.float32))


def as_rows(column):
    row = lax.broadcasted_iota(jnp.int32, (BLOCK, BLOCK), 0)
    lane = lax.broadcasted_iota(jnp.int32, (BLOCK, BLOCK), 1)
    rows = [
        jnp.sum(jnp.where(row == lane, column[i : i + BLOCK], 0.0), axis=0, keepdims=True)
        for i in range(0, column.shape[0], BLOCK)
    ]
    return jnp.concatenate(rows + [jnp.zeros_like(rows[0])] * (8 - len(rows)))


def carry(out, count, stat):
    high = stat.astype(jnp.bfloat16).astype(jnp.float32)
    middle = (stat - high).astype(jnp.bfloat16).astype(jnp.float32)
    low = stat - high - middle
    parts = jnp.concatenate([high, middle, low, jnp.zeros_like(low)])
    out[count:, :] = parts.astype(jnp.bfloat16)


def attend(plan, starts, q, k, v, qa, qb, rk, rv, first, heads):
    rows = q.shape[0]
    here = lambda r: pl.BlockSpec((r, HEAD_DIM), lambda h: (0, h))
    whole = lambda r: pl.BlockSpec((r, HEAD_DIM), lambda h: (0, h + first))
    in_specs = [pl.BlockSpec(memory_space=pltpu.SMEM), whole(rows), whole(rows), whole(rows)]
    operands = [starts, q, k, v]
    for x, skip in (qa, qb, rk, rv):
        if x is not None:
            in_specs.append(
                pl.BlockSpec((x.shape[0], HEAD_DIM), partial(lambda skip, h: (0, h + skip), skip))
            )
            operands.append(x)
    out_specs = [here(rows), pl.BlockSpec((8, BLOCK), lambda h: (h, 0))]
    out_shape = [
        jax.ShapeDtypeStruct((rows, heads * HEAD_DIM), jnp.bfloat16),
        jax.ShapeDtypeStruct((heads * 8, BLOCK), jnp.float32),
    ]
    for count in (plan.na, plan.nb):
        if count:
            out_specs.append(here(count + STAT_ROWS))
            out_shape.append(
                jax.ShapeDtypeStruct((count + STAT_ROWS, heads * HEAD_DIM), jnp.bfloat16)
            )
    queries, keys = rows + plan.na + plan.nb, rows + plan.nk
    return pl.pallas_call(
        partial(attend_kernel, starts.shape[0], plan),
        grid=(heads,),
        in_specs=in_specs,
        out_specs=out_specs,
        out_shape=out_shape,
        scratch_shapes=[
            pltpu.VMEM((HEAD_DIM, keys), jnp.bfloat16),
            pltpu.VMEM((keys, 2 * HEAD_DIM), jnp.bfloat16),
        ],
        compiler_params=compiler_params(),
        cost_estimate=pl.CostEstimate(
            flops=4 * heads * queries * keys * HEAD_DIM,
            bytes_accessed=4 * heads * HEAD_DIM * (queries + keys),
            transcendentals=heads * queries * keys,
        ),
        name="attend_parts",
    )(*operands)


def join_kernel(plan, o, s, *rest):
    rest = list(rest)
    me = lax.axis_index("ctx")
    out = rest[-1]
    rows = o.shape[0]
    block = lax.broadcasted_iota(jnp.int32, (8, BLOCK), 0)
    parts, stats = [(o, rows)], [s[...]]
    for count, flags in ((plan.na, plan.a_from), (plan.nb, plan.b_from)):
        if count:
            part = rest.pop(0)
            carried = part[count:, :].astype(jnp.float32)
            stat = carried[:8] + carried[8:16] + carried[16:24]
            on = one_of(flags, me) & (block < count // BLOCK)
            parts.append((part, count))
            stats.append(jnp.where(on, stat, FAR))
    top = stats[0]
    for x in stats[1:]:
        top = jnp.maximum(top, x)
    weights = [jnp.exp2(x - top) for x in stats]
    total = sum(weights)
    weights = [(w / total).T for w in weights]
    for i in range(rows // BLOCK):
        sl = slice(i * BLOCK, (i + 1) * BLOCK)
        mixed = sum(
            w[:, i : i + 1] * part[sl, :].astype(jnp.float32)
            for w, (part, count) in zip(weights, parts)
            if i * BLOCK < count
        )
        out[sl, :] = mixed.astype(jnp.bfloat16)


def join(plan, o, s, others, first, channels, full):
    rows, wide = o.shape
    here = lambda r: pl.BlockSpec((r, HEAD_DIM), lambda h: (0, h))
    operands = [o, s] + others
    in_specs = [here(rows), pl.BlockSpec((8, BLOCK), lambda h: (h, 0))]
    in_specs += [here(x.shape[0]) for x in others]
    aliases = {}
    if full is not None:
        in_specs.append(pl.BlockSpec(memory_space=pl.ANY))
        operands.append(full)
        aliases = {len(operands) - 1: 0}
    return pl.pallas_call(
        partial(join_kernel, plan),
        grid=(wide // HEAD_DIM,),
        in_specs=in_specs,
        out_specs=pl.BlockSpec((rows, HEAD_DIM), lambda h: (0, h + first)),
        out_shape=jax.ShapeDtypeStruct((rows, channels), jnp.bfloat16),
        input_output_aliases=aliases,
        compiler_params=compiler_params(),
        cost_estimate=pl.CostEstimate(
            flops=6 * rows * wide, bytes_accessed=8 * rows * wide, transcendentals=0
        ),
        name="join_parts",
    )(*operands)


class Plan:
    def __init__(self, n, down_1, rows_1, down_2, rows_2, up, rows_up, heads, ahead):
        self.a = [(l + 1, l) for l in down_1]
        self.b = [(d + 2, d) for d in down_2]
        self.k = [(l, l + 1) for l in up]
        self.na = rows_1 if down_1 else 0
        self.nb = rows_2 if down_2 else 0
        self.nk = rows_up if up else 0
        self.heads, self.ahead = heads, ahead
        ends = lambda pairs, side: [int(any(p[side] == d for p in pairs)) for d in range(n)]
        self.a_from, self.a_to = ends(self.a, 0), ends(self.a, 1)
        self.b_from, self.b_to = ends(self.b, 0), ends(self.b, 1)
        self.k_to = ends(self.k, 1)


def after(value, *earlier):
    return lax.optimization_barrier((value, *earlier))[0]


def run_plan(plan, hq, hk, hv, filters, gain, q, k, starts):
    n = lax.axis_size("ctx")
    rows, channels = hk.shape
    send = lambda x, pairs: lax.ppermute(x, "ctx", pairs)
    back = lambda pairs: [(t, s) for s, t in pairs]
    halo = send(halo_product(hk, hv), [(i, i + 1) for i in range(n - 1)])
    mix = hyena(starts, hq, hk, hv, halo, filters, gain)

    def ahead(whole, heads, pairs, waits):
        cols = slice(heads[0] * HEAD_DIM, (heads[0] + heads[1]) * HEAD_DIM)
        return send(after(whole[:, cols], *waits), pairs)

    groups, at = [], 0
    for heads in plan.ahead:
        groups.append((at, heads))
        at += heads
    sent = []
    first, out, waits = 0, None, []
    rv, earlier = None, None
    for heads in plan.heads:
        if len(sent) < len(groups) and first == groups[len(sent)][0]:
            group = groups[len(sent)]
            got = [
                ahead(x, group, pairs, waits) if pairs else None
                for x, pairs in (
                    (q[: plan.na], plan.a),
                    (q[: plan.nb], plan.b),
                    (k[rows - plan.nk :], plan.k),
                )
            ]
            sent.append((group[0], got))
        start, (qa, qb, rk) = sent[-1]
        skip = first - start
        if plan.nk:
            cols = slice(first * HEAD_DIM, (first + heads) * HEAD_DIM)
            rv = send(after(mix[rows - plan.nk :, cols], *waits), plan.k)
        waits = [x for x in (rv, qa, qb, rk, earlier) if x is not None]
        o, s, *parts = attend(
            plan,
            starts,
            q,
            k,
            mix,
            (qa, skip),
            (qb, skip),
            (rk, skip),
            (rv, 0),
            first,
            heads,
        )
        earlier = s
        pairs = [p for p in (plan.a, plan.b) if p]
        others = [send(x, back(p)) for x, p in zip(parts, pairs)]
        out = join(plan, o, s, others, first, channels, out)
        first += heads
    return mix, out


def attend_update(queries, query_pos, query_begin, key_heads, value_heads, key_pos):
    score_scale = 1.0 / math.sqrt(HEAD_DIM)
    scores = (
        jnp.einsum("qhd,khd->hqk", queries, key_heads, preferred_element_type=jnp.float32)
        * score_scale
    )
    visible = (key_pos[None, :] <= query_pos[:, None]) & (key_pos[None, :] >= query_begin[:, None])
    new_max = jnp.max(jnp.where(visible[None], scores, FAR), axis=2)
    weights = jnp.exp(jnp.where(visible[None], scores - new_max[:, :, None], FAR))
    mixed = jnp.einsum(
        "hqk,khd->hqd",
        weights.astype(jnp.bfloat16),
        value_heads,
        preferred_element_type=jnp.float32,
    )
    return mixed / jnp.sum(weights, axis=2)[:, :, None]


def run_gathered(hq, hk, hv, filters, gain, q, k, starts):
    n = lax.axis_size("ctx")
    rows, channels = hk.shape
    heads = channels // HEAD_DIM
    own = (lax.axis_index("ctx") * rows).astype(jnp.int32)
    halo = lax.ppermute(halo_product(hk, hv), "ctx", [(i, i + 1) for i in range(n - 1)])
    mix = hyena(starts, hq, hk, hv, halo, filters, gain)
    keys = lax.all_gather(k, "ctx", axis=0, tiled=True)
    values = lax.all_gather(mix, "ctx", axis=0, tiled=True)
    key_pos = jnp.arange(n * rows, dtype=jnp.int32)
    pos = own + jnp.arange(rows, dtype=jnp.int32)
    mixed = attend_update(
        q.reshape(rows, heads, HEAD_DIM),
        pos,
        begin_of(pos, [starts[i] for i in range(starts.shape[0])]),
        keys.reshape(n * rows, heads, HEAD_DIM),
        values.reshape(n * rows, heads, HEAD_DIM),
        key_pos,
    )
    return mix, mixed.astype(jnp.bfloat16).transpose(1, 0, 2).reshape(rows, channels)


def per_device(hq, hk, hv, filters, skip_gain, q, k, starts):
    rows, channels = hk.shape
    n = lax.axis_size("ctx")
    gain = skip_gain[None, :]
    if n != 4:
        return run_gathered(hq, hk, hv, filters, gain, q, k, starts)
    plan = Plan(n, [1, 2], rows, [1], rows - BLOCK, [0], rows, [4, 4, 4, 4], [8, 8])
    return run_plan(plan, hq, hk, hv, filters, gain, q, k, starts)


def solution(mesh):
    split = P(("rep", "ctx"), ("ch", "sub"))
    return jax.shard_map(
        per_device,
        mesh=mesh,
        in_specs=(
            split,
            split,
            split,
            P(("ch", "sub"), None),
            P(("ch", "sub")),
            split,
            split,
            P("rep"),
        ),
        out_specs=(split, split),
        check_vma=False,
    )
```

profile of v0, /device:TPU:26, one launch (start us, length us, event | category | flops | bytes accessed | tf_op | source)
XLA Modules:
  0.0 155.6 jit_solution(16568860030442492248)
XLA Ops:
  0.6 0.0 copy-start
  0.6 0.0 copy-start.1
  0.7 1.5 copy-done.1
  2.2 1.4 copy-done.2
  3.6 0.3 halo_product.1
  3.9 1.3 collective-permute-start
  5.2 0.0 copy-done
  5.2 0.1 fusion.3
  5.3 0.0 copy-start.7
  5.4 4.7 %collective-permute-start.2 = (bf16[384,1024]{1,0:T(8,128)(2,1)S(1)}, bf16[384,1024]{1,0:T(8,128)(2,1)S(1)}, u32[]{:S(2)}, u32[]{:S(2)}) collective-permute-start(bf16[384,1024]{1,0:T(8,128)(2,1)S(1)} %get-tuple-element.54), channel_id=1, source_target_pairs={{8,4},{12,8},{9,5},{13,9},{10,6},{14,10},{11,7},{15,11},{24,20},{2... | collective-permute-start | bytes 2359304 | tf_op jit(solution)/shard_map/ppermute | solution.py:391
  10.1 0.1 fusion.2
  10.2 0.0 copy-start.3
  10.2 0.0 copy-start.4
  10.2 0.0 copy-start.5
  10.2 0.0 copy-start.6
  10.2 1.5 collective-permute-start.3
  11.7 0.0 copy-done.7
  11.7 0.1 fusion.1
  11.8 0.7 collective-permute-start.4
  12.6 6.9 %collective-permute-done.halo = bf16[128,2048]{1,0:T(8,128)(2,1)S(1)} collective-permute-done((bf16[128,2048]{1,0:T(8,128)(2,1)S(1)}, bf16[128,2048]{1,0:T(8,128)(2,1)S(1)}, u32[]{:S(2)}, u32[]{:S(2)}) %collective-permute-start) | collective-permute-done | bytes 524320 | tf_op jit(solution)/shard_map/ppermute | solution.py:391
  19.5 0.0 copy-done.5
  19.5 21.0 %hyena_mix.1.v = bf16[384,2048]{1,0:T(8,128)(2,1)} custom-call(s32[4]{0:T(128)S(1)} %copy-done.3, bf16[384,2048]{1,0:T(8,128)(2,1)S(1)} %copy-done.4, bf16[384,2048]{1,0:T(8,128)(2,1)S(1)} %copy-done.1, bf16[384,2048]{1,0:T(8,128)(2,1)S(1)} %copy-done.2, bf16[128,2048]{1,0:T(8,128)(2,1)S(1)} %collective-permute-done.halo, bf16[128,128]{1,0:T(8,128)(2,1)S(1)} %copy-done.5, ...), custom_call_target="tpu_custom_call" | custom-call | flops 3221225472 | bytes 6291456 | tf_op jit(solution)/shard_map/hyena_mix/pallas_call | solution.py:136
  40.5 1.5 fusion
  41.9 0.7 collective-permute-start.1
  42.6 0.0 collective-permute-done.3.rest_1_
  42.6 0.0 collective-permute-done.2.rest_0_
  42.6 0.0 collective-permute-done.4.rest_2_
  42.6 0.0 collective-permute-done.1.rest_3_
  42.7 0.7 collective-permute-start.5
  43.3 4.6 %attend_parts.4 = (bf16[384,512]{1,0:T(8,128)(2,1)S(1)}, f32[32,128]{1,0:T(8,128)S(1)}, bf16[416,512]{1,0:T(8,128)(2,1)S(1)}, bf16[288,512]{1,0:T(8,128)(2,1)S(1)}) custom-call(s32[4]{0:T(128)S(1)} %copy-done.3, bf16[384,2048]{1,0:T(8,128)(2,1)S(1)} %copy-done, bf16[384,2048]{1,0:T(8,128)(2,1)} %k.7, bf16[384,2048]{1,0:T(8,128)(2,1)} %hyena_mix.1.v, ...), custom_call_target="tpu_custom_call" | custom-call | flops 1610612736 | bytes 3670016 | tf_op jit(solution)/shard_map/attend_parts/pallas_call | solution.py:292
  47.9 0.0 collective-permute-done.5.rest_3_
  47.9 4.7 %collective-permute-start.6 = (bf16[384,1024]{1,0:T(8,128)(2,1)S(1)}, bf16[384,1024]{1,0:T(8,128)(2,1)S(1)}, u32[]{:S(2)}, u32[]{:S(2)}) collective-permute-start(bf16[384,1024]{1,0:T(8,128)(2,1)S(1)} %get-tuple-element.26), channel_id=1, source_target_pairs={{8,4},{12,8},{9,5},{13,9},{10,6},{14,10},{11,7},{15,11},{24,20},{2... | collective-permute-start | bytes 2359304 | tf_op jit(solution)/shard_map/ppermute | solution.py:391
  52.6 0.7 collective-permute-start.8
  53.3 15.1 %collective-permute-start.7 = (bf16[256,1024]{1,0:T(8,128)(2,1)S(1)}, bf16[256,1024]{1,0:T(8,128)(2,1)S(1)}, u32[]{:S(2)}, u32[]{:S(2)}) collective-permute-start(bf16[256,1024]{1,0:T(8,128)(2,1)S(1)} %get-tuple-element.27), channel_id=1, source_target_pairs={{12,4},{13,5},{14,6},{15,7},{28,20},{29,21},{30,22},{31,23}} | collective-permute-start | bytes 1572872 | tf_op jit(solution)/shard_map/ppermute | solution.py:391
  68.5 0.7 collective-permute-start.9
  69.2 4.6 %attend_parts.5 = (bf16[384,512]{1,0:T(8,128)(2,1)S(1)}, f32[32,128]{1,0:T(8,128)S(1)}, bf16[416,512]{1,0:T(8,128)(2,1)S(1)}, bf16[288,512]{1,0:T(8,128)(2,1)S(1)}) custom-call(s32[4]{0:T(128)S(1)} %copy-done.3, bf16[384,2048]{1,0:T(8,128)(2,1)S(1)} %copy-done, bf16[384,2048]{1,0:T(8,128)(2,1)} %k.7, bf16[384,2048]{1,0:T(8,128)(2,1)} %hyena_mix.1.v, ...), custom_call_target="tpu_custom_call" | custom-call | flops 1610612736 | bytes 3670016 | tf_op jit(solution)/shard_map/attend_parts/pallas_call | solution.py:292
  73.8 0.0 collective-permute-done.9.rest_3_
  73.8 6.0 %collective-permute-done.7.rest_1_ = bf16[256,1024]{1,0:T(8,128)(2,1)S(1)} collective-permute-done((bf16[256,1024]{1,0:T(8,128)(2,1)S(1)}, bf16[256,1024]{1,0:T(8,128)(2,1)S(1)}, u32[]{:S(2)}, u32[]{:S(2)}) %collective-permute-start.7) | collective-permute-done | bytes 524320 | tf_op jit(solution)/shard_map/ppermute | solution.py:391
  79.8 0.0 collective-permute-done.6.rest_0_
  79.8 0.0 collective-permute-done.8.rest_2_
  79.8 0.7 collective-permute-start.10
  80.5 1.3 collective-permute-start.17
  81.8 1.3 collective-permute-start.18
  83.1 1.3 collective-permute-start.15
  84.4 1.5 collective-permute-start.16
  85.9 4.6 %attend_parts.7 = (bf16[384,512]{1,0:T(8,128)(2,1)S(1)}, f32[32,128]{1,0:T(8,128)S(1)}, bf16[416,512]{1,0:T(8,128)(2,1)S(1)}, bf16[288,512]{1,0:T(8,128)(2,1)S(1)}) custom-call(s32[4]{0:T(128)S(1)} %copy-done.3, bf16[384,2048]{1,0:T(8,128)(2,1)S(1)} %copy-done, bf16[384,2048]{1,0:T(8,128)(2,1)} %k.7, bf16[384,2048]{1,0:T(8,128)(2,1)} %hyena_mix.1.v, ...), custom_call_target="tpu_custom_call" | custom-call | flops 1610612736 | bytes 3670016 | tf_op jit(solution)/shard_map/attend_parts/pallas_call | solution.py:292
  90.5 0.0 collective-permute-done.10.rest_3_
  90.5 1.3 collective-permute-start.13
  91.8 4.6 %attend_parts.6 = (bf16[384,512]{1,0:T(8,128)(2,1)S(1)}, f32[32,128]{1,0:T(8,128)S(1)}, bf16[416,512]{1,0:T(8,128)(2,1)S(1)}, bf16[288,512]{1,0:T(8,128)(2,1)S(1)}) custom-call(s32[4]{0:T(128)S(1)} %copy-done.3, bf16[384,2048]{1,0:T(8,128)(2,1)S(1)} %copy-done, bf16[384,2048]{1,0:T(8,128)(2,1)} %k.7, bf16[384,2048]{1,0:T(8,128)(2,1)} %hyena_mix.1.v, ...), custom_call_target="tpu_custom_call" | custom-call | flops 1610612736 | bytes 3670016 | tf_op jit(solution)/shard_map/attend_parts/pallas_call | solution.py:292
  96.4 15.8 %collective-permute-done.18.rest_1_ = bf16[288,512]{1,0:T(8,128)(2,1)S(1)} collective-permute-done((bf16[288,512]{1,0:T(8,128)(2,1)S(1)}, bf16[288,512]{1,0:T(8,128)(2,1)S(1)}, u32[]{:S(2)}, u32[]{:S(2)}) %collective-permute-start.18) | collective-permute-done | bytes 294944 | tf_op jit(solution)/shard_map/ppermute | solution.py:391
  112.2 1.3 collective-permute-start.11
  113.5 0.0 collective-permute-done.17.rest_0_
  113.5 1.3 collective-permute-start.14
  114.8 12.8 %collective-permute-done.16.rest_1_ = bf16[288,512]{1,0:T(8,128)(2,1)S(1)} collective-permute-done((bf16[288,512]{1,0:T(8,128)(2,1)S(1)}, bf16[288,512]{1,0:T(8,128)(2,1)S(1)}, u32[]{:S(2)}, u32[]{:S(2)}) %collective-permute-start.16) | collective-permute-done | bytes 294944 | tf_op jit(solution)/shard_map/ppermute | solution.py:391
  127.6 1.3 collective-permute-start.12
  128.9 2.7 %join_parts.4.rest_2_ = bf16[384,2048]{1,0:T(8,128)(2,1)} custom-call(bf16[384,512]{1,0:T(8,128)(2,1)S(1)} %get-tuple-element.43.o, f32[32,128]{1,0:T(8,128)S(1)} %get-tuple-element.25.s, bf16[416,512]{1,0:T(8,128)(2,1)S(1)} %collective-permute-done.17.rest_0_, bf16[288,512]{1,0:T(8,128)(2,1)S(1)} %collective-permute-done.18.rest_1_), custom_call_target="tpu_custom_call" | custom-call | flops 1179648 | bytes 1572864 | tf_op jit(solution)/shard_map/join_parts/pallas_call | solution.py:354
  131.6 0.0 collective-permute-done.15.rest_0_
  131.6 2.7 %join_parts.5.rest_2_ = bf16[384,2048]{1,0:T(8,128)(2,1)} custom-call(bf16[384,512]{1,0:T(8,128)(2,1)S(1)} %get-tuple-element.40.o, f32[32,128]{1,0:T(8,128)S(1)} %get-tuple-element.30.s, bf16[416,512]{1,0:T(8,128)(2,1)S(1)} %collective-permute-done.15.rest_0_, bf16[288,512]{1,0:T(8,128)(2,1)S(1)} %collective-permute-done.16.rest_1_, ...), custom_call_target="tpu_custom_call", output_to_operand_aliasing={{}: (4, {})} | custom-call | flops 1179648 | bytes 1572864 | tf_op jit(solution)/shard_map/join_parts/pallas_call | solution.py:354
  134.2 15.5 %collective-permute-done.14.rest_1_ = bf16[288,512]{1,0:T(8,128)(2,1)S(1)} collective-permute-done((bf16[288,512]{1,0:T(8,128)(2,1)S(1)}, bf16[288,512]{1,0:T(8,128)(2,1)S(1)}, u32[]{:S(2)}, u32[]{:S(2)}) %collective-permute-start.14) | collective-permute-done | bytes 294944 | tf_op jit(solution)/shard_map/ppermute | solution.py:391
  149.7 0.0 collective-permute-done.13.rest_0_
  149.7 2.7 %join_parts.6.rest_2_ = bf16[384,2048]{1,0:T(8,128)(2,1)} custom-call(bf16[384,512]{1,0:T(8,128)(2,1)S(1)} %get-tuple-element.36.o, f32[32,128]{1,0:T(8,128)S(1)} %get-tuple-element.37.s, bf16[416,512]{1,0:T(8,128)(2,1)S(1)} %collective-permute-done.13.rest_0_, bf16[288,512]{1,0:T(8,128)(2,1)S(1)} %collective-permute-done.14.rest_1_, ...), custom_call_target="tpu_custom_call", output_to_operand_aliasing={{}: (4, {})} | custom-call | flops 1179648 | bytes 1572864 | tf_op jit(solution)/shard_map/join_parts/pallas_call | solution.py:354
  152.4 0.5 collective-permute-done.12.rest_1_
  152.9 0.0 collective-permute-done.11.rest_0_
  152.9 2.7 %join_parts.7 = bf16[384,2048]{1,0:T(8,128)(2,1)} custom-call(bf16[384,512]{1,0:T(8,128)(2,1)S(1)} %get-tuple-element.32.o, f32[32,128]{1,0:T(8,128)S(1)} %get-tuple-element.33.s, bf16[416,512]{1,0:T(8,128)(2,1)S(1)} %collective-permute-done.11.rest_0_, bf16[288,512]{1,0:T(8,128)(2,1)S(1)} %collective-permute-done.12.rest_1_, ...), custom_call_target="tpu_custom_call", output_to_operand_aliasing={{}: (4, {})} | custom-call | flops 1179648 | bytes 1572864 | tf_op jit(solution)/shard_map/join_parts/pallas_call | solution.py:354
  (4 shorter events, 0.0 us)
Async XLA Ops:
  0.6 4.6 %copy-start = (bf16[384,2048]{1,0:T(8,128)(2,1)S(1)}, bf16[384,2048]{1,0:T(8,128)(2,1)}, u32[]{:S(2)}) copy-start(bf16[384,2048]{1,0:T(8,128)(2,1)} %q.7) | copy-start | bytes 4718596
  0.6 1.5 copy-start.1
  2.2 1.4 copy-start.2
  3.9 15.6 %collective-permute-start = (bf16[128,2048]{1,0:T(8,128)(2,1)S(1)}, bf16[128,2048]{1,0:T(8,128)(2,1)S(1)}, u32[]{:S(2)}, u32[]{:S(2)}) collective-permute-start(bf16[128,2048]{1,0:T(8,128)(2,1)S(1)} %halo_product.1), channel_id=1, source_target_pairs={{0,4},{4,8},{8,12},{1,5},{5,9},{9,13},{2,6},{6,10},{10,14},{3,7},{... | collective-permute-start | bytes 1572872 | tf_op jit(solution)/shard_map/ppermute | solution.py:391
  5.3 6.3 %copy-start.7 = (bf16[384,2048]{1,0:T(8,128)(2,1)S(1)}, bf16[384,2048]{1,0:T(8,128)(2,1)}, u32[]{:S(2)}) copy-start(bf16[384,2048]{1,0:T(8,128)(2,1)} %k.7) | copy-start | bytes 4718596
  5.4 37.3 %collective-permute-start.2 = (bf16[384,1024]{1,0:T(8,128)(2,1)S(1)}, bf16[384,1024]{1,0:T(8,128)(2,1)S(1)}, u32[]{:S(2)}, u32[]{:S(2)}) collective-permute-start(bf16[384,1024]{1,0:T(8,128)(2,1)S(1)} %get-tuple-element.54), channel_id=1, source_target_pairs={{8,4},{12,8},{9,5},{13,9},{10,6},{14,10},{11,7},{15,11},{24,20},{2... | collective-permute-start | bytes 2359304 | tf_op jit(solution)/shard_map/ppermute | solution.py:391
  10.2 9.3 %copy-start.3 = (s32[4]{0:T(128)S(1)}, s32[4]{0:T(128)}, u32[]{:S(2)}) copy-start(s32[4]{0:T(128)} %info.9) | copy-start | bytes 52
  10.2 9.3 %copy-start.4 = (bf16[384,2048]{1,0:T(8,128)(2,1)S(1)}, bf16[384,2048]{1,0:T(8,128)(2,1)}, u32[]{:S(2)}) copy-start(bf16[384,2048]{1,0:T(8,128)(2,1)} %hq.1) | copy-start | bytes 4718596
  10.2 9.3 %copy-start.5 = (bf16[128,128]{1,0:T(8,128)(2,1)S(1)}, bf16[128,128]{1,0:T(8,128)(2,1)}, u32[]{:S(2)}) copy-start(bf16[128,128]{1,0:T(8,128)(2,1)} %filters.1) | copy-start | bytes 98308
  10.2 9.3 %copy-start.6 = (f32[2048]{0:T(1024)S(1)}, f32[2048]{0:T(1024)}, u32[]{:S(2)}) copy-start(f32[2048]{0:T(1024)} %param.12) | copy-start | bytes 24580
  10.2 32.4 %collective-permute-start.3 = (bf16[256,1024]{1,0:T(8,128)(2,1)S(1)}, bf16[256,1024]{1,0:T(8,128)(2,1)S(1)}, u32[]{:S(2)}, u32[]{:S(2)}) collective-permute-start(bf16[256,1024]{1,0:T(8,128)(2,1)S(1)} %get-tuple-element.53), channel_id=1, source_target_pairs={{12,4},{13,5},{14,6},{15,7},{28,20},{29,21},{30,22},{31,23}} | collective-permute-start | bytes 1572872 | tf_op jit(solution)/shard_map/ppermute | solution.py:391
  11.8 30.8 %collective-permute-start.4 = (bf16[384,1024]{1,0:T(8,128)(2,1)S(1)}, bf16[384,1024]{1,0:T(8,128)(2,1)S(1)}, u32[]{:S(2)}, u32[]{:S(2)}) collective-permute-start(bf16[384,1024]{1,0:T(8,128)(2,1)S(1)} %get-tuple-element.51), channel_id=1, source_target_pairs={{0,4},{1,5},{2,6},{3,7},{16,20},{17,21},{18,22},{19,23}} | collective-permute-start | bytes 2359304 | tf_op jit(solution)/shard_map/ppermute | solution.py:391
  41.9 0.7 collective-permute-start.1
  42.7 5.3 %collective-permute-start.5 = (bf16[384,512]{1,0:T(8,128)(2,1)S(1)}, bf16[384,512]{1,0:T(8,128)(2,1)S(1)}, u32[]{:S(2)}, u32[]{:S(2)}) collective-permute-start(bf16[384,512]{1,0:T(8,128)(2,1)S(1)} %get-tuple-element.24), channel_id=1, source_target_pairs={{0,4},{1,5},{2,6},{3,7},{16,20},{17,21},{18,22},{19,23}} | collective-permute-start | bytes 1179656 | tf_op jit(solution)/shard_map/ppermute | solution.py:391
  47.9 31.9 %collective-permute-start.6 = (bf16[384,1024]{1,0:T(8,128)(2,1)S(1)}, bf16[384,1024]{1,0:T(8,128)(2,1)S(1)}, u32[]{:S(2)}, u32[]{:S(2)}) collective-permute-start(bf16[384,1024]{1,0:T(8,128)(2,1)S(1)} %get-tuple-element.26), channel_id=1, source_target_pairs={{8,4},{12,8},{9,5},{13,9},{10,6},{14,10},{11,7},{15,11},{24,20},{2... | collective-permute-start | bytes 2359304 | tf_op jit(solution)/shard_map/ppermute | solution.py:391
  52.6 27.2 %collective-permute-start.8 = (bf16[384,1024]{1,0:T(8,128)(2,1)S(1)}, bf16[384,1024]{1,0:T(8,128)(2,1)S(1)}, u32[]{:S(2)}, u32[]{:S(2)}) collective-permute-start(bf16[384,1024]{1,0:T(8,128)(2,1)S(1)} %get-tuple-element.28), channel_id=1, source_target_pairs={{0,4},{1,5},{2,6},{3,7},{16,20},{17,21},{18,22},{19,23}} | collective-permute-start | bytes 2359304 | tf_op jit(solution)/shard_map/ppermute | solution.py:391
  53.3 26.4 %collective-permute-start.7 = (bf16[256,1024]{1,0:T(8,128)(2,1)S(1)}, bf16[256,1024]{1,0:T(8,128)(2,1)S(1)}, u32[]{:S(2)}, u32[]{:S(2)}) collective-permute-start(bf16[256,1024]{1,0:T(8,128)(2,1)S(1)} %get-tuple-element.27), channel_id=1, source_target_pairs={{12,4},{13,5},{14,6},{15,7},{28,20},{29,21},{30,22},{31,23}} | collective-permute-start | bytes 1572872 | tf_op jit(solution)/shard_map/ppermute | solution.py:391
  68.5 5.3 %collective-permute-start.9 = (bf16[384,512]{1,0:T(8,128)(2,1)S(1)}, bf16[384,512]{1,0:T(8,128)(2,1)S(1)}, u32[]{:S(2)}, u32[]{:S(2)}) collective-permute-start(bf16[384,512]{1,0:T(8,128)(2,1)S(1)} %get-tuple-element.29), channel_id=1, source_target_pairs={{0,4},{1,5},{2,6},{3,7},{16,20},{17,21},{18,22},{19,23}} | collective-permute-start | bytes 1179656 | tf_op jit(solution)/shard_map/ppermute | solution.py:391
  79.8 10.7 %collective-permute-start.10 = (bf16[384,512]{1,0:T(8,128)(2,1)S(1)}, bf16[384,512]{1,0:T(8,128)(2,1)S(1)}, u32[]{:S(2)}, u32[]{:S(2)}) collective-permute-start(bf16[384,512]{1,0:T(8,128)(2,1)S(1)} %get-tuple-element.31), channel_id=1, source_target_pairs={{0,4},{1,5},{2,6},{3,7},{16,20},{17,21},{18,22},{19,23}} | collective-permute-start | bytes 1179656 | tf_op jit(solution)/shard_map/ppermute | solution.py:391
  80.5 33.0 %collective-permute-start.17 = (bf16[416,512]{1,0:T(8,128)(2,1)S(1)}, bf16[416,512]{1,0:T(8,128)(2,1)S(1)}, u32[]{:S(2)}, u32[]{:S(2)}) collective-permute-start(bf16[416,512]{1,0:T(8,128)(2,1)S(1)} %get-tuple-element.44), channel_id=1, source_target_pairs={{4,8},{8,12},{5,9},{9,13},{6,10},{10,14},{7,11},{11,15},{20,24},{2... | collective-permute-start | bytes 1277960 | tf_op jit(solution)/shard_map/ppermute | solution.py:391
  81.8 30.5 %collective-permute-start.18 = (bf16[288,512]{1,0:T(8,128)(2,1)S(1)}, bf16[288,512]{1,0:T(8,128)(2,1)S(1)}, u32[]{:S(2)}, u32[]{:S(2)}) collective-permute-start(bf16[288,512]{1,0:T(8,128)(2,1)S(1)} %get-tuple-element.45), channel_id=1, source_target_pairs={{4,12},{5,13},{6,14},{7,15},{20,28},{21,29},{22,30},{23,31}} | collective-permute-start | bytes 884744 | tf_op jit(solution)/shard_map/ppermute | solution.py:391
  83.1 48.5 %collective-permute-start.15 = (bf16[416,512]{1,0:T(8,128)(2,1)S(1)}, bf16[416,512]{1,0:T(8,128)(2,1)S(1)}, u32[]{:S(2)}, u32[]{:S(2)}) collective-permute-start(bf16[416,512]{1,0:T(8,128)(2,1)S(1)} %get-tuple-element.41), channel_id=1, source_target_pairs={{4,8},{8,12},{5,9},{9,13},{6,10},{10,14},{7,11},{11,15},{20,24},{2... | collective-permute-start | bytes 1277960 | tf_op jit(solution)/shard_map/ppermute | solution.py:391
  84.4 43.3 %collective-permute-start.16 = (bf16[288,512]{1,0:T(8,128)(2,1)S(1)}, bf16[288,512]{1,0:T(8,128)(2,1)S(1)}, u32[]{:S(2)}, u32[]{:S(2)}) collective-permute-start(bf16[288,512]{1,0:T(8,128)(2,1)S(1)} %get-tuple-element.42), channel_id=1, source_target_pairs={{4,12},{5,13},{6,14},{7,15},{20,28},{21,29},{22,30},{23,31}} | collective-permute-start | bytes 884744 | tf_op jit(solution)/shard_map/ppermute | solution.py:391
  90.5 59.2 %collective-permute-start.13 = (bf16[416,512]{1,0:T(8,128)(2,1)S(1)}, bf16[416,512]{1,0:T(8,128)(2,1)S(1)}, u32[]{:S(2)}, u32[]{:S(2)}) collective-permute-start(bf16[416,512]{1,0:T(8,128)(2,1)S(1)} %get-tuple-element.38), channel_id=1, source_target_pairs={{4,8},{8,12},{5,9},{9,13},{6,10},{10,14},{7,11},{11,15},{20,24},{2... | collective-permute-start | bytes 1277960 | tf_op jit(solution)/shard_map/ppermute | solution.py:391
  112.2 40.7 %collective-permute-start.11 = (bf16[416,512]{1,0:T(8,128)(2,1)S(1)}, bf16[416,512]{1,0:T(8,128)(2,1)S(1)}, u32[]{:S(2)}, u32[]{:S(2)}) collective-permute-start(bf16[416,512]{1,0:T(8,128)(2,1)S(1)} %get-tuple-element.34), channel_id=1, source_target_pairs={{4,8},{8,12},{5,9},{9,13},{6,10},{10,14},{7,11},{11,15},{20,24},{2... | collective-permute-start | bytes 1277960 | tf_op jit(solution)/shard_map/ppermute | solution.py:391
  113.5 36.2 %collective-permute-start.14 = (bf16[288,512]{1,0:T(8,128)(2,1)S(1)}, bf16[288,512]{1,0:T(8,128)(2,1)S(1)}, u32[]{:S(2)}, u32[]{:S(2)}) collective-permute-start(bf16[288,512]{1,0:T(8,128)(2,1)S(1)} %get-tuple-element.39), channel_id=1, source_target_pairs={{4,12},{5,13},{6,14},{7,15},{20,28},{21,29},{22,30},{23,31}} | collective-permute-start | bytes 884744 | tf_op jit(solution)/shard_map/ppermute | solution.py:391
  127.6 25.3 %collective-permute-start.12 = (bf16[288,512]{1,0:T(8,128)(2,1)S(1)}, bf16[288,512]{1,0:T(8,128)(2,1)S(1)}, u32[]{:S(2)}, u32[]{:S(2)}) collective-permute-start(bf16[288,512]{1,0:T(8,128)(2,1)S(1)} %get-tuple-element.35), channel_id=1, source_target_pairs={{4,12},{5,13},{6,14},{7,15},{20,28},{21,29},{22,30},{23,31}} | collective-permute-start | bytes 884744 | tf_op jit(solution)/shard_map/ppermute | solution.py:391
where the time goes:
time: 158 us; the launch traced here: 156 us
  waiting for transfers between devices  57.5 us (36%)
  Pallas kernels  50.4 us (32%)
  starting transfers between devices  41.9 us (27%)
  local copies, waits for them, and re-layouts  4.76 us (3%)
    ppermute x19, waiting for transfers between devices, run_plan(): send = lambda x, pairs: lax.ppermute(x, 'ctx', pairs)  57.5 us
    ppermute x19, starting transfers between devices, run_plan(): send = lambda x, pairs: lax.ppermute(x, 'ctx', pairs)  41.9 us
    pallas_call x1, Pallas kernels, hyena(): pl.pallas_call(partial(hyena_kernel, starts.shape[0], group), grid=(chann...  21 us
    pallas_call x4, Pallas kernels, attend(): pl.pallas_call(partial(attend_kernel, starts.shape[0], plan), grid=(heads...  18.5 us
    pallas_call x4, Pallas kernels, join(): pl.pallas_call(partial(join_kernel, plan), grid=(wide // HEAD_DIM,), in_s...  10.6 us
  transfers between devices with their start and end apart: 19, of which 6 were waited for; matrix products, arithmetic and copies ran while one was open for 1% of the time, Pallas kernels for 30%

commit v1 on v0

--- a/solution.py
+++ b/solution.py
@@ -13,6 +13,7 @@
 FAR = -1e30
 TO_LOG2 = math.log2(math.e) / math.sqrt(HEAD_DIM)
 VMEM_LIMIT = 48 * 1024 * 1024
+HEADS_AT_ONCE = 2
 STAT_ROWS = 32
 
 
@@ -53,89 +54,68 @@
     )(hk, hv)
 
 
-def hyena_kernel(genomes, group, info, hq, hk, hv, halo, filters, gain, out, lines, ext, tall):
+def hyena_kernel(genomes, group, info, hq, hk, hv, halo, filters, gain, out, lines, ext, mask):
     rows, width = out.shape
     blocks = rows // BLOCK
-    groups = width // group
+    groups = BLOCK // group
+    tiles = width // BLOCK
     starts = [info[i] for i in range(genomes)]
     step = pl.program_id(0)
     first = lax.axis_index("ctx") * rows
+    row = lax.broadcasted_iota(jnp.int32, (BLOCK, BLOCK), 0)
+    col = lax.broadcasted_iota(jnp.int32, (BLOCK, BLOCK), 1)
 
     @pl.when(step == 0)
     def _():
-        tap = lax.broadcasted_iota(jnp.int32, (BLOCK, BLOCK), 0)
-        col = lax.broadcasted_iota(jnp.int32, (BLOCK, BLOCK), 1)
-        turn = jnp.where((tap + col) % BLOCK == 0, 1.0, 0.0).astype(jnp.bfloat16)
+        turn = jnp.where((row + col) % BLOCK == 0, 1.0, 0.0).astype(jnp.bfloat16)
         lines[...] = jnp.dot(filters[...], turn, preferred_element_type=jnp.float32)
-
-    ext[:BLOCK] = halo[...]
-    ext[BLOCK:] = rounded_product(hk[...], hv[...])
-    ours = lines[pl.ds(pl.multiple_of(step * groups, groups), groups), :]
-    row = lax.broadcasted_iota(jnp.int32, (BLOCK, BLOCK), 0)
-    col = lax.broadcasted_iota(jnp.int32, (BLOCK, BLOCK), 1)
-    before = jnp.where(col > row, 1.0, 0.0).astype(jnp.bfloat16)
-    within = jnp.where(col <= row, 1.0, 0.0).astype(jnp.bfloat16)
-    for g in range(groups):
-        line = jnp.broadcast_to(ours[g : g + 1, :], (BLOCK, BLOCK))
-        circulant = pltpu.roll(line, 0, 1, stride=1, stride_axis=0).astype(jnp.bfloat16)
-        at = slice(g * BLOCK, (g + 1) * BLOCK)
-        tall[at, :BLOCK] = circulant * before
-        tall[at, BLOCK:] = circulant * within
-    lane_group = lax.broadcasted_iota(jnp.int32, (BLOCK, width), 1) // group
-
-    def finish(b, parts):
-        filtered = parts[0]
-        for g in range(1, groups):
-            filtered = jnp.where(lane_group == g, parts[g], filtered)
-        at = pl.ds(b * BLOCK, BLOCK)
-        direct = ext[(b + 1) * BLOCK : (b + 2) * BLOCK, :].astype(jnp.float32)
-        mix = hq[at, :].astype(jnp.float32) * (filtered + gain[...] * direct)
-        out[at, :] = mix.astype(jnp.bfloat16)
-
-    for b in range(blocks):
-        here = first + b * BLOCK
-        window = ext[b * BLOCK : (b + 2) * BLOCK, :]
-        cut = begin_of(here + BLOCK - 1, starts) > here - BLOCK
-
-        @pl.when(jnp.logical_not(cut))
-        def _():
-            finish(
-                b,
+        for b in range(blocks):
+            here = first + b * BLOCK
+            begin = begin_of(here + row, starts)
+            before = (col > row) & (here - BLOCK + col >= begin)
+            within = (col <= row) & (here + col >= begin)
+            mask[b, :, :BLOCK] = jnp.where(before, 1.0, 0.0).astype(jnp.bfloat16)
+            mask[b, :, BLOCK:] = jnp.where(within, 1.0, 0.0).astype(jnp.bfloat16)
+
+    ext[:BLOCK, :] = halo[...]
+    ext[BLOCK:, :] = rounded_product(hk[...], hv[...])
+    ours = lines[pl.ds(pl.multiple_of(step * groups * tiles, groups * tiles), groups * tiles), :]
+    lane_group = col // group
+    for t in range(tiles):
+        lanes = slice(t * BLOCK, (t + 1) * BLOCK)
+        turned = []
+        for g in range(groups):
+            line = jnp.broadcast_to(ours[t * groups + g, :][None, :], (BLOCK, BLOCK))
+            turned.append(pltpu.roll(line, 0, 1, stride=1, stride_axis=0).astype(jnp.bfloat16))
+        for b in range(blocks):
+            tall = jnp.concatenate(
                 [
-                    jnp.dot(
-                        tall[g * BLOCK : (g + 1) * BLOCK, :],
-                        window,
-                        preferred_element_type=jnp.float32,
-                    )
-                    for g in range(groups)
+                    jnp.concatenate([one * mask[b, :, :BLOCK], one * mask[b, :, BLOCK:]], axis=1)
+                    for one in turned
                 ],
+                axis=0,
             )
-
-        @pl.when(cut)
-        def _():
-            row = here + lax.broadcasted_iota(jnp.int32, (BLOCK, 2 * BLOCK), 0)
-            col = here - BLOCK + lax.broadcasted_iota(jnp.int32, (BLOCK, 2 * BLOCK), 1)
-            seen = jnp.where(col >= begin_of(row, starts), 1.0, 0.0).astype(jnp.bfloat16)
-            finish(
-                b,
-                [
-                    jnp.dot(
-                        tall[g * BLOCK : (g + 1) * BLOCK, :] * seen,
-                        window,
-                        preferred_element_type=jnp.float32,
-                    )
-                    for g in range(groups)
-                ],
-            )
+            window = ext[b * BLOCK : (b + 2) * BLOCK, lanes]
+            every = jnp.dot(tall, window, preferred_element_type=jnp.float32)
+            filtered = every[:BLOCK]
+            for g in range(1, groups):
+                filtered = jnp.where(
+                    lane_group == g, every[g * BLOCK : (g + 1) * BLOCK], filtered
+                )
+            at = slice(b * BLOCK, (b + 1) * BLOCK)
+            direct = ext[(b + 1) * BLOCK : (b + 2) * BLOCK, lanes].astype(jnp.float32)
+            mix = hq[at, lanes].astype(jnp.float32) * (filtered + gain[:, lanes] * direct)
+            out[at, lanes] = mix.astype(jnp.bfloat16)
 
 
 def hyena(starts, hq, hk, hv, halo, filters, gain):
     rows, channels = hk.shape
     group = channels // filters.shape[0]
-    here = lambda r: pl.BlockSpec((r, BLOCK), lambda j: (0, j))
+    width = 2 * BLOCK
+    here = lambda r: pl.BlockSpec((r, width), lambda j: (0, j))
     return pl.pallas_call(
         partial(hyena_kernel, starts.shape[0], group),
-        grid=(channels // BLOCK,),
+        grid=(channels // width,),
         in_specs=[
             pl.BlockSpec(memory_space=pltpu.SMEM),
             here(rows),
@@ -149,8 +129,8 @@
         out_shape=jax.ShapeDtypeStruct((rows, channels), jnp.bfloat16),
         scratch_shapes=[
             pltpu.VMEM((filters.shape[0], BLOCK), jnp.float32),
-            pltpu.VMEM((rows + BLOCK, BLOCK), jnp.bfloat16),
-            pltpu.VMEM((BLOCK // group * BLOCK, 2 * BLOCK), jnp.bfloat16),
+            pltpu.VMEM((rows + BLOCK, width), jnp.bfloat16),
+            pltpu.VMEM((rows // BLOCK, BLOCK, 2 * BLOCK), jnp.bfloat16),
         ],
         compiler_params=compiler_params(),
         cost_estimate=pl.CostEstimate(
@@ -175,7 +155,6 @@
     me = lax.axis_index("ctx")
     own = me * rows
     rest = list(rest)
-    turned, wide = rest[-2:]
     jobs = [(rows, q, own, None)]
     if plan.na:
         jobs.append((plan.na, rest.pop(0), own + rows, one_of(plan.a_to, me)))
@@ -186,13 +165,6 @@
     outs = [out] + rest[: len(jobs) - 1]
     starts = [info[i] for i in range(genomes)]
 
-    turned[:, :rows] = k[...].T
-    wide[:rows, :HEAD_DIM] = v[...]
-    if plan.nk:
-        turned[:, rows:] = rk[...].T
-        wide[rows:, :HEAD_DIM] = rv[...]
-    wide[:, HEAD_DIM:] = jnp.ones((rows + plan.nk, HEAD_DIM), jnp.bfloat16)
-
     def seen(row_at, count, col_at, columns):
         row = row_at + lax.broadcasted_iota(jnp.int32, (count, columns), 0)
         col = col_at + lax.broadcasted_iota(jnp.int32, (count, columns), 1)
@@ -200,25 +172,40 @@
         return (col <= row) & (col >= begin)
 
     def piece(queries, out, count, row_at, far, put):
-        keys = rows + plan.nk if far else rows
-        scores = jnp.dot(queries[...], turned[:, :keys], preferred_element_type=jnp.float32)
-        visible = seen(row_at, count, own, rows)
+        sets = [(k, v, seen(row_at, count, own, rows))]
         if far:
-            other = seen(row_at, count, own - plan.nk, plan.nk)
-            visible = jnp.concatenate([visible, other], axis=1)
-        scores = jnp.where(visible, scores, FAR)
-        top = jnp.max(scores, axis=1, keepdims=True)
-        weights = jnp.exp2((scores - top) * TO_LOG2).astype(jnp.bfloat16)
-        mixed = jnp.dot(weights, wide[:keys, :], preferred_element_type=jnp.float32)
-        total = mixed[:, HEAD_DIM:]
-        out[:count, :] = (mixed[:, :HEAD_DIM] / total).astype(jnp.bfloat16)
-        put(as_rows(top * TO_LOG2 + jnp.log2(total)))
+            sets.append((rk, rv, seen(row_at, count, own - plan.nk, plan.nk)))
+        for h in range(q.shape[1] // HEAD_DIM):
+            lanes = slice(h * HEAD_DIM, (h + 1) * HEAD_DIM)
+            scores = [
+                jnp.where(
+                    visible,
+                    lax.dot_general(
+                        queries[:, lanes],
+                        keys[:, lanes],
+                        (((1,), (1,)), ((), ())),
+                        preferred_element_type=jnp.float32,
+                    ),
+                    FAR,
+                )
+                for keys, _, visible in sets
+            ]
+            top = jnp.max(scores[0], axis=1, keepdims=True)
+            for one in scores[1:]:
+                top = jnp.maximum(top, jnp.max(one, axis=1, keepdims=True))
+            mixed = 0.0
+            for one, (_, values, _) in zip(scores, sets):
+                weights = jnp.exp2((one - top) * TO_LOG2).astype(jnp.bfloat16)
+                wide = [values[:, lanes], jnp.ones((values.shape[0], HEAD_DIM), jnp.bfloat16)]
+                mixed = mixed + jnp.dot(
+                    weights, jnp.concatenate(wide, axis=1), preferred_element_type=jnp.float32
+                )
+            total = mixed[:, HEAD_DIM:]
+            out[:count, lanes] = (mixed[:, :HEAD_DIM] / total).astype(jnp.bfloat16)
+            put(h, as_rows(top * TO_LOG2 + jnp.log2(total)))
 
     for (count, queries, at, on), out in zip(jobs, outs):
-        if on is None:
-            put = partial(stats.__setitem__, ...)
-        else:
-            put = partial(carry, out, count)
+        put = partial(keep, stats) if on is None else partial(carry, out, count)
 
         begin = begin_of(at, starts)
         on = True if on is None else on & (begin < own + rows)
@@ -243,8 +230,9 @@
 
             @pl.when(jnp.logical_not(on))
             def _():
-                out[:count, :] = jnp.zeros((count, HEAD_DIM), jnp.bfloat16)
-                put(jnp.full((8, BLOCK), FAR, jnp.float32))
+                out[:count, :] = jnp.zeros((count, out.shape[1]), jnp.bfloat16)
+                for h in range(out.shape[1] // HEAD_DIM):
+                    put(h, jnp.full((8, BLOCK), FAR, jnp.float32))
 
 
 def as_rows(column):
@@ -257,27 +245,31 @@
     return jnp.concatenate(rows + [jnp.zeros_like(rows[0])] * (8 - len(rows)))
 
 
-def carry(out, count, stat):
+def keep(out, h, stat):
+    out[h * 8 : (h + 1) * 8, :] = stat
+
+
+def carry(out, count, h, stat):
     high = stat.astype(jnp.bfloat16).astype(jnp.float32)
     middle = (stat - high).astype(jnp.bfloat16).astype(jnp.float32)
     low = stat - high - middle
     parts = jnp.concatenate([high, middle, low, jnp.zeros_like(low)])
-    out[count:, :] = parts.astype(jnp.bfloat16)
+    out[count:, h * HEAD_DIM : (h + 1) * HEAD_DIM] = parts.astype(jnp.bfloat16)
 
 
 def attend(plan, starts, q, k, v, qa, qb, rk, rv, first, heads):
     rows = q.shape[0]
-    here = lambda r: pl.BlockSpec((r, HEAD_DIM), lambda h: (0, h))
-    whole = lambda r: pl.BlockSpec((r, HEAD_DIM), lambda h: (0, h + first))
+    width = HEADS_AT_ONCE * HEAD_DIM
+    here = lambda r: pl.BlockSpec((r, width), lambda h: (0, h))
+    later = lambda r, skip: pl.BlockSpec((r, width), lambda h: (0, h + skip // HEADS_AT_ONCE))
+    whole = lambda r: later(r, first)
     in_specs = [pl.BlockSpec(memory_space=pltpu.SMEM), whole(rows), whole(rows), whole(rows)]
     operands = [starts, q, k, v]
     for x, skip in (qa, qb, rk, rv):
         if x is not None:
-            in_specs.append(
-                pl.BlockSpec((x.shape[0], HEAD_DIM), partial(lambda skip, h: (0, h + skip), skip))
-            )
+            in_specs.append(later(x.shape[0], skip))
             operands.append(x)
-    out_specs = [here(rows), pl.BlockSpec((8, BLOCK), lambda h: (h, 0))]
+    out_specs = [here(rows), pl.BlockSpec((HEADS_AT_ONCE * 8, BLOCK), lambda h: (h, 0))]
     out_shape = [
         jax.ShapeDtypeStruct((rows, heads * HEAD_DIM), jnp.bfloat16),
         jax.ShapeDtypeStruct((heads * 8, BLOCK), jnp.float32),
@@ -291,14 +283,10 @@
     queries, keys = rows + plan.na + plan.nb, rows + plan.nk
     return pl.pallas_call(
         partial(attend_kernel, starts.shape[0], plan),
-        grid=(heads,),
+        grid=(heads // HEADS_AT_ONCE,),
         in_specs=in_specs,
         out_specs=out_specs,
         out_shape=out_shape,
-        scratch_shapes=[
-            pltpu.VMEM((HEAD_DIM, keys), jnp.bfloat16),
-            pltpu.VMEM((keys, 2 * HEAD_DIM), jnp.bfloat16),
-        ],
         compiler_params=compiler_params(),
         cost_estimate=pl.CostEstimate(
             flops=4 * heads * queries * keys * HEAD_DIM,
@@ -315,36 +303,39 @@
     out = rest[-1]
     rows = o.shape[0]
     block = lax.broadcasted_iota(jnp.int32, (8, BLOCK), 0)
-    parts, stats = [(o, rows)], [s[...]]
+    parts = [(o, rows, None)]
     for count, flags in ((plan.na, plan.a_from), (plan.nb, plan.b_from)):
         if count:
-            part = rest.pop(0)
-            carried = part[count:, :].astype(jnp.float32)
-            stat = carried[:8] + carried[8:16] + carried[16:24]
-            on = one_of(flags, me) & (block < count // BLOCK)
-            parts.append((part, count))
-            stats.append(jnp.where(on, stat, FAR))
-    top = stats[0]
-    for x in stats[1:]:
-        top = jnp.maximum(top, x)
-    weights = [jnp.exp2(x - top) for x in stats]
-    total = sum(weights)
-    weights = [(w / total).T for w in weights]
-    for i in range(rows // BLOCK):
-        sl = slice(i * BLOCK, (i + 1) * BLOCK)
-        mixed = sum(
-            w[:, i : i + 1] * part[sl, :].astype(jnp.float32)
-            for w, (part, count) in zip(weights, parts)
-            if i * BLOCK < count
-        )
-        out[sl, :] = mixed.astype(jnp.bfloat16)
+            parts.append((rest.pop(0), count, one_of(flags, me) & (block < count // BLOCK)))
+    for h in range(o.shape[1] // HEAD_DIM):
+        lanes = slice(h * HEAD_DIM, (h + 1) * HEAD_DIM)
+        stats = [s[h * 8 : (h + 1) * 8, :]]
+        for part, count, on in parts[1:]:
+            carried = part[count:, lanes].astype(jnp.float32)
+            stats.append(jnp.where(on, carried[:8] + carried[8:16] + carried[16:24], FAR))
+        top = stats[0]
+        for x in stats[1:]:
+            top = jnp.maximum(top, x)
+        weights = [jnp.exp2(x - top) for x in stats]
+        total = sum(weights)
+        weights = [(w / total).T for w in weights]
+        for i in range(rows // BLOCK):
+            sl = slice(i * BLOCK, (i + 1) * BLOCK)
+            mixed = sum(
+                w[:, i : i + 1] * part[sl, lanes].astype(jnp.float32)
+                for w, (part, count, _) in zip(weights, parts)
+                if i * BLOCK < count
+            )
+            out[sl, lanes] = mixed.astype(jnp.bfloat16)
 
 
 def join(plan, o, s, others, first, channels, full):
     rows, wide = o.shape
-    here = lambda r: pl.BlockSpec((r, HEAD_DIM), lambda h: (0, h))
+    width = HEADS_AT_ONCE * HEAD_DIM
+    skip = first // HEADS_AT_ONCE
+    here = lambda r: pl.BlockSpec((r, width), lambda h: (0, h))
     operands = [o, s] + others
-    in_specs = [here(rows), pl.BlockSpec((8, BLOCK), lambda h: (h, 0))]
+    in_specs = [here(rows), pl.BlockSpec((HEADS_AT_ONCE * 8, BLOCK), lambda h: (h, 0))]
     in_specs += [here(x.shape[0]) for x in others]
     aliases = {}
     if full is not None:
@@ -353,9 +344,9 @@
         aliases = {len(operands) - 1: 0}
     return pl.pallas_call(
         partial(join_kernel, plan),
-        grid=(wide // HEAD_DIM,),
+        grid=(wide // width,),
         in_specs=in_specs,
-        out_specs=pl.BlockSpec((rows, HEAD_DIM), lambda h: (0, h + first)),
+        out_specs=pl.BlockSpec((rows, width), lambda h: (0, h + skip)),
         out_shape=jax.ShapeDtypeStruct((rows, channels), jnp.bfloat16),
         input_output_aliases=aliases,
         compiler_params=compiler_params(),
@@ -403,7 +394,7 @@
         at += heads
     sent = []
     first, out, waits = 0, None, []
-    rv, earlier = None, None
+    rv, earlier, came_back = None, None, []
     for heads in plan.heads:
         if len(sent) < len(groups) and first == groups[len(sent)][0]:
             group = groups[len(sent)]
@@ -424,7 +415,7 @@
         waits = [x for x in (rv, qa, qb, rk, earlier) if x is not None]
         o, s, *parts = attend(
             plan,
-            starts,
+            after(starts, *(came_back[-2] if len(came_back) > 1 else [])),
             q,
             k,
             mix,
@@ -438,6 +429,7 @@
         earlier = s
         pairs = [p for p in (plan.a, plan.b) if p]
         others = [send(x, back(p)) for x, p in zip(parts, pairs)]
+        came_back.append(others)
         out = join(plan, o, s, others, first, channels, out)
         first += heads
     return mix, out

time: 158 us -> 141 us (0.89); the launches traced: 156 us -> 141 us
  Pallas kernels: 50.4 us -> 31.2 us
  waiting for transfers between devices: 57.5 us -> 63 us
    pallas_call x1, Pallas kernels: 21 us -> 11 us  [hyena(): pl.pallas_call(partial(hyena_kernel, starts.shape[0], group), grid=(chann...]
    pallas_call x4, Pallas kernels: 18.5 us -> 12.2 us  [attend(): pl.pallas_call(partial(attend_kernel, starts.shape[0], plan), grid=(heads...]
    ppermute x19, waiting for transfers between devices: 57.5 us -> 63 us  [run_plan(): send = lambda x, pairs: lax.ppermute(x, 'ctx', pairs)]
    pallas_call x4, Pallas kernels: 10.6 us -> 7.69 us  [join(): pl.pallas_call(partial(join_kernel, plan), grid=(wide // width,), in_spec...]
  transfers between devices with their start and end apart: 19 -> 19, of which waited for: 6 -> 8; matrix products, arithmetic and copies ran while one was open for 1% -> 1% of each run, Pallas kernels for 30% -> 21%
where the time goes in v1:
time: 141 us
  waiting for transfers between devices  63 us (45%)
  starting transfers between devices  40.6 us (29%)
  Pallas kernels  31.2 us (22%)
  local copies, waits for them, and re-layouts  4.76 us (3%)
    ppermute x19, waiting for transfers between devices, run_plan(): send = lambda x, pairs: lax.ppermute(x, 'ctx', pairs)  63 us
    ppermute x19, starting transfers between devices, run_plan(): send = lambda x, pairs: lax.ppermute(x, 'ctx', pairs)  40.6 us
    pallas_call x4, Pallas kernels, attend(): pl.pallas_call(partial(attend_kernel, starts.shape[0], plan), grid=(heads...  12.2 us
    pallas_call x1, Pallas kernels, hyena(): pl.pallas_call(partial(hyena_kernel, starts.shape[0], group), grid=(chann...  11 us
    pallas_call x4, Pallas kernels, join(): pl.pallas_call(partial(join_kernel, plan), grid=(wide // width,), in_spec...  7.69 us
    unnamed x16, local copies, waits for them, and re-layouts  2.96 us
  transfers between devices with their start and end apart: 19, of which 8 were waited for; matrix products, arithmetic and copies ran while one was open for 1% of the time, Pallas kernels for 21%

profile of v1, /device:TPU:26, one launch (start us, length us, event | category | flops | bytes accessed | tf_op | source)
XLA Modules:
  0.0 140.6 jit_solution(8923170238433759498)
XLA Ops:
  0.6 0.0 copy-start
  0.6 0.0 copy-start.1
  0.7 1.5 %copy-done.1 = bf16[384,2048]{1,0:T(8,128)(2,1)S(1)} copy-done((bf16[384,2048]{1,0:T(8,128)(2,1)S(1)}, bf16[384,2048]{1,0:T(8,128)(2,1)}, u32[]{:S(2)}) %copy-start.1) | copy-done | bytes 1572888
  2.2 1.4 %copy-done.2 = bf16[384,2048]{1,0:T(8,128)(2,1)S(1)} copy-done((bf16[384,2048]{1,0:T(8,128)(2,1)S(1)}, bf16[384,2048]{1,0:T(8,128)(2,1)}, u32[]{:S(2)}) %copy-start.2) | copy-done | bytes 1572888
  3.6 0.3 halo_product.1
  3.9 0.0 copy-start.7
  3.9 1.4 %collective-permute-start = (bf16[128,2048]{1,0:T(8,128)(2,1)S(1)}, bf16[128,2048]{1,0:T(8,128)(2,1)S(1)}, u32[]{:S(2)}, u32[]{:S(2)}) collective-permute-start(bf16[128,2048]{1,0:T(8,128)(2,1)S(1)} %halo_product.1), channel_id=1, source_target_pairs={{0,4},{4,8},{8,12},{1,5},{5,9},{9,13},{2,6},{6,10},{10,14},{3,7},{... | collective-permute-start | bytes 1572872 | tf_op jit(solution)/shard_map/ppermute | solution.py:382
  5.3 0.0 copy-done
  5.3 0.1 fusion.2
  5.4 4.5 %collective-permute-start.2 = (bf16[256,1024]{1,0:T(8,128)(2,1)S(1)}, bf16[256,1024]{1,0:T(8,128)(2,1)S(1)}, u32[]{:S(2)}, u32[]{:S(2)}) collective-permute-start(bf16[256,1024]{1,0:T(8,128)(2,1)S(1)} %get-tuple-element.57), channel_id=1, source_target_pairs={{12,4},{13,5},{14,6},{15,7},{28,20},{29,21},{30,22},{31,23}} | collective-permute-start | bytes 1572872 | tf_op jit(solution)/shard_map/ppermute | solution.py:382
  9.9 0.0 copy-done.7
  9.9 0.1 fusion.1
  10.1 0.0 copy-start.3
  10.1 0.0 copy-start.4
  10.1 0.0 copy-start.5
  10.1 0.0 copy-start.6
  10.1 0.8 collective-permute-start.3
  11.0 0.1 fusion.3
  11.1 1.3 collective-permute-start.1
  12.4 7.2 %collective-permute-done.halo = bf16[128,2048]{1,0:T(8,128)(2,1)S(1)} collective-permute-done((bf16[128,2048]{1,0:T(8,128)(2,1)S(1)}, bf16[128,2048]{1,0:T(8,128)(2,1)S(1)}, u32[]{:S(2)}, u32[]{:S(2)}) %collective-permute-start) | collective-permute-done | bytes 524320 | tf_op jit(solution)/shard_map/ppermute | solution.py:382
  19.6 0.0 copy-done.3
  19.6 11.0 %hyena_mix.1.v = bf16[384,2048]{1,0:T(8,128)(2,1)} custom-call(s32[4]{0:T(128)S(1)} %copy-done.3, bf16[384,2048]{1,0:T(8,128)(2,1)S(1)} %copy-done.4, bf16[384,2048]{1,0:T(8,128)(2,1)S(1)} %copy-done.1, bf16[384,2048]{1,0:T(8,128)(2,1)S(1)} %copy-done.2, bf16[128,2048]{1,0:T(8,128)(2,1)S(1)} %collective-permute-done.halo, bf16[128,128]{1,0:T(8,128)(2,1)S(1)} %copy-done.5, ...), custom_call_target="tpu_custom_call" | custom-call | flops 3221225472 | bytes 6291456 | tf_op jit(solution)/shard_map/hyena_mix/pallas_call | solution.py:116
  30.6 1.5 %fusion = (bf16[384,512]{1,0:T(8,128)(2,1)S(1)}, bf16[384,512]{1,0:T(8,128)(2,1)S(1)}, bf16[384,512]{1,0:T(8,128)(2,1)S(1)}, bf16[384,512]{1,0:T(8,128)(2,1)S(1)}) fusion(bf16[384,2048]{1,0:T(8,128)(2,1)} %hyena_mix.1.v), kind=kLoop, calls=%fused_computation | loop fusion | bytes 3145728 | tf_op jit(solution)/shard_map/slice | solution.py:414
  32.1 0.7 collective-permute-start.4
  32.8 0.0 collective-permute-done.2.rest_1_
  32.8 0.0 collective-permute-done.3.rest_2_
  32.8 4.9 %collective-permute-done.1.rest_0_ = bf16[384,1024]{1,0:T(8,128)(2,1)S(1)} collective-permute-done((bf16[384,1024]{1,0:T(8,128)(2,1)S(1)}, bf16[384,1024]{1,0:T(8,128)(2,1)S(1)}, u32[]{:S(2)}, u32[]{:S(2)}) %collective-permute-start.1) | collective-permute-done | bytes 786464 | tf_op jit(solution)/shard_map/ppermute | solution.py:382
  37.7 0.0 collective-permute-done.4.rest_3_
  37.7 0.7 collective-permute-start.5
  38.3 3.0 %attend_parts.5 = (bf16[384,512]{1,0:T(8,128)(2,1)S(1)}, f32[32,128]{1,0:T(8,128)S(1)}, bf16[416,512]{1,0:T(8,128)(2,1)S(1)}, bf16[288,512]{1,0:T(8,128)(2,1)S(1)}) custom-call(s32[4]{0:T(128)S(1)} %copy-done.3, bf16[384,2048]{1,0:T(8,128)(2,1)S(1)} %copy-done, bf16[384,2048]{1,0:T(8,128)(2,1)} %k.7, bf16[384,2048]{1,0:T(8,128)(2,1)} %hyena_mix.1.v, ...), custom_call_target="tpu_custom_call" | custom-call | flops 1610612736 | bytes 3670016 | tf_op jit(solution)/shard_map/attend_parts/pallas_call | solution.py:284
  41.4 0.0 collective-permute-done.5.rest_3_
  41.4 6.1 %collective-permute-start.8 = (bf16[384,1024]{1,0:T(8,128)(2,1)S(1)}, bf16[384,1024]{1,0:T(8,128)(2,1)S(1)}, u32[]{:S(2)}, u32[]{:S(2)}) collective-permute-start(bf16[384,1024]{1,0:T(8,128)(2,1)S(1)} %get-tuple-element.31), channel_id=1, source_target_pairs={{8,4},{12,8},{9,5},{13,9},{10,6},{14,10},{11,7},{15,11},{24,20},{2... | collective-permute-start | bytes 2359304 | tf_op jit(solution)/shard_map/ppermute | solution.py:382
  47.5 0.7 collective-permute-start.10
  48.2 12.3 %collective-permute-start.9 = (bf16[256,1024]{1,0:T(8,128)(2,1)S(1)}, bf16[256,1024]{1,0:T(8,128)(2,1)S(1)}, u32[]{:S(2)}, u32[]{:S(2)}) collective-permute-start(bf16[256,1024]{1,0:T(8,128)(2,1)S(1)} %get-tuple-element.32), channel_id=1, source_target_pairs={{12,4},{13,5},{14,6},{15,7},{28,20},{29,21},{30,22},{31,23}} | collective-permute-start | bytes 1572872 | tf_op jit(solution)/shard_map/ppermute | solution.py:382
  60.5 0.7 collective-permute-start.11
  61.2 1.5 %collective-permute-start.15 = (bf16[416,512]{1,0:T(8,128)(2,1)S(1)}, bf16[416,512]{1,0:T(8,128)(2,1)S(1)}, u32[]{:S(2)}, u32[]{:S(2)}) collective-permute-start(bf16[416,512]{1,0:T(8,128)(2,1)S(1)} %get-tuple-element.41), channel_id=1, source_target_pairs={{4,8},{8,12},{5,9},{9,13},{6,10},{10,14},{7,11},{11,15},{20,24},{2... | collective-permute-start | bytes 1277960 | tf_op jit(solution)/shard_map/ppermute | solution.py:382
  62.7 3.1 %attend_parts.4 = (bf16[384,512]{1,0:T(8,128)(2,1)S(1)}, f32[32,128]{1,0:T(8,128)S(1)}, bf16[416,512]{1,0:T(8,128)(2,1)S(1)}, bf16[288,512]{1,0:T(8,128)(2,1)S(1)}) custom-call(s32[4]{0:T(128)S(1)} %copy-done.3, bf16[384,2048]{1,0:T(8,128)(2,1)S(1)} %copy-done, bf16[384,2048]{1,0:T(8,128)(2,1)} %k.7, bf16[384,2048]{1,0:T(8,128)(2,1)} %hyena_mix.1.v, ...), custom_call_target="tpu_custom_call" | custom-call | flops 1610612736 | bytes 3670016 | tf_op jit(solution)/shard_map/attend_parts/pallas_call | solution.py:284
  65.7 0.0 collective-permute-done.11.rest_3_
  65.7 1.3 collective-permute-start.6
  67.0 7.6 %collective-permute-done.9.rest_1_ = bf16[256,1024]{1,0:T(8,128)(2,1)S(1)} collective-permute-done((bf16[256,1024]{1,0:T(8,128)(2,1)S(1)}, bf16[256,1024]{1,0:T(8,128)(2,1)S(1)}, u32[]{:S(2)}, u32[]{:S(2)}) %collective-permute-start.9) | collective-permute-done | bytes 524320 | tf_op jit(solution)/shard_map/ppermute | solution.py:382
  74.6 1.3 collective-permute-start.16
  75.9 0.0 collective-permute-done.8.rest_0_
  75.9 1.3 collective-permute-start.7
  77.2 0.0 collective-permute-done.10.rest_2_
  77.2 0.7 collective-permute-start.12
  77.9 22.7 %collective-permute-done.16.rest_1_ = bf16[288,512]{1,0:T(8,128)(2,1)S(1)} collective-permute-done((bf16[288,512]{1,0:T(8,128)(2,1)S(1)}, bf16[288,512]{1,0:T(8,128)(2,1)S(1)}, u32[]{:S(2)}, u32[]{:S(2)}) %collective-permute-start.16) | collective-permute-done | bytes 294944 | tf_op jit(solution)/shard_map/ppermute | solution.py:382
  100.6 0.0 collective-permute-done.15.rest_0_
  100.6 3.2 %collective-permute-done.7.rest_1_ = bf16[288,512]{1,0:T(8,128)(2,1)S(1)} collective-permute-done((bf16[288,512]{1,0:T(8,128)(2,1)S(1)}, bf16[288,512]{1,0:T(8,128)(2,1)S(1)}, u32[]{:S(2)}, u32[]{:S(2)}) %collective-permute-start.7) | collective-permute-done | bytes 294944 | tf_op jit(solution)/shard_map/ppermute | solution.py:382
  103.8 0.0 collective-permute-done.6.rest_0_
  103.8 3.0 %attend_parts.7 = (bf16[384,512]{1,0:T(8,128)(2,1)S(1)}, f32[32,128]{1,0:T(8,128)S(1)}, bf16[416,512]{1,0:T(8,128)(2,1)S(1)}, bf16[288,512]{1,0:T(8,128)(2,1)S(1)}) custom-call(s32[4]{0:T(128)S(1)} %copy-done.3, bf16[384,2048]{1,0:T(8,128)(2,1)S(1)} %copy-done, bf16[384,2048]{1,0:T(8,128)(2,1)} %k.7, bf16[384,2048]{1,0:T(8,128)(2,1)} %hyena_mix.1.v, ...), custom_call_target="tpu_custom_call" | custom-call | flops 1610612736 | bytes 3670016 | tf_op jit(solution)/shard_map/attend_parts/pallas_call | solution.py:284
  106.8 1.5 %collective-permute-start.17 = (bf16[416,512]{1,0:T(8,128)(2,1)S(1)}, bf16[416,512]{1,0:T(8,128)(2,1)S(1)}, u32[]{:S(2)}, u32[]{:S(2)}) collective-permute-start(bf16[416,512]{1,0:T(8,128)(2,1)S(1)} %get-tuple-element.46), channel_id=1, source_target_pairs={{4,8},{8,12},{5,9},{9,13},{6,10},{10,14},{7,11},{11,15},{20,24},{2... | collective-permute-start | bytes 1277960 | tf_op jit(solution)/shard_map/ppermute | solution.py:382
  108.4 0.0 collective-permute-done.12.rest_3_
  108.4 3.1 %attend_parts.6 = (bf16[384,512]{1,0:T(8,128)(2,1)S(1)}, f32[32,128]{1,0:T(8,128)S(1)}, bf16[416,512]{1,0:T(8,128)(2,1)S(1)}, bf16[288,512]{1,0:T(8,128)(2,1)S(1)}) custom-call(s32[4]{0:T(128)S(1)} %copy-done.3, bf16[384,2048]{1,0:T(8,128)(2,1)S(1)} %copy-done, bf16[384,2048]{1,0:T(8,128)(2,1)} %k.7, bf16[384,2048]{1,0:T(8,128)(2,1)} %hyena_mix.1.v, ...), custom_call_target="tpu_custom_call" | custom-call | flops 1610612736 | bytes 3670016 | tf_op jit(solution)/shard_map/attend_parts/pallas_call | solution.py:284
  111.5 1.3 collective-permute-start.13
  112.8 1.3 collective-permute-start.18
  114.1 1.3 collective-permute-start.14
  115.4 1.9 %join_parts.4.rest_2_ = bf16[384,2048]{1,0:T(8,128)(2,1)} custom-call(bf16[384,512]{1,0:T(8,128)(2,1)S(1)} %get-tuple-element.49.o, f32[32,128]{1,0:T(8,128)S(1)} %get-tuple-element.30.s, bf16[416,512]{1,0:T(8,128)(2,1)S(1)} %collective-permute-done.15.rest_0_, bf16[288,512]{1,0:T(8,128)(2,1)S(1)} %collective-permute-done.16.rest_1_), custom_call_target="tpu_custom_call" | custom-call | flops 1179648 | bytes 1572864 | tf_op jit(solution)/shard_map/join_parts/pallas_call | solution.py:345
  117.3 1.9 %join_parts.5.rest_2_ = bf16[384,2048]{1,0:T(8,128)(2,1)} custom-call(bf16[384,512]{1,0:T(8,128)(2,1)S(1)} %get-tuple-element.48.o, f32[32,128]{1,0:T(8,128)S(1)} %get-tuple-element.35.s, bf16[416,512]{1,0:T(8,128)(2,1)S(1)} %collective-permute-done.6.rest_0_, bf16[288,512]{1,0:T(8,128)(2,1)S(1)} %collective-permute-done.7.rest_1_, ...), custom_call_target="tpu_custom_call", output_to_operand_aliasing={{}: (4, {})} | custom-call | flops 1179648 | bytes 1572864 | tf_op jit(solution)/shard_map/join_parts/pallas_call | solution.py:345
  119.2 15.7 %collective-permute-done.18.rest_1_ = bf16[288,512]{1,0:T(8,128)(2,1)S(1)} collective-permute-done((bf16[288,512]{1,0:T(8,128)(2,1)S(1)}, bf16[288,512]{1,0:T(8,128)(2,1)S(1)}, u32[]{:S(2)}, u32[]{:S(2)}) %collective-permute-start.18) | collective-permute-done | bytes 294944 | tf_op jit(solution)/shard_map/ppermute | solution.py:382
  134.9 0.0 collective-permute-done.17.rest_0_
  134.9 1.9 %join_parts.6.rest_2_ = bf16[384,2048]{1,0:T(8,128)(2,1)} custom-call(bf16[384,512]{1,0:T(8,128)(2,1)S(1)} %get-tuple-element.44.o, f32[32,128]{1,0:T(8,128)S(1)} %get-tuple-element.45.s, bf16[416,512]{1,0:T(8,128)(2,1)S(1)} %collective-permute-done.17.rest_0_, bf16[288,512]{1,0:T(8,128)(2,1)S(1)} %collective-permute-done.18.rest_1_, ...), custom_call_target="tpu_custom_call", output_to_operand_aliasing={{}: (4, {})} | custom-call | flops 1179648 | bytes 1572864 | tf_op jit(solution)/shard_map/join_parts/pallas_call | solution.py:345
  136.8 1.2 collective-permute-done.14.rest_1_
  138.1 0.6 collective-permute-done.13.rest_0_
  138.6 1.9 %join_parts.7 = bf16[384,2048]{1,0:T(8,128)(2,1)} custom-call(bf16[384,512]{1,0:T(8,128)(2,1)S(1)} %get-tuple-element.37.o, f32[32,128]{1,0:T(8,128)S(1)} %get-tuple-element.38.s, bf16[416,512]{1,0:T(8,128)(2,1)S(1)} %collective-permute-done.13.rest_0_, bf16[288,512]{1,0:T(8,128)(2,1)S(1)} %collective-permute-done.14.rest_1_, ...), custom_call_target="tpu_custom_call", output_to_operand_aliasing={{}: (4, {})} | custom-call | flops 1179648 | bytes 1572864 | tf_op jit(solution)/shard_map/join_parts/pallas_call | solution.py:345
  (4 shorter events, 0.0 us)
Async XLA Ops:
  0.6 4.7 %copy-start = (bf16[384,2048]{1,0:T(8,128)(2,1)S(1)}, bf16[384,2048]{1,0:T(8,128)(2,1)}, u32[]{:S(2)}) copy-start(bf16[384,2048]{1,0:T(8,128)(2,1)} %q.7) | copy-start | bytes 4718596
  0.6 1.5 %copy-start.1 = (bf16[384,2048]{1,0:T(8,128)(2,1)S(1)}, bf16[384,2048]{1,0:T(8,128)(2,1)}, u32[]{:S(2)}) copy-start(bf16[384,2048]{1,0:T(8,128)(2,1)} %hk.3) | copy-start | bytes 4718596
  2.2 1.4 %copy-start.2 = (bf16[384,2048]{1,0:T(8,128)(2,1)S(1)}, bf16[384,2048]{1,0:T(8,128)(2,1)}, u32[]{:S(2)}) copy-start(bf16[384,2048]{1,0:T(8,128)(2,1)} %hv.3) | copy-start | bytes 4718596
  3.9 6.0 %copy-start.7 = (bf16[384,2048]{1,0:T(8,128)(2,1)S(1)}, bf16[384,2048]{1,0:T(8,128)(2,1)}, u32[]{:S(2)}) copy-start(bf16[384,2048]{1,0:T(8,128)(2,1)} %k.7) | copy-start | bytes 4718596
  3.9 15.7 %collective-permute-start = (bf16[128,2048]{1,0:T(8,128)(2,1)S(1)}, bf16[128,2048]{1,0:T(8,128)(2,1)S(1)}, u32[]{:S(2)}, u32[]{:S(2)}) collective-permute-start(bf16[128,2048]{1,0:T(8,128)(2,1)S(1)} %halo_product.1), channel_id=1, source_target_pairs={{0,4},{4,8},{8,12},{1,5},{5,9},{9,13},{2,6},{6,10},{10,14},{3,7},{... | collective-permute-start | bytes 1572872 | tf_op jit(solution)/shard_map/ppermute | solution.py:382
  5.4 27.3 %collective-permute-start.2 = (bf16[256,1024]{1,0:T(8,128)(2,1)S(1)}, bf16[256,1024]{1,0:T(8,128)(2,1)S(1)}, u32[]{:S(2)}, u32[]{:S(2)}) collective-permute-start(bf16[256,1024]{1,0:T(8,128)(2,1)S(1)} %get-tuple-element.57), channel_id=1, source_target_pairs={{12,4},{13,5},{14,6},{15,7},{28,20},{29,21},{30,22},{31,23}} | collective-permute-start | bytes 1572872 | tf_op jit(solution)/shard_map/ppermute | solution.py:382
  10.1 9.5 %copy-start.3 = (s32[4]{0:T(128)S(1)}, s32[4]{0:T(128)}, u32[]{:S(2)}) copy-start(s32[4]{0:T(128)} %info.5) | copy-start | bytes 52
  10.1 9.5 %copy-start.4 = (bf16[384,2048]{1,0:T(8,128)(2,1)S(1)}, bf16[384,2048]{1,0:T(8,128)(2,1)}, u32[]{:S(2)}) copy-start(bf16[384,2048]{1,0:T(8,128)(2,1)} %hq.1) | copy-start | bytes 4718596
  10.1 9.5 %copy-start.5 = (bf16[128,128]{1,0:T(8,128)(2,1)S(1)}, bf16[128,128]{1,0:T(8,128)(2,1)}, u32[]{:S(2)}) copy-start(bf16[128,128]{1,0:T(8,128)(2,1)} %filters.1) | copy-start | bytes 98308
  10.1 9.5 %copy-start.6 = (f32[2048]{0:T(1024)S(1)}, f32[2048]{0:T(1024)}, u32[]{:S(2)}) copy-start(f32[2048]{0:T(1024)} %param.12) | copy-start | bytes 24580
  10.1 22.7 %collective-permute-start.3 = (bf16[384,1024]{1,0:T(8,128)(2,1)S(1)}, bf16[384,1024]{1,0:T(8,128)(2,1)S(1)}, u32[]{:S(2)}, u32[]{:S(2)}) collective-permute-start(bf16[384,1024]{1,0:T(8,128)(2,1)S(1)} %get-tuple-element.55), channel_id=1, source_target_pairs={{0,4},{1,5},{2,6},{3,7},{16,20},{17,21},{18,22},{19,23}} | collective-permute-start | bytes 2359304 | tf_op jit(solution)/shard_map/ppermute | solution.py:382
  11.1 26.6 %collective-permute-start.1 = (bf16[384,1024]{1,0:T(8,128)(2,1)S(1)}, bf16[384,1024]{1,0:T(8,128)(2,1)S(1)}, u32[]{:S(2)}, u32[]{:S(2)}) collective-permute-start(bf16[384,1024]{1,0:T(8,128)(2,1)S(1)} %get-tuple-element.59), channel_id=1, source_target_pairs={{8,4},{12,8},{9,5},{13,9},{10,6},{14,10},{11,7},{15,11},{24,20},{2... | collective-permute-start | bytes 2359304 | tf_op jit(solution)/shard_map/ppermute | solution.py:382
  32.1 5.6 %collective-permute-start.4 = (bf16[384,512]{1,0:T(8,128)(2,1)S(1)}, bf16[384,512]{1,0:T(8,128)(2,1)S(1)}, u32[]{:S(2)}, u32[]{:S(2)}) collective-permute-start(bf16[384,512]{1,0:T(8,128)(2,1)S(1)} %get-tuple-element.52), channel_id=1, source_target_pairs={{0,4},{1,5},{2,6},{3,7},{16,20},{17,21},{18,22},{19,23}} | collective-permute-start | bytes 1179656 | tf_op jit(solution)/shard_map/ppermute | solution.py:382
  37.7 3.7 %collective-permute-start.5 = (bf16[384,512]{1,0:T(8,128)(2,1)S(1)}, bf16[384,512]{1,0:T(8,128)(2,1)S(1)}, u32[]{:S(2)}, u32[]{:S(2)}) collective-permute-start(bf16[384,512]{1,0:T(8,128)(2,1)S(1)} %get-tuple-element.26), channel_id=1, source_target_pairs={{0,4},{1,5},{2,6},{3,7},{16,20},{17,21},{18,22},{19,23}} | collective-permute-start | bytes 1179656 | tf_op jit(solution)/shard_map/ppermute | solution.py:382
  41.4 34.5 %collective-permute-start.8 = (bf16[384,1024]{1,0:T(8,128)(2,1)S(1)}, bf16[384,1024]{1,0:T(8,128)(2,1)S(1)}, u32[]{:S(2)}, u32[]{:S(2)}) collective-permute-start(bf16[384,1024]{1,0:T(8,128)(2,1)S(1)} %get-tuple-element.31), channel_id=1, source_target_pairs={{8,4},{12,8},{9,5},{13,9},{10,6},{14,10},{11,7},{15,11},{24,20},{2... | collective-permute-start | bytes 2359304 | tf_op jit(solution)/shard_map/ppermute | solution.py:382
  47.5 29.7 %collective-permute-start.10 = (bf16[384,1024]{1,0:T(8,128)(2,1)S(1)}, bf16[384,1024]{1,0:T(8,128)(2,1)S(1)}, u32[]{:S(2)}, u32[]{:S(2)}) collective-permute-start(bf16[384,1024]{1,0:T(8,128)(2,1)S(1)} %get-tuple-element.33), channel_id=1, source_target_pairs={{0,4},{1,5},{2,6},{3,7},{16,20},{17,21},{18,22},{19,23}} | collective-permute-start | bytes 2359304 | tf_op jit(solution)/shard_map/ppermute | solution.py:382
  48.2 26.4 %collective-permute-start.9 = (bf16[256,1024]{1,0:T(8,128)(2,1)S(1)}, bf16[256,1024]{1,0:T(8,128)(2,1)S(1)}, u32[]{:S(2)}, u32[]{:S(2)}) collective-permute-start(bf16[256,1024]{1,0:T(8,128)(2,1)S(1)} %get-tuple-element.32), channel_id=1, source_target_pairs={{12,4},{13,5},{14,6},{15,7},{28,20},{29,21},{30,22},{31,23}} | collective-permute-start | bytes 1572872 | tf_op jit(solution)/shard_map/ppermute | solution.py:382
  60.5 5.3 %collective-permute-start.11 = (bf16[384,512]{1,0:T(8,128)(2,1)S(1)}, bf16[384,512]{1,0:T(8,128)(2,1)S(1)}, u32[]{:S(2)}, u32[]{:S(2)}) collective-permute-start(bf16[384,512]{1,0:T(8,128)(2,1)S(1)} %get-tuple-element.34), channel_id=1, source_target_pairs={{0,4},{1,5},{2,6},{3,7},{16,20},{17,21},{18,22},{19,23}} | collective-permute-start | bytes 1179656 | tf_op jit(solution)/shard_map/ppermute | solution.py:382
  61.2 39.5 %collective-permute-start.15 = (bf16[416,512]{1,0:T(8,128)(2,1)S(1)}, bf16[416,512]{1,0:T(8,128)(2,1)S(1)}, u32[]{:S(2)}, u32[]{:S(2)}) collective-permute-start(bf16[416,512]{1,0:T(8,128)(2,1)S(1)} %get-tuple-element.41), channel_id=1, source_target_pairs={{4,8},{8,12},{5,9},{9,13},{6,10},{10,14},{7,11},{11,15},{20,24},{2... | collective-permute-start | bytes 1277960 | tf_op jit(solution)/shard_map/ppermute | solution.py:382
  65.7 38.1 %collective-permute-start.6 = (bf16[416,512]{1,0:T(8,128)(2,1)S(1)}, bf16[416,512]{1,0:T(8,128)(2,1)S(1)}, u32[]{:S(2)}, u32[]{:S(2)}) collective-permute-start(bf16[416,512]{1,0:T(8,128)(2,1)S(1)} %get-tuple-element.27), channel_id=1, source_target_pairs={{4,8},{8,12},{5,9},{9,13},{6,10},{10,14},{7,11},{11,15},{20,24},{2... | collective-permute-start | bytes 1277960 | tf_op jit(solution)/shard_map/ppermute | solution.py:382
  74.6 26.0 %collective-permute-start.16 = (bf16[288,512]{1,0:T(8,128)(2,1)S(1)}, bf16[288,512]{1,0:T(8,128)(2,1)S(1)}, u32[]{:S(2)}, u32[]{:S(2)}) collective-permute-start(bf16[288,512]{1,0:T(8,128)(2,1)S(1)} %get-tuple-element.42), channel_id=1, source_target_pairs={{4,12},{5,13},{6,14},{7,15},{20,28},{21,29},{22,30},{23,31}} | collective-permute-start | bytes 884744 | tf_op jit(solution)/shard_map/ppermute | solution.py:382
  75.9 27.9 %collective-permute-start.7 = (bf16[288,512]{1,0:T(8,128)(2,1)S(1)}, bf16[288,512]{1,0:T(8,128)(2,1)S(1)}, u32[]{:S(2)}, u32[]{:S(2)}) collective-permute-start(bf16[288,512]{1,0:T(8,128)(2,1)S(1)} %get-tuple-element.28), channel_id=1, source_target_pairs={{4,12},{5,13},{6,14},{7,15},{20,28},{21,29},{22,30},{23,31}} | collective-permute-start | bytes 884744 | tf_op jit(solution)/shard_map/ppermute | solution.py:382
  77.2 31.2 %collective-permute-start.12 = (bf16[384,512]{1,0:T(8,128)(2,1)S(1)}, bf16[384,512]{1,0:T(8,128)(2,1)S(1)}, u32[]{:S(2)}, u32[]{:S(2)}) collective-permute-start(bf16[384,512]{1,0:T(8,128)(2,1)S(1)} %get-tuple-element.36), channel_id=1, source_target_pairs={{0,4},{1,5},{2,6},{3,7},{16,20},{17,21},{18,22},{19,23}} | collective-permute-start | bytes 1179656 | tf_op jit(solution)/shard_map/ppermute | solution.py:382
  106.8 28.1 %collective-permute-start.17 = (bf16[416,512]{1,0:T(8,128)(2,1)S(1)}, bf16[416,512]{1,0:T(8,128)(2,1)S(1)}, u32[]{:S(2)}, u32[]{:S(2)}) collective-permute-start(bf16[416,512]{1,0:T(8,128)(2,1)S(1)} %get-tuple-element.46), channel_id=1, source_target_pairs={{4,8},{8,12},{5,9},{9,13},{6,10},{10,14},{7,11},{11,15},{20,24},{2... | collective-permute-start | bytes 1277960 | tf_op jit(solution)/shard_map/ppermute | solution.py:382
  111.5 27.2 %collective-permute-start.13 = (bf16[416,512]{1,0:T(8,128)(2,1)S(1)}, bf16[416,512]{1,0:T(8,128)(2,1)S(1)}, u32[]{:S(2)}, u32[]{:S(2)}) collective-permute-start(bf16[416,512]{1,0:T(8,128)(2,1)S(1)} %get-tuple-element.39), channel_id=1, source_target_pairs={{4,8},{8,12},{5,9},{9,13},{6,10},{10,14},{7,11},{11,15},{20,24},{2... | collective-permute-start | bytes 1277960 | tf_op jit(solution)/shard_map/ppermute | solution.py:382
  112.8 22.1 %collective-permute-start.18 = (bf16[288,512]{1,0:T(8,128)(2,1)S(1)}, bf16[288,512]{1,0:T(8,128)(2,1)S(1)}, u32[]{:S(2)}, u32[]{:S(2)}) collective-permute-start(bf16[288,512]{1,0:T(8,128)(2,1)S(1)} %get-tuple-element.47), channel_id=1, source_target_pairs={{4,12},{5,13},{6,14},{7,15},{20,28},{21,29},{22,30},{23,31}} | collective-permute-start | bytes 884744 | tf_op jit(solution)/shard_map/ppermute | solution.py:382
  114.1 24.0 %collective-permute-start.14 = (bf16[288,512]{1,0:T(8,128)(2,1)S(1)}, bf16[288,512]{1,0:T(8,128)(2,1)S(1)}, u32[]{:S(2)}, u32[]{:S(2)}) collective-permute-start(bf16[288,512]{1,0:T(8,128)(2,1)S(1)} %get-tuple-element.40), channel_id=1, source_target_pairs={{4,12},{5,13},{6,14},{7,15},{20,28},{21,29},{22,30},{23,31}} | collective-permute-start | bytes 884744 | tf_op jit(solution)/shard_map/ppermute | solution.py:382

commit v2 on v1

--- a/solution.py
+++ b/solution.py
@@ -14,6 +14,7 @@
 TO_LOG2 = math.log2(math.e) / math.sqrt(HEAD_DIM)
 VMEM_LIMIT = 48 * 1024 * 1024
 HEADS_AT_ONCE = 2
+SMALL = pl.CostEstimate(flops=1024, bytes_accessed=1024, transcendentals=0)
 STAT_ROWS = 32
 
 
@@ -47,9 +48,7 @@
         out_specs=pl.BlockSpec((BLOCK, width), lambda j: (0, j)),
         out_shape=jax.ShapeDtypeStruct((BLOCK, channels), jnp.bfloat16),
         compiler_params=compiler_params(),
-        cost_estimate=pl.CostEstimate(
-            flops=BLOCK * channels, bytes_accessed=6 * BLOCK * channels, transcendentals=0
-        ),
+        cost_estimate=SMALL,
         name="halo_product",
     )(hk, hv)
 
@@ -133,11 +132,7 @@
             pltpu.VMEM((rows // BLOCK, BLOCK, 2 * BLOCK), jnp.bfloat16),
         ],
         compiler_params=compiler_params(),
-        cost_estimate=pl.CostEstimate(
-            flops=2 * rows * channels * 2 * BLOCK * 8,
-            bytes_accessed=2 * rows * channels * 4,
-            transcendentals=0,
-        ),
+        cost_estimate=SMALL,
         name="hyena_mix",
     )(starts, hq, hk, hv, halo, filters, gain)
 
@@ -261,14 +256,16 @@
     rows = q.shape[0]
     width = HEADS_AT_ONCE * HEAD_DIM
     here = lambda r: pl.BlockSpec((r, width), lambda h: (0, h))
-    later = lambda r, skip: pl.BlockSpec((r, width), lambda h: (0, h + skip // HEADS_AT_ONCE))
+    later = lambda r, skip, row=0: pl.BlockSpec(
+        (r, width), lambda h: (row, h + skip // HEADS_AT_ONCE)
+    )
     whole = lambda r: later(r, first)
     in_specs = [pl.BlockSpec(memory_space=pltpu.SMEM), whole(rows), whole(rows), whole(rows)]
     operands = [starts, q, k, v]
-    for x, skip in (qa, qb, rk, rv):
-        if x is not None:
-            in_specs.append(later(x.shape[0], skip))
-            operands.append(x)
+    counts = (plan.na, plan.nb, plan.nk, plan.nk)
+    for (x, *at), count in zip((qa, qb, rk, rv), counts):
+        in_specs.append(later(count, *at))
+        operands.append(x)
     out_specs = [here(rows), pl.BlockSpec((HEADS_AT_ONCE * 8, BLOCK), lambda h: (h, 0))]
     out_shape = [
         jax.ShapeDtypeStruct((rows, heads * HEAD_DIM), jnp.bfloat16),
@@ -288,11 +285,7 @@
         out_specs=out_specs,
         out_shape=out_shape,
         compiler_params=compiler_params(),
-        cost_estimate=pl.CostEstimate(
-            flops=4 * heads * queries * keys * HEAD_DIM,
-            bytes_accessed=4 * heads * HEAD_DIM * (queries + keys),
-            transcendentals=heads * queries * keys,
-        ),
+        cost_estimate=SMALL,
         name="attend_parts",
     )(*operands)
 
@@ -350,22 +343,16 @@
         out_shape=jax.ShapeDtypeStruct((rows, channels), jnp.bfloat16),
         input_output_aliases=aliases,
         compiler_params=compiler_params(),
-        cost_estimate=pl.CostEstimate(
-            flops=6 * rows * wide, bytes_accessed=8 * rows * wide, transcendentals=0
-        ),
+        cost_estimate=SMALL,
         name="join_parts",
     )(*operands)
 
 
 class Plan:
-    def __init__(self, n, down_1, rows_1, down_2, rows_2, up, rows_up, heads, ahead):
-        self.a = [(l + 1, l) for l in down_1]
-        self.b = [(d + 2, d) for d in down_2]
-        self.k = [(l, l + 1) for l in up]
-        self.na = rows_1 if down_1 else 0
-        self.nb = rows_2 if down_2 else 0
-        self.nk = rows_up if up else 0
-        self.heads, self.ahead = heads, ahead
+    def __init__(self, rows, n, heads):
+        self.a, self.b, self.k = [(2, 1), (3, 2)], [(3, 1)], [(0, 1)]
+        self.na, self.nb, self.nk = rows, rows - BLOCK, rows
+        self.heads = heads
         ends = lambda pairs, side: [int(any(p[side] == d for p in pairs)) for d in range(n)]
         self.a_from, self.a_to = ends(self.a, 0), ends(self.a, 1)
         self.b_from, self.b_to = ends(self.b, 0), ends(self.b, 1)
@@ -373,7 +360,7 @@
 
 
 def after(value, *earlier):
-    return lax.optimization_barrier((value, *earlier))[0]
+    return lax.optimization_barrier((value, *earlier))[0] if earlier else value
 
 
 def run_plan(plan, hq, hk, hv, filters, gain, q, k, starts):
@@ -381,57 +368,39 @@
     rows, channels = hk.shape
     send = lambda x, pairs: lax.ppermute(x, "ctx", pairs)
     back = lambda pairs: [(t, s) for s, t in pairs]
+    columns = lambda x, first, end: x[:, first * HEAD_DIM : end * HEAD_DIM]
+
     halo = send(halo_product(hk, hv), [(i, i + 1) for i in range(n - 1)])
     mix = hyena(starts, hq, hk, hv, halo, filters, gain)
-
-    def ahead(whole, heads, pairs, waits):
-        cols = slice(heads[0] * HEAD_DIM, (heads[0] + heads[1]) * HEAD_DIM)
-        return send(after(whole[:, cols], *waits), pairs)
-
-    groups, at = [], 0
-    for heads in plan.ahead:
-        groups.append((at, heads))
-        at += heads
-    sent = []
-    first, out, waits = 0, None, []
-    rv, earlier, came_back = None, None, []
-    for heads in plan.heads:
-        if len(sent) < len(groups) and first == groups[len(sent)][0]:
-            group = groups[len(sent)]
-            got = [
-                ahead(x, group, pairs, waits) if pairs else None
-                for x, pairs in (
-                    (q[: plan.na], plan.a),
-                    (q[: plan.nb], plan.b),
-                    (k[rows - plan.nk :], plan.k),
-                )
-            ]
-            sent.append((group[0], got))
-        start, (qa, qb, rk) = sent[-1]
-        skip = first - start
-        if plan.nk:
-            cols = slice(first * HEAD_DIM, (first + heads) * HEAD_DIM)
-            rv = send(after(mix[rows - plan.nk :, cols], *waits), plan.k)
-        waits = [x for x in (rv, qa, qb, rk, earlier) if x is not None]
+    heads, total = plan.heads, channels // HEAD_DIM
+    early_keys, early_queries = sum(heads[:2]), sum(heads[:3])
+    rk = send(after(columns(k, 0, early_keys), halo), plan.k)
+    qa = send(columns(q, 0, early_queries), plan.a)
+    qb = send(columns(q[: plan.nb], 0, early_queries), plan.b)
+
+    told, came_back, out = [], [], None
+    first = q_at = 0
+    for c, many in enumerate(heads):
+        end = first + many
+        if first == early_queries:
+            q_at = first
+            qa = send(after(columns(q, first, total), *came_back[0]), plan.a)
+            qb = send(after(columns(q[: plan.nb], first, total), *came_back[0]), plan.b)
+        if end <= early_keys:
+            keys = (rk, first)
+            values = (send(columns(mix, first, end), plan.k), 0, 0)
+        else:
+            pair = jnp.concatenate([columns(k, first, end), columns(mix, first, end)])
+            pair = send(after(pair, told[c - 2]), plan.k)
+            keys, values = (pair, 0), (pair, 0, 1)
+        ready = after(starts, *came_back[c - 2]) if c >= 2 else starts
         o, s, *parts = attend(
-            plan,
-            after(starts, *(came_back[-2] if len(came_back) > 1 else [])),
-            q,
-            k,
-            mix,
-            (qa, skip),
-            (qb, skip),
-            (rk, skip),
-            (rv, 0),
-            first,
-            heads,
+            plan, ready, q, k, mix, (qa, first - q_at), (qb, first - q_at), keys, values, first, many
         )
-        earlier = s
-        pairs = [p for p in (plan.a, plan.b) if p]
-        others = [send(x, back(p)) for x, p in zip(parts, pairs)]
-        came_back.append(others)
-        out = join(plan, o, s, others, first, channels, out)
-        first += heads
+        told.append(s)
+        came_back.append([send(x, back(p)) for x, p in zip(parts, (plan.a, plan.b))])
+        out = join(plan, o, s, came_back[-1], first, channels, out)
+        first = end
     return mix, out
 
 
@@ -481,7 +450,7 @@
     gain = skip_gain[None, :]
     if n != 4:
         return run_gathered(hq, hk, hv, filters, gain, q, k, starts)
-    plan = Plan(n, [1, 2], rows, [1], rows - BLOCK, [0], rows, [4, 4, 4, 4], [8, 8])
+    plan = Plan(rows, n, [4, 4, 4, 4])
     return run_plan(plan, hq, hk, hv, filters, gain, q, k, starts)
 
 

time: 141 us -> 138 us (0.979); the launches traced: 141 us -> 139 us
  starting transfers between devices: 40.6 us -> 27.8 us
  waiting for transfers between devices: 63 us -> 74.5 us
    ppermute x19 -> x18, starting transfers between devices: 40.6 us -> 27.8 us  [run_plan(): send = lambda x, pairs: lax.ppermute(x, 'ctx', pairs)]
    ppermute x19 -> x18, waiting for transfers between devices: 63 us -> 74.5 us  [run_plan(): send = lambda x, pairs: lax.ppermute(x, 'ctx', pairs)]
    unnamed x16 -> x18, local copies, waits for them, and re-layouts: 2.96 us -> 2.97 us
  transfers between devices with their start and end apart: 19 -> 18, of which waited for: 8 -> 7; matrix products, arithmetic and copies ran while one was open for 1% -> 1% of each run, Pallas kernels for 21% -> 21%
where the time goes in v2:
time: 138 us; the launch traced here: 139 us
  waiting for transfers between devices  74.5 us (54%)
  Pallas kernels  31.1 us (23%)
  starting transfers between devices  27.8 us (20%)
  local copies, waits for them, and re-layouts  4.74 us (3%)
    ppermute x18, waiting for transfers between devices, run_plan(): send = lambda x, pairs: lax.ppermute(x, 'ctx', pairs)  74.5 us
    ppermute x18, starting transfers between devices, run_plan(): send = lambda x, pairs: lax.ppermute(x, 'ctx', pairs)  27.8 us
    pallas_call x4, Pallas kernels, attend(): pl.pallas_call(partial(attend_kernel, starts.shape[0], plan), grid=(heads...  12.1 us
    pallas_call x1, Pallas kernels, hyena(): pl.pallas_call(partial(hyena_kernel, starts.shape[0], group), grid=(chann...  11 us
    pallas_call x4, Pallas kernels, join(): pl.pallas_call(partial(join_kernel, plan), grid=(wide // width,), in_spec...  7.69 us
    unnamed x18, local copies, waits for them, and re-layouts  2.97 us
  transfers between devices with their start and end apart: 18, of which 7 were waited for; matrix products, arithmetic and copies ran while one was open for 1% of the time, Pallas kernels for 21%

profile of v2, /device:TPU:26, one launch (start us, length us, event | category | flops | bytes accessed | tf_op | source)
XLA Modules:
  0.0 139.2 jit_solution(12507079011032906471)
XLA Ops:
  0.7 1.5 %copy-done.3 = bf16[384,2048]{1,0:T(8,128)(2,1)S(1)} copy-done((bf16[384,2048]{1,0:T(8,128)(2,1)S(1)}, bf16[384,2048]{1,0:T(8,128)(2,1)}, u32[]{:S(2)}) %copy-start.3) | copy-done | bytes 1572888
  2.2 1.4 %copy-done.4 = bf16[384,2048]{1,0:T(8,128)(2,1)S(1)} copy-done((bf16[384,2048]{1,0:T(8,128)(2,1)S(1)}, bf16[384,2048]{1,0:T(8,128)(2,1)}, u32[]{:S(2)}) %copy-start.4) | copy-done | bytes 1572888
  3.6 0.3 halo_product.1
  3.9 0.0 copy-start.1
  3.9 1.4 %collective-permute-start = (bf16[128,2048]{1,0:T(8,128)(2,1)S(1)}, bf16[128,2048]{1,0:T(8,128)(2,1)S(1)}, u32[]{:S(2)}, u32[]{:S(2)}) collective-permute-start(bf16[128,2048]{1,0:T(8,128)(2,1)S(1)} %halo_product.1), channel_id=1, source_target_pairs={{0,4},{4,8},{8,12},{1,5},{5,9},{9,13},{2,6},{6,10},{10,14},{3,7},{... | collective-permute-start | bytes 1572872 | tf_op jit(solution)/shard_map/ppermute | solution.py:369
  5.3 0.0 copy-done
  5.3 0.1 slice.37
  5.4 0.0 copy-start.5
  5.5 0.0 copy-start.6
  5.5 0.0 copy-start.7
  5.5 0.0 copy-start.8
  5.5 4.8 %collective-permute-start.1 = (bf16[384,1536]{1,0:T(8,128)(2,1)S(1)}, bf16[384,1536]{1,0:T(8,128)(2,1)S(1)}, u32[]{:S(2)}, u32[]{:S(2)}) collective-permute-start(bf16[384,1536]{1,0:T(8,128)(2,1)S(1)} %slice.37), channel_id=1, source_target_pairs={{8,4},{12,8},{9,5},{13,9},{10,6},{14,10},{11,7},{15,11},{24,20},{2... | collective-permute-start | bytes 3538952 | tf_op jit(solution)/shard_map/ppermute | solution.py:369
  10.2 0.1 slice.38
  10.3 1.3 collective-permute-start.2
  11.7 0.1 slice.39
  11.7 7.9 %collective-permute-done.halo = bf16[128,2048]{1,0:T(8,128)(2,1)S(1)} collective-permute-done((bf16[128,2048]{1,0:T(8,128)(2,1)S(1)}, bf16[128,2048]{1,0:T(8,128)(2,1)S(1)}, u32[]{:S(2)}, u32[]{:S(2)}) %collective-permute-start) | collective-permute-done | bytes 524320 | tf_op jit(solution)/shard_map/ppermute | solution.py:369
  19.6 0.7 collective-permute-start.3
  20.3 0.0 copy-done.5
  20.3 0.0 copy-done.6
  20.3 0.0 copy-done.7
  20.3 11.0 %hyena_mix.1.v = bf16[384,2048]{1,0:T(8,128)(2,1)} custom-call(s32[4]{0:T(128)S(1)} %copy-done.7, bf16[384,2048]{1,0:T(8,128)(2,1)S(1)} %copy-done.5, bf16[384,2048]{1,0:T(8,128)(2,1)S(1)} %copy-done.3, bf16[384,2048]{1,0:T(8,128)(2,1)S(1)} %copy-done.4, bf16[128,2048]{1,0:T(8,128)(2,1)S(1)} %collective-permute-done.halo, bf16[128,128]{1,0:T(8,128)(2,1)S(1)} %copy-done.6, ...), custom_call_target="tpu_custom_call" | custom-call | flops 1024 | bytes 1024 | tf_op jit(solution)/shard_map/hyena_mix/pallas_call | solution.py:115
  31.3 1.5 %fusion.1 = (bf16[384,512]{1,0:T(8,128)(2,1)S(1)}, bf16[384,512]{1,0:T(8,128)(2,1)S(1)}, bf16[384,512]{1,0:T(8,128)(2,1)S(1)}, bf16[384,512]{1,0:T(8,128)(2,1)S(1)}) fusion(bf16[384,2048]{1,0:T(8,128)(2,1)} %hyena_mix.1.v), kind=kLoop, calls=%fused_computation.3 | loop fusion | bytes 3145728 | tf_op jit(solution)/shard_map/slice | solution.py:371
  32.8 0.7 collective-permute-start.7
  33.5 0.7 collective-permute-start.4
  34.2 0.1 fusion
  34.3 17.7 %collective-permute-done.2.rest_1_ = bf16[256,1536]{1,0:T(8,128)(2,1)S(1)} collective-permute-done((bf16[256,1536]{1,0:T(8,128)(2,1)S(1)}, bf16[256,1536]{1,0:T(8,128)(2,1)S(1)}, u32[]{:S(2)}, u32[]{:S(2)}) %collective-permute-start.2) | collective-permute-done | bytes 786464 | tf_op jit(solution)/shard_map/ppermute | solution.py:369
  52.0 0.0 collective-permute-done.7.rest_3_
  52.0 0.0 collective-permute-done.1.rest_0_
  52.0 0.0 collective-permute-done.3.rest_2_
  52.0 3.0 %attend_parts.5 = (bf16[384,512]{1,0:T(8,128)(2,1)S(1)}, f32[32,128]{1,0:T(8,128)S(1)}, bf16[416,512]{1,0:T(8,128)(2,1)S(1)}, bf16[288,512]{1,0:T(8,128)(2,1)S(1)}) custom-call(s32[4]{0:T(128)S(1)} %copy-done.7, bf16[384,2048]{1,0:T(8,128)(2,1)S(1)} %copy-done, bf16[384,2048]{1,0:T(8,128)(2,1)} %k.7, bf16[384,2048]{1,0:T(8,128)(2,1)} %hyena_mix.1.v, ...), custom_call_target="tpu_custom_call" | custom-call | flops 1024 | bytes 1024 | tf_op jit(solution)/shard_map/attend_parts/pallas_call | solution.py:281
  55.0 1.3 collective-permute-start.8
  56.3 0.1 pad_maximum_fusion
  56.4 0.9 collective-permute-start.15
  57.3 0.0 collective-permute-done.4.rest_3_
  57.3 3.1 %attend_parts.4 = (bf16[384,512]{1,0:T(8,128)(2,1)S(1)}, f32[32,128]{1,0:T(8,128)S(1)}, bf16[416,512]{1,0:T(8,128)(2,1)S(1)}, bf16[288,512]{1,0:T(8,128)(2,1)S(1)}) custom-call(s32[4]{0:T(128)S(1)} %copy-done.7, bf16[384,2048]{1,0:T(8,128)(2,1)S(1)} %copy-done, bf16[384,2048]{1,0:T(8,128)(2,1)} %k.7, bf16[384,2048]{1,0:T(8,128)(2,1)} %hyena_mix.1.v, ...), custom_call_target="tpu_custom_call" | custom-call | flops 1024 | bytes 1024 | tf_op jit(solution)/shard_map/attend_parts/pallas_call | solution.py:281
  60.4 0.7 collective-permute-start.12
  61.1 1.3 collective-permute-start.9
  62.4 1.3 collective-permute-start.6
  63.7 21.1 %collective-permute-done.9.rest_1_ = bf16[288,512]{1,0:T(8,128)(2,1)S(1)} collective-permute-done((bf16[288,512]{1,0:T(8,128)(2,1)S(1)}, bf16[288,512]{1,0:T(8,128)(2,1)S(1)}, u32[]{:S(2)}, u32[]{:S(2)}) %collective-permute-start.9) | collective-permute-done | bytes 294944 | tf_op jit(solution)/shard_map/ppermute | solution.py:369
  84.9 1.3 collective-permute-start.5
  86.2 0.0 collective-permute-done.8.rest_0_
  86.2 4.6 %collective-permute-start.10 = (bf16[384,512]{1,0:T(8,128)(2,1)S(1)}, bf16[384,512]{1,0:T(8,128)(2,1)S(1)}, u32[]{:S(2)}, u32[]{:S(2)}) collective-permute-start(bf16[384,512]{1,0:T(8,128)(2,1)S(1)} %slice.41), channel_id=1, source_target_pairs={{8,4},{12,8},{9,5},{13,9},{10,6},{14,10},{11,7},{15,11},{24,20},{2... | collective-permute-start | bytes 1179656 | tf_op jit(solution)/shard_map/ppermute | solution.py:369
  90.8 0.0 copy-start.2
  90.8 0.4 collective-permute-done.6.rest_1_
  91.2 1.5 %collective-permute-start.11 = (bf16[256,512]{1,0:T(8,128)(2,1)S(1)}, bf16[256,512]{1,0:T(8,128)(2,1)S(1)}, u32[]{:S(2)}, u32[]{:S(2)}) collective-permute-start(bf16[256,512]{1,0:T(8,128)(2,1)S(1)} %slice.43), channel_id=1, source_target_pairs={{12,4},{13,5},{14,6},{15,7},{28,20},{29,21},{30,22},{31,23}} | collective-permute-start | bytes 786440 | tf_op jit(solution)/shard_map/ppermute | solution.py:369
  92.7 5.5 %collective-permute-done.5.rest_0_ = bf16[416,512]{1,0:T(8,128)(2,1)S(1)} collective-permute-done((bf16[416,512]{1,0:T(8,128)(2,1)S(1)}, bf16[416,512]{1,0:T(8,128)(2,1)S(1)}, u32[]{:S(2)}, u32[]{:S(2)}) %collective-permute-start.5) | collective-permute-done | bytes 426016 | tf_op jit(solution)/shard_map/ppermute | solution.py:369
  98.2 0.0 collective-permute-done.15.rest_2_.rest_3_
  98.2 3.0 %attend_parts.7 = (bf16[384,512]{1,0:T(8,128)(2,1)S(1)}, f32[32,128]{1,0:T(8,128)S(1)}, bf16[416,512]{1,0:T(8,128)(2,1)S(1)}, bf16[288,512]{1,0:T(8,128)(2,1)S(1)}) custom-call(s32[4]{0:T(128)S(1)} %copy-done.7, bf16[384,2048]{1,0:T(8,128)(2,1)S(1)} %copy-done, bf16[384,2048]{1,0:T(8,128)(2,1)} %k.7, bf16[384,2048]{1,0:T(8,128)(2,1)} %hyena_mix.1.v, ...), custom_call_target="tpu_custom_call" | custom-call | flops 1024 | bytes 1024 | tf_op jit(solution)/shard_map/attend_parts/pallas_call | solution.py:281
  101.3 1.5 %collective-permute-start.16 = (bf16[416,512]{1,0:T(8,128)(2,1)S(1)}, bf16[416,512]{1,0:T(8,128)(2,1)S(1)}, u32[]{:S(2)}, u32[]{:S(2)}) collective-permute-start(bf16[416,512]{1,0:T(8,128)(2,1)S(1)} %get-tuple-element.44), channel_id=1, source_target_pairs={{4,8},{8,12},{5,9},{9,13},{6,10},{10,14},{7,11},{11,15},{20,24},{2... | collective-permute-start | bytes 1277960 | tf_op jit(solution)/shard_map/ppermute | solution.py:369
  102.8 0.0 collective-permute-done.11.rest_1_
  102.8 0.0 collective-permute-done.12.rest_2_.rest_3_
  102.8 0.0 collective-permute-done.10.rest_0_
  102.8 3.0 %attend_parts.6 = (bf16[384,512]{1,0:T(8,128)(2,1)S(1)}, f32[32,128]{1,0:T(8,128)S(1)}, bf16[416,512]{1,0:T(8,128)(2,1)S(1)}, bf16[288,512]{1,0:T(8,128)(2,1)S(1)}) custom-call(s32[4]{0:T(128)S(1)} %copy-done.7, bf16[384,2048]{1,0:T(8,128)(2,1)S(1)} %copy-done, bf16[384,2048]{1,0:T(8,128)(2,1)S(1)} %copy-done.2, bf16[384,2048]{1,0:T(8,128)(2,1)} %hyena_mix.1.v, ...), custom_call_target="tpu_custom_call" | custom-call | flops 1024 | bytes 1024 | tf_op jit(solution)/shard_map/attend_parts/pallas_call | solution.py:281
  105.8 1.3 collective-permute-start.13
  107.1 1.3 collective-permute-start.17
  108.4 1.3 collective-permute-start.14
  109.7 1.9 %join_parts.4.rest_2_ = bf16[384,2048]{1,0:T(8,128)(2,1)} custom-call(bf16[384,512]{1,0:T(8,128)(2,1)S(1)} %get-tuple-element.47.o, f32[32,128]{1,0:T(8,128)S(1)} %get-tuple-element.40.s, bf16[416,512]{1,0:T(8,128)(2,1)S(1)} %collective-permute-done.8.rest_0_, bf16[288,512]{1,0:T(8,128)(2,1)S(1)} %collective-permute-done.9.rest_1_), custom_call_target="tpu_custom_call" | custom-call | flops 1024 | bytes 1024 | tf_op jit(solution)/shard_map/join_parts/pallas_call | solution.py:338
  111.7 1.9 %join_parts.5.rest_2_ = bf16[384,2048]{1,0:T(8,128)(2,1)} custom-call(bf16[384,512]{1,0:T(8,128)(2,1)S(1)} %get-tuple-element.46.o, f32[32,128]{1,0:T(8,128)S(1)} %get-tuple-element.33.s, bf16[416,512]{1,0:T(8,128)(2,1)S(1)} %collective-permute-done.5.rest_0_, bf16[288,512]{1,0:T(8,128)(2,1)S(1)} %collective-permute-done.6.rest_1_, ...), custom_call_target="tpu_custom_call", output_to_operand_aliasing={{}: (4, {})} | custom-call | flops 1024 | bytes 1024 | tf_op jit(solution)/shard_map/join_parts/pallas_call | solution.py:338
  113.6 20.1 %collective-permute-done.17.rest_1_ = bf16[288,512]{1,0:T(8,128)(2,1)S(1)} collective-permute-done((bf16[288,512]{1,0:T(8,128)(2,1)S(1)}, bf16[288,512]{1,0:T(8,128)(2,1)S(1)}, u32[]{:S(2)}, u32[]{:S(2)}) %collective-permute-start.17) | collective-permute-done | bytes 294944 | tf_op jit(solution)/shard_map/ppermute | solution.py:369
  133.7 0.0 collective-permute-done.16.rest_0_
  133.7 1.9 %join_parts.6.rest_2_ = bf16[384,2048]{1,0:T(8,128)(2,1)} custom-call(bf16[384,512]{1,0:T(8,128)(2,1)S(1)} %get-tuple-element.42.o, f32[32,128]{1,0:T(8,128)S(1)} %get-tuple-element.43.s, bf16[416,512]{1,0:T(8,128)(2,1)S(1)} %collective-permute-done.16.rest_0_, bf16[288,512]{1,0:T(8,128)(2,1)S(1)} %collective-permute-done.17.rest_1_, ...), custom_call_target="tpu_custom_call", output_to_operand_aliasing={{}: (4, {})} | custom-call | flops 1024 | bytes 1024 | tf_op jit(solution)/shard_map/join_parts/pallas_call | solution.py:338
  135.7 1.7 %collective-permute-done.14.rest_1_ = bf16[288,512]{1,0:T(8,128)(2,1)S(1)} collective-permute-done((bf16[288,512]{1,0:T(8,128)(2,1)S(1)}, bf16[288,512]{1,0:T(8,128)(2,1)S(1)}, u32[]{:S(2)}, u32[]{:S(2)}) %collective-permute-start.14) | collective-permute-done | bytes 294944 | tf_op jit(solution)/shard_map/ppermute | solution.py:369
  137.3 0.0 collective-permute-done.13.rest_0_
  137.3 1.9 %join_parts.7 = bf16[384,2048]{1,0:T(8,128)(2,1)} custom-call(bf16[384,512]{1,0:T(8,128)(2,1)S(1)} %get-tuple-element.35.o, f32[32,128]{1,0:T(8,128)S(1)} %get-tuple-element.36.s, bf16[416,512]{1,0:T(8,128)(2,1)S(1)} %collective-permute-done.13.rest_0_, bf16[288,512]{1,0:T(8,128)(2,1)S(1)} %collective-permute-done.14.rest_1_, ...), custom_call_target="tpu_custom_call", output_to_operand_aliasing={{}: (4, {})} | custom-call | flops 1024 | bytes 1024 | tf_op jit(solution)/shard_map/join_parts/pallas_call | solution.py:338
  (8 shorter events, 0.1 us)
Async XLA Ops:
  0.6 4.7 %copy-start = (bf16[384,2048]{1,0:T(8,128)(2,1)S(1)}, bf16[384,2048]{1,0:T(8,128)(2,1)}, u32[]{:S(2)}) copy-start(bf16[384,2048]{1,0:T(8,128)(2,1)} %q.7) | copy-start | bytes 4718596
  0.6 1.5 %copy-start.3 = (bf16[384,2048]{1,0:T(8,128)(2,1)S(1)}, bf16[384,2048]{1,0:T(8,128)(2,1)}, u32[]{:S(2)}) copy-start(bf16[384,2048]{1,0:T(8,128)(2,1)} %hk.3) | copy-start | bytes 4718596
  2.2 1.4 %copy-start.4 = (bf16[384,2048]{1,0:T(8,128)(2,1)S(1)}, bf16[384,2048]{1,0:T(8,128)(2,1)}, u32[]{:S(2)}) copy-start(bf16[384,2048]{1,0:T(8,128)(2,1)} %hv.3) | copy-start | bytes 4718596
  3.9 7.8 %copy-start.1 = (bf16[384,2048]{1,0:T(8,128)(2,1)S(1)}, bf16[384,2048]{1,0:T(8,128)(2,1)}, u32[]{:S(2)}) copy-start(bf16[384,2048]{1,0:T(8,128)(2,1)} %k.7) | copy-start | bytes 4718596
  3.9 15.7 %collective-permute-start = (bf16[128,2048]{1,0:T(8,128)(2,1)S(1)}, bf16[128,2048]{1,0:T(8,128)(2,1)S(1)}, u32[]{:S(2)}, u32[]{:S(2)}) collective-permute-start(bf16[128,2048]{1,0:T(8,128)(2,1)S(1)} %halo_product.1), channel_id=1, source_target_pairs={{0,4},{4,8},{8,12},{1,5},{5,9},{9,13},{2,6},{6,10},{10,14},{3,7},{... | collective-permute-start | bytes 1572872 | tf_op jit(solution)/shard_map/ppermute | solution.py:369
  5.4 14.9 %copy-start.5 = (bf16[384,2048]{1,0:T(8,128)(2,1)S(1)}, bf16[384,2048]{1,0:T(8,128)(2,1)}, u32[]{:S(2)}) copy-start(bf16[384,2048]{1,0:T(8,128)(2,1)} %hq.1) | copy-start | bytes 4718596
  5.5 14.9 %copy-start.6 = (bf16[128,128]{1,0:T(8,128)(2,1)S(1)}, bf16[128,128]{1,0:T(8,128)(2,1)}, u32[]{:S(2)}) copy-start(bf16[128,128]{1,0:T(8,128)(2,1)} %filters.1) | copy-start | bytes 98308
  5.5 14.9 %copy-start.7 = (s32[4]{0:T(128)S(1)}, s32[4]{0:T(128)}, u32[]{:S(2)}) copy-start(s32[4]{0:T(128)} %info.7) | copy-start | bytes 52
  5.5 14.9 %copy-start.8 = (f32[2048]{0:T(1024)S(1)}, f32[2048]{0:T(1024)}, u32[]{:S(2)}) copy-start(f32[2048]{0:T(1024)} %param.12) | copy-start | bytes 24580
  5.5 46.5 %collective-permute-start.1 = (bf16[384,1536]{1,0:T(8,128)(2,1)S(1)}, bf16[384,1536]{1,0:T(8,128)(2,1)S(1)}, u32[]{:S(2)}, u32[]{:S(2)}) collective-permute-start(bf16[384,1536]{1,0:T(8,128)(2,1)S(1)} %slice.37), channel_id=1, source_target_pairs={{8,4},{12,8},{9,5},{13,9},{10,6},{14,10},{11,7},{15,11},{24,20},{2... | collective-permute-start | bytes 3538952 | tf_op jit(solution)/shard_map/ppermute | solution.py:369
  10.3 41.6 %collective-permute-start.2 = (bf16[256,1536]{1,0:T(8,128)(2,1)S(1)}, bf16[256,1536]{1,0:T(8,128)(2,1)S(1)}, u32[]{:S(2)}, u32[]{:S(2)}) collective-permute-start(bf16[256,1536]{1,0:T(8,128)(2,1)S(1)} %slice.38), channel_id=1, source_target_pairs={{12,4},{13,5},{14,6},{15,7},{28,20},{29,21},{30,22},{31,23}} | collective-permute-start | bytes 2359304 | tf_op jit(solution)/shard_map/ppermute | solution.py:369
  19.6 32.4 %collective-permute-start.3 = (bf16[384,1024]{1,0:T(8,128)(2,1)S(1)}, bf16[384,1024]{1,0:T(8,128)(2,1)S(1)}, u32[]{:S(2)}, u32[]{:S(2)}) collective-permute-start(bf16[384,1024]{1,0:T(8,128)(2,1)S(1)} %slice.39), channel_id=1, source_target_pairs={{0,4},{1,5},{2,6},{3,7},{16,20},{17,21},{18,22},{19,23}} | collective-permute-start | bytes 2359304 | tf_op jit(solution)/shard_map/ppermute | solution.py:369
  32.8 19.2 %collective-permute-start.7 = (bf16[384,512]{1,0:T(8,128)(2,1)S(1)}, bf16[384,512]{1,0:T(8,128)(2,1)S(1)}, u32[]{:S(2)}, u32[]{:S(2)}) collective-permute-start(bf16[384,512]{1,0:T(8,128)(2,1)S(1)} %get-tuple-element.52), channel_id=1, source_target_pairs={{0,4},{1,5},{2,6},{3,7},{16,20},{17,21},{18,22},{19,23}} | collective-permute-start | bytes 1179656 | tf_op jit(solution)/shard_map/ppermute | solution.py:369
  33.5 23.8 %collective-permute-start.4 = (bf16[384,512]{1,0:T(8,128)(2,1)S(1)}, bf16[384,512]{1,0:T(8,128)(2,1)S(1)}, u32[]{:S(2)}, u32[]{:S(2)}) collective-permute-start(bf16[384,512]{1,0:T(8,128)(2,1)S(1)} %get-tuple-element.53), channel_id=1, source_target_pairs={{0,4},{1,5},{2,6},{3,7},{16,20},{17,21},{18,22},{19,23}} | collective-permute-start | bytes 1179656 | tf_op jit(solution)/shard_map/ppermute | solution.py:369
  55.0 31.2 %collective-permute-start.8 = (bf16[416,512]{1,0:T(8,128)(2,1)S(1)}, bf16[416,512]{1,0:T(8,128)(2,1)S(1)}, u32[]{:S(2)}, u32[]{:S(2)}) collective-permute-start(bf16[416,512]{1,0:T(8,128)(2,1)S(1)} %get-tuple-element.29), channel_id=1, source_target_pairs={{4,8},{8,12},{5,9},{9,13},{6,10},{10,14},{7,11},{11,15},{20,24},{2... | collective-permute-start | bytes 1277960 | tf_op jit(solution)/shard_map/ppermute | solution.py:369
  56.4 41.8 %collective-permute-start.15 = (bf16[768,512]{1,0:T(8,128)(2,1)S(1)}, bf16[768,512]{1,0:T(8,128)(2,1)S(1)}, u32[]{:S(2)}, u32[]{:S(2)}) collective-permute-start(bf16[768,512]{1,0:T(8,128)(2,1)S(1)} %get-tuple-element.41), channel_id=1, source_target_pairs={{0,4},{1,5},{2,6},{3,7},{16,20},{17,21},{18,22},{19,23}} | collective-permute-start | bytes 2359304 | tf_op jit(solution)/shard_map/ppermute | solution.py:369
  60.4 42.4 %collective-permute-start.12 = (bf16[768,512]{1,0:T(8,128)(2,1)S(1)}, bf16[768,512]{1,0:T(8,128)(2,1)S(1)}, u32[]{:S(2)}, u32[]{:S(2)}) collective-permute-start(bf16[768,512]{1,0:T(8,128)(2,1)S(1)} %get-tuple-element.34), channel_id=1, source_target_pairs={{0,4},{1,5},{2,6},{3,7},{16,20},{17,21},{18,22},{19,23}} | collective-permute-start | bytes 2359304 | tf_op jit(solution)/shard_map/ppermute | solution.py:369
  61.1 23.7 %collective-permute-start.9 = (bf16[288,512]{1,0:T(8,128)(2,1)S(1)}, bf16[288,512]{1,0:T(8,128)(2,1)S(1)}, u32[]{:S(2)}, u32[]{:S(2)}) collective-permute-start(bf16[288,512]{1,0:T(8,128)(2,1)S(1)} %get-tuple-element.30), channel_id=1, source_target_pairs={{4,12},{5,13},{6,14},{7,15},{20,28},{21,29},{22,30},{23,31}} | collective-permute-start | bytes 884744 | tf_op jit(solution)/shard_map/ppermute | solution.py:369
  62.4 28.8 %collective-permute-start.6 = (bf16[288,512]{1,0:T(8,128)(2,1)S(1)}, bf16[288,512]{1,0:T(8,128)(2,1)S(1)}, u32[]{:S(2)}, u32[]{:S(2)}) collective-permute-start(bf16[288,512]{1,0:T(8,128)(2,1)S(1)} %get-tuple-element.27), channel_id=1, source_target_pairs={{4,12},{5,13},{6,14},{7,15},{20,28},{21,29},{22,30},{23,31}} | collective-permute-start | bytes 884744 | tf_op jit(solution)/shard_map/ppermute | solution.py:369
  84.9 13.3 %collective-permute-start.5 = (bf16[416,512]{1,0:T(8,128)(2,1)S(1)}, bf16[416,512]{1,0:T(8,128)(2,1)S(1)}, u32[]{:S(2)}, u32[]{:S(2)}) collective-permute-start(bf16[416,512]{1,0:T(8,128)(2,1)S(1)} %get-tuple-element.26), channel_id=1, source_target_pairs={{4,8},{8,12},{5,9},{9,13},{6,10},{10,14},{7,11},{11,15},{20,24},{2... | collective-permute-start | bytes 1277960 | tf_op jit(solution)/shard_map/ppermute | solution.py:369
  86.2 16.6 %collective-permute-start.10 = (bf16[384,512]{1,0:T(8,128)(2,1)S(1)}, bf16[384,512]{1,0:T(8,128)(2,1)S(1)}, u32[]{:S(2)}, u32[]{:S(2)}) collective-permute-start(bf16[384,512]{1,0:T(8,128)(2,1)S(1)} %slice.41), channel_id=1, source_target_pairs={{8,4},{12,8},{9,5},{13,9},{10,6},{14,10},{11,7},{15,11},{24,20},{2... | collective-permute-start | bytes 1179656 | tf_op jit(solution)/shard_map/ppermute | solution.py:369
  90.8 12.0 %copy-start.2 = (bf16[384,2048]{1,0:T(8,128)(2,1)S(1)}, bf16[384,2048]{1,0:T(8,128)(2,1)}, u32[]{:S(2)}) copy-start(bf16[384,2048]{1,0:T(8,128)(2,1)} %k.7) | copy-start | bytes 4718596
  91.2 11.6 %collective-permute-start.11 = (bf16[256,512]{1,0:T(8,128)(2,1)S(1)}, bf16[256,512]{1,0:T(8,128)(2,1)S(1)}, u32[]{:S(2)}, u32[]{:S(2)}) collective-permute-start(bf16[256,512]{1,0:T(8,128)(2,1)S(1)} %slice.43), channel_id=1, source_target_pairs={{12,4},{13,5},{14,6},{15,7},{28,20},{29,21},{30,22},{31,23}} | collective-permute-start | bytes 786440 | tf_op jit(solution)/shard_map/ppermute | solution.py:369
  101.3 32.5 %collective-permute-start.16 = (bf16[416,512]{1,0:T(8,128)(2,1)S(1)}, bf16[416,512]{1,0:T(8,128)(2,1)S(1)}, u32[]{:S(2)}, u32[]{:S(2)}) collective-permute-start(bf16[416,512]{1,0:T(8,128)(2,1)S(1)} %get-tuple-element.44), channel_id=1, source_target_pairs={{4,8},{8,12},{5,9},{9,13},{6,10},{10,14},{7,11},{11,15},{20,24},{2... | collective-permute-start | bytes 1277960 | tf_op jit(solution)/shard_map/ppermute | solution.py:369
  105.8 31.5 %collective-permute-start.13 = (bf16[416,512]{1,0:T(8,128)(2,1)S(1)}, bf16[416,512]{1,0:T(8,128)(2,1)S(1)}, u32[]{:S(2)}, u32[]{:S(2)}) collective-permute-start(bf16[416,512]{1,0:T(8,128)(2,1)S(1)} %get-tuple-element.37), channel_id=1, source_target_pairs={{4,8},{8,12},{5,9},{9,13},{6,10},{10,14},{7,11},{11,15},{20,24},{2... | collective-permute-start | bytes 1277960 | tf_op jit(solution)/shard_map/ppermute | solution.py:369
  107.1 26.6 %collective-permute-start.17 = (bf16[288,512]{1,0:T(8,128)(2,1)S(1)}, bf16[288,512]{1,0:T(8,128)(2,1)S(1)}, u32[]{:S(2)}, u32[]{:S(2)}) collective-permute-start(bf16[288,512]{1,0:T(8,128)(2,1)S(1)} %get-tuple-element.45), channel_id=1, source_target_pairs={{4,12},{5,13},{6,14},{7,15},{20,28},{21,29},{22,30},{23,31}} | collective-permute-start | bytes 884744 | tf_op jit(solution)/shard_map/ppermute | solution.py:369
  108.4 28.9 %collective-permute-start.14 = (bf16[288,512]{1,0:T(8,128)(2,1)S(1)}, bf16[288,512]{1,0:T(8,128)(2,1)S(1)}, u32[]{:S(2)}, u32[]{:S(2)}) collective-permute-start(bf16[288,512]{1,0:T(8,128)(2,1)S(1)} %get-tuple-element.38), channel_id=1, source_target_pairs={{4,12},{5,13},{6,14},{7,15},{20,28},{21,29},{22,30},{23,31}} | collective-permute-start | bytes 884744 | tf_op jit(solution)/shard_map/ppermute | solution.py:369

commit v3 on v2

--- a/solution.py
+++ b/solution.py
@@ -15,7 +15,7 @@
 VMEM_LIMIT = 48 * 1024 * 1024
 HEADS_AT_ONCE = 2
 SMALL = pl.CostEstimate(flops=1024, bytes_accessed=1024, transcendentals=0)
-STAT_ROWS = 32
+STAT_ROWS = 16
 
 
 def begin_of(pos, starts):
@@ -39,7 +39,7 @@
 
 def halo_product(hk, hv):
     rows, channels = hk.shape
-    width = min(channels, 512)
+    width = min(channels, 1024)
     last = pl.BlockSpec((BLOCK, width), lambda j: (rows // BLOCK - 1, j))
     return pl.pallas_call(
         halo_kernel,
@@ -47,7 +47,7 @@
         in_specs=[last, last],
         out_specs=pl.BlockSpec((BLOCK, width), lambda j: (0, j)),
         out_shape=jax.ShapeDtypeStruct((BLOCK, channels), jnp.bfloat16),
-        compiler_params=compiler_params(),
+        compiler_params=pltpu.CompilerParams(vmem_limit_bytes=60 * 1024 * 1024),
         cost_estimate=SMALL,
         name="halo_product",
     )(hk, hv)
@@ -245,10 +245,12 @@
 
 
 def carry(out, count, h, stat):
+    row = lax.broadcasted_iota(jnp.int32, stat.shape, 0)
+    stat = jnp.where(row < count // BLOCK, stat, 0.0)
     high = stat.astype(jnp.bfloat16).astype(jnp.float32)
     middle = (stat - high).astype(jnp.bfloat16).astype(jnp.float32)
     low = stat - high - middle
-    parts = jnp.concatenate([high, middle, low, jnp.zeros_like(low)])
+    parts = jnp.concatenate([high + pltpu.roll(low, 4, 0), middle])
     out[count:, h * HEAD_DIM : (h + 1) * HEAD_DIM] = parts.astype(jnp.bfloat16)
 
 
@@ -305,7 +307,8 @@
         stats = [s[h * 8 : (h + 1) * 8, :]]
         for part, count, on in parts[1:]:
             carried = part[count:, lanes].astype(jnp.float32)
-            stats.append(jnp.where(on, carried[:8] + carried[8:16] + carried[16:24], FAR))
+            stat = carried[:8] + pltpu.roll(carried[:8], 4, 0) + carried[8:]
+            stats.append(jnp.where(on, stat, FAR))
         top = stats[0]
         for x in stats[1:]:
             top = jnp.maximum(top, x)
@@ -373,25 +376,26 @@
     halo = send(halo_product(hk, hv), [(i, i + 1) for i in range(n - 1)])
     mix = hyena(starts, hq, hk, hv, halo, filters, gain)
     heads, total = plan.heads, channels // HEAD_DIM
-    early_keys, early_queries = sum(heads[:2]), sum(heads[:3])
-    rk = send(after(columns(k, 0, early_keys), halo), plan.k)
-    qa = send(columns(q, 0, early_queries), plan.a)
-    qb = send(columns(q[: plan.nb], 0, early_queries), plan.b)
-
-    told, came_back, out = [], [], None
+    early = sum(heads[:2])
+    rk = send(after(columns(k, 0, early), halo), plan.k)
+    qa = send(columns(q, 0, early), plan.a)
+    qb = send(columns(q[: plan.nb], 0, early), plan.b)
+    later_a = send(after(columns(q, early, total), halo), plan.a)
+    later_b = send(after(columns(q[: plan.nb], early, total), halo), plan.b)
+
+    told, came_back, out, go = [], [], None, None
     first = q_at = 0
     for c, many in enumerate(heads):
         end = first + many
-        if first == early_queries:
-            q_at = first
-            qa = send(after(columns(q, first, total), *came_back[0]), plan.a)
-            qb = send(after(columns(q[: plan.nb], first, total), *came_back[0]), plan.b)
-        if end <= early_keys:
+        if first == early:
+            q_at, qa, qb = first, later_a, later_b
+        if end <= early:
             keys = (rk, first)
             values = (send(columns(mix, first, end), plan.k), 0, 0)
+            go = values[0] if go is None else go
         else:
             pair = jnp.concatenate([columns(k, first, end), columns(mix, first, end)])
-            pair = send(after(pair, told[c - 2]), plan.k)
+            pair = send(after(pair, told[c - 3] if c >= 3 else go), plan.k)
             keys, values = (pair, 0), (pair, 0, 1)
         ready = after(starts, *came_back[c - 2]) if c >= 2 else starts
         o, s, *parts = attend(
@@ -450,7 +454,7 @@
     gain = skip_gain[None, :]
     if n != 4:
         return run_gathered(hq, hk, hv, filters, gain, q, k, starts)
-    plan = Plan(rows, n, [4, 4, 4, 4])
+    plan = Plan(rows, n, [4, 4, 4, 2, 2])
     return run_plan(plan, hq, hk, hv, filters, gain, q, k, starts)
 
 

time: 138 us -> 124 us (0.90)
  the two profiles are of different devices: /device:TPU:26 before, /device:TPU:8 now
where the time goes in v3:
time: 124 us
  Pallas kernels  54.5 us (44%)
  starting transfers between devices  34.5 us (28%)
  waiting for transfers between devices  30.7 us (25%)
  local copies, waits for them, and re-layouts  2.79 us (2%)
    ppermute x21, starting transfers between devices, run_plan(): send = lambda x, pairs: lax.ppermute(x, 'ctx', pairs)  34.5 us
    pallas_call x5, Pallas kernels, attend(): pl.pallas_call(partial(attend_kernel, starts.shape[0], plan), grid=(heads...  33.2 us
    ppermute x21, waiting for transfers between devices, run_plan(): send = lambda x, pairs: lax.ppermute(x, 'ctx', pairs)  30.7 us
    pallas_call x1, Pallas kernels, hyena(): pl.pallas_call(partial(hyena_kernel, starts.shape[0], group), grid=(chann...  11 us
    pallas_call x5, Pallas kernels, join(): pl.pallas_call(partial(join_kernel, plan), grid=(wide // width,), in_spec...  8.25 us
    slice x8, local copies, waits for them, and re-layouts, run_plan(): columns = lambda x, first, end: x[:, first * HEAD_DIM:end * HEAD_DIM]  2.73 us
  transfers between devices with their start and end apart: 21, of which 4 were waited for; matrix products, arithmetic and copies ran while one was open for 2% of the time, Pallas kernels for 41%

profile of v3, /device:TPU:8, one launch (start us, length us, event | category | flops | bytes accessed | tf_op | source)
XLA Modules:
  0.0 123.7 jit_solution(13406257430490444229)
XLA Ops:
  0.6 2.1 %halo_product.1 = bf16[128,2048]{1,0:T(8,128)(2,1)} custom-call(bf16[384,2048]{1,0:T(8,128)(2,1)} %hk.3, bf16[384,2048]{1,0:T(8,128)(2,1)} %hv.3), custom_call_target="tpu_custom_call" | custom-call | flops 1024 | bytes 1024 | tf_op jit(solution)/shard_map/halo_product/pallas_call | solution.py:44
  2.7 3.5 %collective-permute-start = (bf16[128,2048]{1,0:T(8,128)(2,1)}, bf16[128,2048]{1,0:T(8,128)(2,1)S(1)}, u32[]{:S(2)}, u32[]{:S(2)}) collective-permute-start(bf16[128,2048]{1,0:T(8,128)(2,1)} %halo_product.1), channel_id=1, source_target_pairs={{0,4},{4,8},{8,12},{1,5},{5,9},{9,13},{2,6},{6,10},{10,14},{3,7},{... | collective-permute-start | bytes 1572872 | tf_op jit(solution)/shard_map/ppermute | solution.py:372
  6.2 0.0 copy-start.6
  6.2 0.0 copy-start.7
  6.2 0.0 copy-start.9
  6.2 0.1 fusion.3
  6.3 0.0 copy-start.1
  6.3 1.6 %collective-permute-start.2 = (bf16[256,1024]{1,0:T(8,128)(2,1)S(1)}, bf16[256,1024]{1,0:T(8,128)(2,1)S(1)}, u32[]{:S(2)}, u32[]{:S(2)}) collective-permute-start(bf16[256,1024]{1,0:T(8,128)(2,1)S(1)} %get-tuple-element.68), channel_id=1, source_target_pairs={{12,4},{13,5},{14,6},{15,7},{28,20},{29,21},{30,22},{31,23}} | collective-permute-start | bytes 1572872 | tf_op jit(solution)/shard_map/ppermute | solution.py:372
  7.9 0.0 copy-start.5
  7.9 0.1 fusion.4
  8.1 0.0 copy-start.4
  8.1 0.0 copy-start.8
  8.1 1.6 %collective-permute-start.1 = (bf16[384,1024]{1,0:T(8,128)(2,1)S(1)}, bf16[384,1024]{1,0:T(8,128)(2,1)S(1)}, u32[]{:S(2)}, u32[]{:S(2)}) collective-permute-start(bf16[384,1024]{1,0:T(8,128)(2,1)S(1)} %get-tuple-element.70), channel_id=1, source_target_pairs={{8,4},{12,8},{9,5},{13,9},{10,6},{14,10},{11,7},{15,11},{24,20},{2... | collective-permute-start | bytes 2359304 | tf_op jit(solution)/shard_map/ppermute | solution.py:372
  9.7 0.1 slice.45
  9.7 8.7 %collective-permute-done.halo = bf16[128,2048]{1,0:T(8,128)(2,1)S(1)} collective-permute-done((bf16[128,2048]{1,0:T(8,128)(2,1)}, bf16[128,2048]{1,0:T(8,128)(2,1)S(1)}, u32[]{:S(2)}, u32[]{:S(2)}) %collective-permute-start) | collective-permute-done | bytes 524320 | tf_op jit(solution)/shard_map/ppermute | solution.py:372
  18.5 1.3 %collective-permute-start.3 = (bf16[384,1024]{1,0:T(8,128)(2,1)S(1)}, bf16[384,1024]{1,0:T(8,128)(2,1)S(1)}, u32[]{:S(2)}, u32[]{:S(2)}) collective-permute-start(bf16[384,1024]{1,0:T(8,128)(2,1)S(1)} %slice.45), channel_id=1, source_target_pairs={{0,4},{1,5},{2,6},{3,7},{16,20},{17,21},{18,22},{19,23}} | collective-permute-start | bytes 2359304 | tf_op jit(solution)/shard_map/ppermute | solution.py:372
  19.8 11.0 %hyena_mix.1.v = bf16[384,2048]{1,0:T(8,128)(2,1)} custom-call(s32[4]{0:T(128)S(1)} %copy-done.8, bf16[384,2048]{1,0:T(8,128)(2,1)S(1)} %copy-done.6, bf16[384,2048]{1,0:T(8,128)(2,1)S(1)} %copy-done.4, bf16[384,2048]{1,0:T(8,128)(2,1)S(1)} %copy-done.5, bf16[128,2048]{1,0:T(8,128)(2,1)S(1)} %collective-permute-done.halo, bf16[128,128]{1,0:T(8,128)(2,1)S(1)} %copy-done.7, ...), custom_call_target="tpu_custom_call" | custom-call | flops 1024 | bytes 1024 | tf_op jit(solution)/shard_map/hyena_mix/pallas_call | solution.py:115
  30.8 1.4 %fusion.2 = (bf16[384,512]{1,0:T(8,128)(2,1)S(1)}, bf16[384,512]{1,0:T(8,128)(2,1)S(1)}, bf16[384,512]{1,0:T(8,128)(2,1)S(1)}) fusion(bf16[384,2048]{1,0:T(8,128)(2,1)} %hyena_mix.1.v), kind=kLoop, calls=%fused_computation.5 | loop fusion | bytes 2359296 | tf_op jit(solution)/shard_map/slice | solution.py:374
  32.2 1.3 %collective-permute-start.4 = (bf16[384,512]{1,0:T(8,128)(2,1)S(1)}, bf16[384,512]{1,0:T(8,128)(2,1)S(1)}, u32[]{:S(2)}, u32[]{:S(2)}) collective-permute-start(bf16[384,512]{1,0:T(8,128)(2,1)S(1)} %get-tuple-element.66), channel_id=1, source_target_pairs={{0,4},{1,5},{2,6},{3,7},{16,20},{17,21},{18,22},{19,23}} | collective-permute-start | bytes 1179656 | tf_op jit(solution)/shard_map/ppermute | solution.py:372
  33.5 1.3 %collective-permute-start.12 = (bf16[384,512]{1,0:T(8,128)(2,1)S(1)}, bf16[384,512]{1,0:T(8,128)(2,1)S(1)}, u32[]{:S(2)}, u32[]{:S(2)}) collective-permute-start(bf16[384,512]{1,0:T(8,128)(2,1)S(1)} %get-tuple-element.64), channel_id=1, source_target_pairs={{0,4},{1,5},{2,6},{3,7},{16,20},{17,21},{18,22},{19,23}} | collective-permute-start | bytes 1179656 | tf_op jit(solution)/shard_map/ppermute | solution.py:372
  34.8 0.1 pad_maximum_fusion
  34.9 14.4 %collective-permute-done.4.rest_3_ = bf16[384,512]{1,0:T(8,128)(2,1)S(1)} collective-permute-done((bf16[384,512]{1,0:T(8,128)(2,1)S(1)}, bf16[384,512]{1,0:T(8,128)(2,1)S(1)}, u32[]{:S(2)}, u32[]{:S(2)}) %collective-permute-start.4) | collective-permute-done | bytes 393248 | tf_op jit(solution)/shard_map/ppermute | solution.py:372
  49.3 1.3 %collective-permute-start.7 = (bf16[384,1024]{1,0:T(8,128)(2,1)S(1)}, bf16[384,1024]{1,0:T(8,128)(2,1)S(1)}, u32[]{:S(2)}, u32[]{:S(2)}) collective-permute-start(bf16[384,1024]{1,0:T(8,128)(2,1)S(1)} %get-tuple-element.35), channel_id=1, source_target_pairs={{8,4},{12,8},{9,5},{13,9},{10,6},{14,10},{11,7},{15,11},{24,20},{2... | collective-permute-start | bytes 2359304 | tf_op jit(solution)/shard_map/ppermute | solution.py:372
  50.5 0.0 collective-permute-done.2.rest_1_
  50.6 1.3 %collective-permute-start.9 = (bf16[768,512]{1,0:T(8,128)(2,1)S(1)}, bf16[768,512]{1,0:T(8,128)(2,1)S(1)}, u32[]{:S(2)}, u32[]{:S(2)}) collective-permute-start(bf16[768,512]{1,0:T(8,128)(2,1)S(1)} %pad_maximum_fusion), channel_id=1, source_target_pairs={{0,4},{1,5},{2,6},{3,7},{16,20},{17,21},{18,22},{19,23}} | collective-permute-start | bytes 2359304 | tf_op jit(solution)/shard_map/ppermute | solution.py:372
  51.9 0.0 copy-start.2
  51.9 0.0 collective-permute-done.1.rest_0_
  51.9 1.4 %collective-permute-start.8 = (bf16[256,1024]{1,0:T(8,128)(2,1)S(1)}, bf16[256,1024]{1,0:T(8,128)(2,1)S(1)}, u32[]{:S(2)}, u32[]{:S(2)}) collective-permute-start(bf16[256,1024]{1,0:T(8,128)(2,1)S(1)} %get-tuple-element.36), channel_id=1, source_target_pairs={{12,4},{13,5},{14,6},{15,7},{28,20},{29,21},{30,22},{31,23}} | collective-permute-start | bytes 1572872 | tf_op jit(solution)/shard_map/ppermute | solution.py:372
  53.3 0.0 collective-permute-done.3.rest_2_
  53.3 8.0 %attend_parts.5 = (bf16[384,512]{1,0:T(8,128)(2,1)S(1)}, f32[32,128]{1,0:T(8,128)S(1)}, bf16[400,512]{1,0:T(8,128)(2,1)S(1)}, bf16[272,512]{1,0:T(8,128)(2,1)S(1)}) custom-call(s32[4]{0:T(128)S(1)} %copy-done.8, bf16[384,2048]{1,0:T(8,128)(2,1)S(1)} %copy-done, bf16[384,2048]{1,0:T(8,128)(2,1)} %k.9, bf16[384,2048]{1,0:T(8,128)(2,1)} %hyena_mix.1.v, ...), custom_call_target="tpu_custom_call" | custom-call | flops 1024 | bytes 1024 | tf_op jit(solution)/shard_map/attend_parts/pallas_call | solution.py:283
  61.3 1.3 %collective-permute-start.6 = (bf16[272,512]{1,0:T(8,128)(2,1)S(1)}, bf16[272,512]{1,0:T(8,128)(2,1)S(1)}, u32[]{:S(2)}, u32[]{:S(2)}) collective-permute-start(bf16[272,512]{1,0:T(8,128)(2,1)S(1)} %get-tuple-element.33), channel_id=1, source_target_pairs={{4,12},{5,13},{6,14},{7,15},{20,28},{21,29},{22,30},{23,31}} | collective-permute-start | bytes 835592 | tf_op jit(solution)/shard_map/ppermute | solution.py:372
  62.7 0.0 collective-permute-done.12.rest_3_
  62.7 1.5 %collective-permute-start.5 = (bf16[400,512]{1,0:T(8,128)(2,1)S(1)}, bf16[400,512]{1,0:T(8,128)(2,1)S(1)}, u32[]{:S(2)}, u32[]{:S(2)}) collective-permute-start(bf16[400,512]{1,0:T(8,128)(2,1)S(1)} %get-tuple-element.32), channel_id=1, source_target_pairs={{4,8},{8,12},{5,9},{9,13},{6,10},{10,14},{7,11},{11,15},{20,24},{2... | collective-permute-start | bytes 1228808 | tf_op jit(solution)/shard_map/ppermute | solution.py:372
  64.2 1.1 fusion.1
  65.3 8.0 %attend_parts.7 = (bf16[384,512]{1,0:T(8,128)(2,1)S(1)}, f32[32,128]{1,0:T(8,128)S(1)}, bf16[400,512]{1,0:T(8,128)(2,1)S(1)}, bf16[272,512]{1,0:T(8,128)(2,1)S(1)}) custom-call(s32[4]{0:T(128)S(1)} %copy-done.8, bf16[384,2048]{1,0:T(8,128)(2,1)S(1)} %copy-done, bf16[384,2048]{1,0:T(8,128)(2,1)} %k.9, bf16[384,2048]{1,0:T(8,128)(2,1)} %hyena_mix.1.v, ...), custom_call_target="tpu_custom_call" | custom-call | flops 1024 | bytes 1024 | tf_op jit(solution)/shard_map/attend_parts/pallas_call | solution.py:283
  73.3 0.0 collective-permute-done.6.rest_1_
  73.3 1.5 %collective-permute-start.17 = (bf16[272,512]{1,0:T(8,128)(2,1)S(1)}, bf16[272,512]{1,0:T(8,128)(2,1)S(1)}, u32[]{:S(2)}, u32[]{:S(2)}) collective-permute-start(bf16[272,512]{1,0:T(8,128)(2,1)S(1)} %get-tuple-element.48), channel_id=1, source_target_pairs={{4,12},{5,13},{6,14},{7,15},{20,28},{21,29},{22,30},{23,31}} | collective-permute-start | bytes 835592 | tf_op jit(solution)/shard_map/ppermute | solution.py:372
  74.8 1.7 %collective-permute-done.5.rest_0_ = bf16[400,512]{1,0:T(8,128)(2,1)S(1)} collective-permute-done((bf16[400,512]{1,0:T(8,128)(2,1)S(1)}, bf16[400,512]{1,0:T(8,128)(2,1)S(1)}, u32[]{:S(2)}, u32[]{:S(2)}) %collective-permute-start.5) | collective-permute-done | bytes 409632 | tf_op jit(solution)/shard_map/ppermute | solution.py:372
  76.5 1.3 %collective-permute-start.18 = (bf16[768,256]{1,0:T(8,128)(2,1)S(1)}, bf16[768,256]{1,0:T(8,128)(2,1)S(1)}, u32[]{:S(2)}, u32[]{:S(2)}) collective-permute-start(bf16[768,256]{1,0:T(8,128)(2,1)S(1)} %pad_maximum_fusion.2), channel_id=1, source_target_pairs={{0,4},{1,5},{2,6},{3,7},{16,20},{17,21},{18,22},{19,23}} | collective-permute-start | bytes 1179656 | tf_op jit(solution)/shard_map/ppermute | solution.py:372
  77.8 0.0 collective-permute-done.8.rest_1_
  77.8 3.8 %collective-permute-start.16 = (bf16[400,512]{1,0:T(8,128)(2,1)S(1)}, bf16[400,512]{1,0:T(8,128)(2,1)S(1)}, u32[]{:S(2)}, u32[]{:S(2)}) collective-permute-start(bf16[400,512]{1,0:T(8,128)(2,1)S(1)} %get-tuple-element.47), channel_id=1, source_target_pairs={{4,8},{8,12},{5,9},{9,13},{6,10},{10,14},{7,11},{11,15},{20,24},{2... | collective-permute-start | bytes 1228808 | tf_op jit(solution)/shard_map/ppermute | solution.py:372
  81.6 0.0 collective-permute-done.7.rest_0_
  81.6 0.0 collective-permute-done.9.rest_2_.rest_3_
  81.7 0.0 copy-start.3
  81.7 8.1 %attend_parts.6 = (bf16[384,512]{1,0:T(8,128)(2,1)S(1)}, f32[32,128]{1,0:T(8,128)S(1)}, bf16[400,512]{1,0:T(8,128)(2,1)S(1)}, bf16[272,512]{1,0:T(8,128)(2,1)S(1)}) custom-call(s32[4]{0:T(128)S(1)} %copy-done.8, bf16[384,2048]{1,0:T(8,128)(2,1)S(1)} %copy-done, bf16[384,2048]{1,0:T(8,128)(2,1)} %k.9, bf16[384,2048]{1,0:T(8,128)(2,1)} %hyena_mix.1.v, ...), custom_call_target="tpu_custom_call" | custom-call | flops 1024 | bytes 1024 | tf_op jit(solution)/shard_map/attend_parts/pallas_call | solution.py:283
  89.8 1.3 %collective-permute-start.10 = (bf16[400,512]{1,0:T(8,128)(2,1)S(1)}, bf16[400,512]{1,0:T(8,128)(2,1)S(1)}, u32[]{:S(2)}, u32[]{:S(2)}) collective-permute-start(bf16[400,512]{1,0:T(8,128)(2,1)S(1)} %get-tuple-element.38), channel_id=1, source_target_pairs={{4,8},{8,12},{5,9},{9,13},{6,10},{10,14},{7,11},{11,15},{20,24},{2... | collective-permute-start | bytes 1228808 | tf_op jit(solution)/shard_map/ppermute | solution.py:372
  91.2 1.3 %collective-permute-start.13 = (bf16[768,256]{1,0:T(8,128)(2,1)S(1)}, bf16[768,256]{1,0:T(8,128)(2,1)S(1)}, u32[]{:S(2)}, u32[]{:S(2)}) collective-permute-start(bf16[768,256]{1,0:T(8,128)(2,1)S(1)} %pad_maximum_fusion.1), channel_id=1, source_target_pairs={{0,4},{1,5},{2,6},{3,7},{16,20},{17,21},{18,22},{19,23}} | collective-permute-start | bytes 1179656 | tf_op jit(solution)/shard_map/ppermute | solution.py:372
  92.5 1.3 %collective-permute-start.11 = (bf16[272,512]{1,0:T(8,128)(2,1)S(1)}, bf16[272,512]{1,0:T(8,128)(2,1)S(1)}, u32[]{:S(2)}, u32[]{:S(2)}) collective-permute-start(bf16[272,512]{1,0:T(8,128)(2,1)S(1)} %get-tuple-element.39), channel_id=1, source_target_pairs={{4,12},{5,13},{6,14},{7,15},{20,28},{21,29},{22,30},{23,31}} | collective-permute-start | bytes 835592 | tf_op jit(solution)/shard_map/ppermute | solution.py:372
  93.8 0.0 collective-permute-done.18.rest_2_.rest_3_
  93.8 4.6 %attend_parts.9 = (bf16[384,256]{1,0:T(8,128)(2,1)S(1)}, f32[16,128]{1,0:T(8,128)S(1)}, bf16[400,256]{1,0:T(8,128)(2,1)S(1)}, bf16[272,256]{1,0:T(8,128)(2,1)S(1)}) custom-call(s32[4]{0:T(128)S(1)} %copy-done.8, bf16[384,2048]{1,0:T(8,128)(2,1)S(1)} %copy-done, bf16[384,2048]{1,0:T(8,128)(2,1)S(1)} %copy-done.3, bf16[384,2048]{1,0:T(8,128)(2,1)} %hyena_mix.1.v, ...), custom_call_target="tpu_custom_call" | custom-call | flops 1024 | bytes 1024 | tf_op jit(solution)/shard_map/attend_parts/pallas_call | solution.py:283
  98.4 1.3 %collective-permute-start.19 = (bf16[400,256]{1,0:T(8,128)(2,1)S(1)}, bf16[400,256]{1,0:T(8,128)(2,1)S(1)}, u32[]{:S(2)}, u32[]{:S(2)}) collective-permute-start(bf16[400,256]{1,0:T(8,128)(2,1)S(1)} %get-tuple-element.54), channel_id=1, source_target_pairs={{4,8},{8,12},{5,9},{9,13},{6,10},{10,14},{7,11},{11,15},{20,24},{2... | collective-permute-start | bytes 614408 | tf_op jit(solution)/shard_map/ppermute | solution.py:372
  99.8 5.8 %collective-permute-done.11.rest_1_ = bf16[272,512]{1,0:T(8,128)(2,1)S(1)} collective-permute-done((bf16[272,512]{1,0:T(8,128)(2,1)S(1)}, bf16[272,512]{1,0:T(8,128)(2,1)S(1)}, u32[]{:S(2)}, u32[]{:S(2)}) %collective-permute-start.11) | collective-permute-done | bytes 278560 | tf_op jit(solution)/shard_map/ppermute | solution.py:372
  105.5 0.0 collective-permute-done.10.rest_0_
  105.5 0.0 collective-permute-done.13.rest_2_.rest_3_
  105.5 4.4 %attend_parts.8 = (bf16[384,256]{1,0:T(8,128)(2,1)S(1)}, f32[16,128]{1,0:T(8,128)S(1)}, bf16[400,256]{1,0:T(8,128)(2,1)S(1)}, bf16[272,256]{1,0:T(8,128)(2,1)S(1)}) custom-call(s32[4]{0:T(128)S(1)} %copy-done.8, bf16[384,2048]{1,0:T(8,128)(2,1)S(1)} %copy-done, bf16[384,2048]{1,0:T(8,128)(2,1)S(1)} %copy-done.3, bf16[384,2048]{1,0:T(8,128)(2,1)} %hyena_mix.1.v, ...), custom_call_target="tpu_custom_call" | custom-call | flops 1024 | bytes 1024 | tf_op jit(solution)/shard_map/attend_parts/pallas_call | solution.py:283
  109.9 1.3 %collective-permute-start.14 = (bf16[400,256]{1,0:T(8,128)(2,1)S(1)}, bf16[400,256]{1,0:T(8,128)(2,1)S(1)}, u32[]{:S(2)}, u32[]{:S(2)}) collective-permute-start(bf16[400,256]{1,0:T(8,128)(2,1)S(1)} %get-tuple-element.45), channel_id=1, source_target_pairs={{4,8},{8,12},{5,9},{9,13},{6,10},{10,14},{7,11},{11,15},{20,24},{2... | collective-permute-start | bytes 614408 | tf_op jit(solution)/shard_map/ppermute | solution.py:372
  111.2 2.8 %collective-permute-start.20 = (bf16[272,256]{1,0:T(8,128)(2,1)S(1)}, bf16[272,256]{1,0:T(8,128)(2,1)S(1)}, u32[]{:S(2)}, u32[]{:S(2)}) collective-permute-start(bf16[272,256]{1,0:T(8,128)(2,1)S(1)} %get-tuple-element.55), channel_id=1, source_target_pairs={{4,12},{5,13},{6,14},{7,15},{20,28},{21,29},{22,30},{23,31}} | collective-permute-start | bytes 417800 | tf_op jit(solution)/shard_map/ppermute | solution.py:372
  114.1 1.3 %collective-permute-start.15 = (bf16[272,256]{1,0:T(8,128)(2,1)S(1)}, bf16[272,256]{1,0:T(8,128)(2,1)S(1)}, u32[]{:S(2)}, u32[]{:S(2)}) collective-permute-start(bf16[272,256]{1,0:T(8,128)(2,1)S(1)} %get-tuple-element.46), channel_id=1, source_target_pairs={{4,12},{5,13},{6,14},{7,15},{20,28},{21,29},{22,30},{23,31}} | collective-permute-start | bytes 417800 | tf_op jit(solution)/shard_map/ppermute | solution.py:372
  115.4 1.9 %join_parts.5.rest_2_ = bf16[384,2048]{1,0:T(8,128)(2,1)} custom-call(bf16[384,512]{1,0:T(8,128)(2,1)S(1)} %get-tuple-element.59.o, f32[32,128]{1,0:T(8,128)S(1)} %get-tuple-element.50.s, bf16[400,512]{1,0:T(8,128)(2,1)S(1)} %collective-permute-done.5.rest_0_, bf16[272,512]{1,0:T(8,128)(2,1)S(1)} %collective-permute-done.6.rest_1_), custom_call_target="tpu_custom_call" | custom-call | flops 1024 | bytes 1024 | tf_op jit(solution)/shard_map/join_parts/pallas_call | solution.py:341
  117.3 1.9 %join_parts.6.rest_2_ = bf16[384,2048]{1,0:T(8,128)(2,1)} custom-call(bf16[384,512]{1,0:T(8,128)(2,1)S(1)} %get-tuple-element.58.o, f32[32,128]{1,0:T(8,128)S(1)} %get-tuple-element.41.s, bf16[400,512]{1,0:T(8,128)(2,1)S(1)} %collective-permute-done.16.rest_0_, bf16[272,512]{1,0:T(8,128)(2,1)S(1)} %collective-permute-done.17.rest_1_, ...), custom_call_target="tpu_custom_call", output_to_operand_aliasing={{}: (4, {})} | custom-call | flops 1024 | bytes 1024 | tf_op jit(solution)/shard_map/join_parts/pallas_call | solution.py:341
  119.2 1.9 %join_parts.7.rest_2_ = bf16[384,2048]{1,0:T(8,128)(2,1)} custom-call(bf16[384,512]{1,0:T(8,128)(2,1)S(1)} %get-tuple-element.56.o, f32[32,128]{1,0:T(8,128)S(1)} %get-tuple-element.57.s, bf16[400,512]{1,0:T(8,128)(2,1)S(1)} %collective-permute-done.10.rest_0_, bf16[272,512]{1,0:T(8,128)(2,1)S(1)} %collective-permute-done.11.rest_1_, ...), custom_call_target="tpu_custom_call", output_to_operand_aliasing={{}: (4, {})} | custom-call | flops 1024 | bytes 1024 | tf_op jit(solution)/shard_map/join_parts/pallas_call | solution.py:341
  121.2 1.2 %join_parts.8.rest_2_ = bf16[384,2048]{1,0:T(8,128)(2,1)} custom-call(bf16[384,256]{1,0:T(8,128)(2,1)S(1)} %get-tuple-element.52.o, f32[16,128]{1,0:T(8,128)S(1)} %get-tuple-element.53.s, bf16[400,256]{1,0:T(8,128)(2,1)S(1)} %collective-permute-done.19.rest_0_, bf16[272,256]{1,0:T(8,128)(2,1)S(1)} %collective-permute-done.20.rest_1_, ...), custom_call_target="tpu_custom_call", output_to_operand_aliasing={{}: (4, {})} | custom-call | flops 1024 | bytes 1024 | tf_op jit(solution)/shard_map/join_parts/pallas_call | solution.py:341
  122.4 0.0 collective-permute-done.15.rest_1_
  122.4 1.2 %join_parts.9 = bf16[384,2048]{1,0:T(8,128)(2,1)} custom-call(bf16[384,256]{1,0:T(8,128)(2,1)S(1)} %get-tuple-element.43.o, f32[16,128]{1,0:T(8,128)S(1)} %get-tuple-element.44.s, bf16[400,256]{1,0:T(8,128)(2,1)S(1)} %collective-permute-done.14.rest_0_, bf16[272,256]{1,0:T(8,128)(2,1)S(1)} %collective-permute-done.15.rest_1_, ...), custom_call_target="tpu_custom_call", output_to_operand_aliasing={{}: (4, {})} | custom-call | flops 1024 | bytes 1024 | tf_op jit(solution)/shard_map/join_parts/pallas_call | solution.py:341
  (21 shorter events, 0.1 us)
Async XLA Ops:
  0.6 5.6 %copy-start = (bf16[384,2048]{1,0:T(8,128)(2,1)S(1)}, bf16[384,2048]{1,0:T(8,128)(2,1)}, u32[]{:S(2)}) copy-start(bf16[384,2048]{1,0:T(8,128)(2,1)} %q.9) | copy-start | bytes 4718596
  2.7 15.8 %collective-permute-start = (bf16[128,2048]{1,0:T(8,128)(2,1)}, bf16[128,2048]{1,0:T(8,128)(2,1)S(1)}, u32[]{:S(2)}, u32[]{:S(2)}) collective-permute-start(bf16[128,2048]{1,0:T(8,128)(2,1)} %halo_product.1), channel_id=1, source_target_pairs={{0,4},{4,8},{8,12},{1,5},{5,9},{9,13},{2,6},{6,10},{10,14},{3,7},{... | collective-permute-start | bytes 1572872 | tf_op jit(solution)/shard_map/ppermute | solution.py:372
  6.2 13.6 %copy-start.6 = (bf16[384,2048]{1,0:T(8,128)(2,1)S(1)}, bf16[384,2048]{1,0:T(8,128)(2,1)}, u32[]{:S(2)}) copy-start(bf16[384,2048]{1,0:T(8,128)(2,1)} %hq.1) | copy-start | bytes 4718596
  6.2 13.6 %copy-start.7 = (bf16[128,128]{1,0:T(8,128)(2,1)S(1)}, bf16[128,128]{1,0:T(8,128)(2,1)}, u32[]{:S(2)}) copy-start(bf16[128,128]{1,0:T(8,128)(2,1)} %filters.1) | copy-start | bytes 98308
  6.2 13.6 %copy-start.9 = (f32[2048]{0:T(1024)S(1)}, f32[2048]{0:T(1024)}, u32[]{:S(2)}) copy-start(f32[2048]{0:T(1024)} %param.12) | copy-start | bytes 24580
  6.3 3.3 %copy-start.1 = (bf16[384,2048]{1,0:T(8,128)(2,1)S(1)}, bf16[384,2048]{1,0:T(8,128)(2,1)}, u32[]{:S(2)}) copy-start(bf16[384,2048]{1,0:T(8,128)(2,1)} %k.9) | copy-start | bytes 4718596
  6.3 44.2 %collective-permute-start.2 = (bf16[256,1024]{1,0:T(8,128)(2,1)S(1)}, bf16[256,1024]{1,0:T(8,128)(2,1)S(1)}, u32[]{:S(2)}, u32[]{:S(2)}) collective-permute-start(bf16[256,1024]{1,0:T(8,128)(2,1)S(1)} %get-tuple-element.68), channel_id=1, source_target_pairs={{12,4},{13,5},{14,6},{15,7},{28,20},{29,21},{30,22},{31,23}} | collective-permute-start | bytes 1572872 | tf_op jit(solution)/shard_map/ppermute | solution.py:372
  7.9 11.9 %copy-start.5 = (bf16[384,2048]{1,0:T(8,128)(2,1)S(1)}, bf16[384,2048]{1,0:T(8,128)(2,1)}, u32[]{:S(2)}) copy-start(bf16[384,2048]{1,0:T(8,128)(2,1)} %hv.3) | copy-start | bytes 4718596
  8.1 11.7 %copy-start.4 = (bf16[384,2048]{1,0:T(8,128)(2,1)S(1)}, bf16[384,2048]{1,0:T(8,128)(2,1)}, u32[]{:S(2)}) copy-start(bf16[384,2048]{1,0:T(8,128)(2,1)} %hk.3) | copy-start | bytes 4718596
  8.1 11.7 %copy-start.8 = (s32[4]{0:T(128)S(1)}, s32[4]{0:T(128)}, u32[]{:S(2)}) copy-start(s32[4]{0:T(128)} %info.8) | copy-start | bytes 52
  8.1 43.8 %collective-permute-start.1 = (bf16[384,1024]{1,0:T(8,128)(2,1)S(1)}, bf16[384,1024]{1,0:T(8,128)(2,1)S(1)}, u32[]{:S(2)}, u32[]{:S(2)}) collective-permute-start(bf16[384,1024]{1,0:T(8,128)(2,1)S(1)} %get-tuple-element.70), channel_id=1, source_target_pairs={{8,4},{12,8},{9,5},{13,9},{10,6},{14,10},{11,7},{15,11},{24,20},{2... | collective-permute-start | bytes 2359304 | tf_op jit(solution)/shard_map/ppermute | solution.py:372
  18.5 34.8 %collective-permute-start.3 = (bf16[384,1024]{1,0:T(8,128)(2,1)S(1)}, bf16[384,1024]{1,0:T(8,128)(2,1)S(1)}, u32[]{:S(2)}, u32[]{:S(2)}) collective-permute-start(bf16[384,1024]{1,0:T(8,128)(2,1)S(1)} %slice.45), channel_id=1, source_target_pairs={{0,4},{1,5},{2,6},{3,7},{16,20},{17,21},{18,22},{19,23}} | collective-permute-start | bytes 2359304 | tf_op jit(solution)/shard_map/ppermute | solution.py:372
  30.8 4.0 %slice-start = ((bf16[384,2048]{1,0:T(8,128)(2,1)}), bf16[384,512]{1,0:T(8,128)(2,1)S(1)}, s32[]{:S(2)}) async-start(bf16[384,2048]{1,0:T(8,128)(2,1)} %k.9), calls=%async_computation | async-start | bytes 786432 | tf_op jit(solution)/shard_map/slice | solution.py:374
  32.2 17.1 %collective-permute-start.4 = (bf16[384,512]{1,0:T(8,128)(2,1)S(1)}, bf16[384,512]{1,0:T(8,128)(2,1)S(1)}, u32[]{:S(2)}, u32[]{:S(2)}) collective-permute-start(bf16[384,512]{1,0:T(8,128)(2,1)S(1)} %get-tuple-element.66), channel_id=1, source_target_pairs={{0,4},{1,5},{2,6},{3,7},{16,20},{17,21},{18,22},{19,23}} | collective-permute-start | bytes 1179656 | tf_op jit(solution)/shard_map/ppermute | solution.py:372
  33.5 29.2 %collective-permute-start.12 = (bf16[384,512]{1,0:T(8,128)(2,1)S(1)}, bf16[384,512]{1,0:T(8,128)(2,1)S(1)}, u32[]{:S(2)}, u32[]{:S(2)}) collective-permute-start(bf16[384,512]{1,0:T(8,128)(2,1)S(1)} %get-tuple-element.64), channel_id=1, source_target_pairs={{0,4},{1,5},{2,6},{3,7},{16,20},{17,21},{18,22},{19,23}} | collective-permute-start | bytes 1179656 | tf_op jit(solution)/shard_map/ppermute | solution.py:372
  49.3 32.4 %collective-permute-start.7 = (bf16[384,1024]{1,0:T(8,128)(2,1)S(1)}, bf16[384,1024]{1,0:T(8,128)(2,1)S(1)}, u32[]{:S(2)}, u32[]{:S(2)}) collective-permute-start(bf16[384,1024]{1,0:T(8,128)(2,1)S(1)} %get-tuple-element.35), channel_id=1, source_target_pairs={{8,4},{12,8},{9,5},{13,9},{10,6},{14,10},{11,7},{15,11},{24,20},{2... | collective-permute-start | bytes 2359304 | tf_op jit(solution)/shard_map/ppermute | solution.py:372
  50.6 31.1 %collective-permute-start.9 = (bf16[768,512]{1,0:T(8,128)(2,1)S(1)}, bf16[768,512]{1,0:T(8,128)(2,1)S(1)}, u32[]{:S(2)}, u32[]{:S(2)}) collective-permute-start(bf16[768,512]{1,0:T(8,128)(2,1)S(1)} %pad_maximum_fusion), channel_id=1, source_target_pairs={{0,4},{1,5},{2,6},{3,7},{16,20},{17,21},{18,22},{19,23}} | collective-permute-start | bytes 2359304 | tf_op jit(solution)/shard_map/ppermute | solution.py:372
  51.9 12.3 %copy-start.2 = (bf16[384,2048]{1,0:T(8,128)(2,1)S(1)}, bf16[384,2048]{1,0:T(8,128)(2,1)}, u32[]{:S(2)}) copy-start(bf16[384,2048]{1,0:T(8,128)(2,1)} %k.9) | copy-start | bytes 4718596
  51.9 25.9 %collective-permute-start.8 = (bf16[256,1024]{1,0:T(8,128)(2,1)S(1)}, bf16[256,1024]{1,0:T(8,128)(2,1)S(1)}, u32[]{:S(2)}, u32[]{:S(2)}) collective-permute-start(bf16[256,1024]{1,0:T(8,128)(2,1)S(1)} %get-tuple-element.36), channel_id=1, source_target_pairs={{12,4},{13,5},{14,6},{15,7},{28,20},{29,21},{30,22},{31,23}} | collective-permute-start | bytes 1572872 | tf_op jit(solution)/shard_map/ppermute | solution.py:372
  61.3 12.0 %collective-permute-start.6 = (bf16[272,512]{1,0:T(8,128)(2,1)S(1)}, bf16[272,512]{1,0:T(8,128)(2,1)S(1)}, u32[]{:S(2)}, u32[]{:S(2)}) collective-permute-start(bf16[272,512]{1,0:T(8,128)(2,1)S(1)} %get-tuple-element.33), channel_id=1, source_target_pairs={{4,12},{5,13},{6,14},{7,15},{20,28},{21,29},{22,30},{23,31}} | collective-permute-start | bytes 835592 | tf_op jit(solution)/shard_map/ppermute | solution.py:372
  62.7 13.9 %collective-permute-start.5 = (bf16[400,512]{1,0:T(8,128)(2,1)S(1)}, bf16[400,512]{1,0:T(8,128)(2,1)S(1)}, u32[]{:S(2)}, u32[]{:S(2)}) collective-permute-start(bf16[400,512]{1,0:T(8,128)(2,1)S(1)} %get-tuple-element.32), channel_id=1, source_target_pairs={{4,8},{8,12},{5,9},{9,13},{6,10},{10,14},{7,11},{11,15},{20,24},{2... | collective-permute-start | bytes 1228808 | tf_op jit(solution)/shard_map/ppermute | solution.py:372
  73.3 19.1 %collective-permute-start.17 = (bf16[272,512]{1,0:T(8,128)(2,1)S(1)}, bf16[272,512]{1,0:T(8,128)(2,1)S(1)}, u32[]{:S(2)}, u32[]{:S(2)}) collective-permute-start(bf16[272,512]{1,0:T(8,128)(2,1)S(1)} %get-tuple-element.48), channel_id=1, source_target_pairs={{4,12},{5,13},{6,14},{7,15},{20,28},{21,29},{22,30},{23,31}} | collective-permute-start | bytes 835592 | tf_op jit(solution)/shard_map/ppermute | solution.py:372
  76.5 17.3 %collective-permute-start.18 = (bf16[768,256]{1,0:T(8,128)(2,1)S(1)}, bf16[768,256]{1,0:T(8,128)(2,1)S(1)}, u32[]{:S(2)}, u32[]{:S(2)}) collective-permute-start(bf16[768,256]{1,0:T(8,128)(2,1)S(1)} %pad_maximum_fusion.2), channel_id=1, source_target_pairs={{0,4},{1,5},{2,6},{3,7},{16,20},{17,21},{18,22},{19,23}} | collective-permute-start | bytes 1179656 | tf_op jit(solution)/shard_map/ppermute | solution.py:372
  77.8 16.0 %collective-permute-start.16 = (bf16[400,512]{1,0:T(8,128)(2,1)S(1)}, bf16[400,512]{1,0:T(8,128)(2,1)S(1)}, u32[]{:S(2)}, u32[]{:S(2)}) collective-permute-start(bf16[400,512]{1,0:T(8,128)(2,1)S(1)} %get-tuple-element.47), channel_id=1, source_target_pairs={{4,8},{8,12},{5,9},{9,13},{6,10},{10,14},{7,11},{11,15},{20,24},{2... | collective-permute-start | bytes 1228808 | tf_op jit(solution)/shard_map/ppermute | solution.py:372
  81.7 12.2 %copy-start.3 = (bf16[384,2048]{1,0:T(8,128)(2,1)S(1)}, bf16[384,2048]{1,0:T(8,128)(2,1)}, u32[]{:S(2)}) copy-start(bf16[384,2048]{1,0:T(8,128)(2,1)} %k.9) | copy-start | bytes 4718596
  89.8 15.7 %collective-permute-start.10 = (bf16[400,512]{1,0:T(8,128)(2,1)S(1)}, bf16[400,512]{1,0:T(8,128)(2,1)S(1)}, u32[]{:S(2)}, u32[]{:S(2)}) collective-permute-start(bf16[400,512]{1,0:T(8,128)(2,1)S(1)} %get-tuple-element.38), channel_id=1, source_target_pairs={{4,8},{8,12},{5,9},{9,13},{6,10},{10,14},{7,11},{11,15},{20,24},{2... | collective-permute-start | bytes 1228808 | tf_op jit(solution)/shard_map/ppermute | solution.py:372
  91.2 14.4 %collective-permute-start.13 = (bf16[768,256]{1,0:T(8,128)(2,1)S(1)}, bf16[768,256]{1,0:T(8,128)(2,1)S(1)}, u32[]{:S(2)}, u32[]{:S(2)}) collective-permute-start(bf16[768,256]{1,0:T(8,128)(2,1)S(1)} %pad_maximum_fusion.1), channel_id=1, source_target_pairs={{0,4},{1,5},{2,6},{3,7},{16,20},{17,21},{18,22},{19,23}} | collective-permute-start | bytes 1179656 | tf_op jit(solution)/shard_map/ppermute | solution.py:372
  92.5 13.0 %collective-permute-start.11 = (bf16[272,512]{1,0:T(8,128)(2,1)S(1)}, bf16[272,512]{1,0:T(8,128)(2,1)S(1)}, u32[]{:S(2)}, u32[]{:S(2)}) collective-permute-start(bf16[272,512]{1,0:T(8,128)(2,1)S(1)} %get-tuple-element.39), channel_id=1, source_target_pairs={{4,12},{5,13},{6,14},{7,15},{20,28},{21,29},{22,30},{23,31}} | collective-permute-start | bytes 835592 | tf_op jit(solution)/shard_map/ppermute | solution.py:372
  98.4 22.7 %collective-permute-start.19 = (bf16[400,256]{1,0:T(8,128)(2,1)S(1)}, bf16[400,256]{1,0:T(8,128)(2,1)S(1)}, u32[]{:S(2)}, u32[]{:S(2)}) collective-permute-start(bf16[400,256]{1,0:T(8,128)(2,1)S(1)} %get-tuple-element.54), channel_id=1, source_target_pairs={{4,8},{8,12},{5,9},{9,13},{6,10},{10,14},{7,11},{11,15},{20,24},{2... | collective-permute-start | bytes 614408 | tf_op jit(solution)/shard_map/ppermute | solution.py:372
  109.9 12.5 %collective-permute-start.14 = (bf16[400,256]{1,0:T(8,128)(2,1)S(1)}, bf16[400,256]{1,0:T(8,128)(2,1)S(1)}, u32[]{:S(2)}, u32[]{:S(2)}) collective-permute-start(bf16[400,256]{1,0:T(8,128)(2,1)S(1)} %get-tuple-element.45), channel_id=1, source_target_pairs={{4,8},{8,12},{5,9},{9,13},{6,10},{10,14},{7,11},{11,15},{20,24},{2... | collective-permute-start | bytes 614408 | tf_op jit(solution)/shard_map/ppermute | solution.py:372
  111.2 9.9 %collective-permute-start.20 = (bf16[272,256]{1,0:T(8,128)(2,1)S(1)}, bf16[272,256]{1,0:T(8,128)(2,1)S(1)}, u32[]{:S(2)}, u32[]{:S(2)}) collective-permute-start(bf16[272,256]{1,0:T(8,128)(2,1)S(1)} %get-tuple-element.55), channel_id=1, source_target_pairs={{4,12},{5,13},{6,14},{7,15},{20,28},{21,29},{22,30},{23,31}} | collective-permute-start | bytes 417800 | tf_op jit(solution)/shard_map/ppermute | solution.py:372
  114.1 8.3 %collective-permute-start.15 = (bf16[272,256]{1,0:T(8,128)(2,1)S(1)}, bf16[272,256]{1,0:T(8,128)(2,1)S(1)}, u32[]{:S(2)}, u32[]{:S(2)}) collective-permute-start(bf16[272,256]{1,0:T(8,128)(2,1)S(1)} %get-tuple-element.46), channel_id=1, source_target_pairs={{4,12},{5,13},{6,14},{7,15},{20,28},{21,29},{22,30},{23,31}} | collective-permute-start | bytes 417800 | tf_op jit(solution)/shard_map/ppermute | solution.py:372

commit v4 on v3

--- a/solution.py
+++ b/solution.py
@@ -295,8 +295,9 @@
 def join_kernel(plan, o, s, *rest):
     rest = list(rest)
     me = lax.axis_index("ctx")
-    out = rest[-1]
+    out, done = rest[-2:]
     rows = o.shape[0]
+    done[...] = s[:8, :]
     block = lax.broadcasted_iota(jnp.int32, (8, BLOCK), 0)
     parts = [(o, rows, None)]
     for count, flags in ((plan.na, plan.a_from), (plan.nb, plan.b_from)):
@@ -342,8 +343,14 @@
         partial(join_kernel, plan),
         grid=(wide // width,),
         in_specs=in_specs,
-        out_specs=pl.BlockSpec((rows, width), lambda h: (0, h + skip)),
-        out_shape=jax.ShapeDtypeStruct((rows, channels), jnp.bfloat16),
+        out_specs=[
+            pl.BlockSpec((rows, width), lambda h: (0, h + skip)),
+            pl.BlockSpec((8, BLOCK), lambda h: (0, 0)),
+        ],
+        out_shape=[
+            jax.ShapeDtypeStruct((rows, channels), jnp.bfloat16),
+            jax.ShapeDtypeStruct((8, BLOCK), jnp.float32),
+        ],
         input_output_aliases=aliases,
         compiler_params=compiler_params(),
         cost_estimate=SMALL,
@@ -381,29 +388,30 @@
     qa = send(columns(q, 0, early), plan.a)
     qb = send(columns(q[: plan.nb], 0, early), plan.b)
     later_a = send(after(columns(q, early, total), halo), plan.a)
-    later_b = send(after(columns(q[: plan.nb], early, total), halo), plan.b)
-
-    told, came_back, out, go = [], [], None, None
+
+    told, joined, came_back, out, go = [], [], [], None, None
     first = q_at = 0
     for c, many in enumerate(heads):
         end = first + many
         if first == early:
-            q_at, qa, qb = first, later_a, later_b
+            q_at, qa = first, later_a
+            qb = send(after(columns(q[: plan.nb], early, total), told[0]), plan.b)
         if end <= early:
             keys = (rk, first)
             values = (send(columns(mix, first, end), plan.k), 0, 0)
             go = values[0] if go is None else go
         else:
             pair = jnp.concatenate([columns(k, first, end), columns(mix, first, end)])
-            pair = send(after(pair, told[c - 3] if c >= 3 else go), plan.k)
+            pair = send(after(pair, told[max(0, c - 3)]), plan.k)
             keys, values = (pair, 0), (pair, 0, 1)
-        ready = after(starts, *came_back[c - 2]) if c >= 2 else starts
+        ready = after(starts, *(came_back[c - 2] if c >= 2 else ()), *joined[: max(0, c - 2)])
         o, s, *parts = attend(
             plan, ready, q, k, mix, (qa, first - q_at), (qb, first - q_at), keys, values, first, many
         )
         told.append(s)
         came_back.append([send(x, back(p)) for x, p in zip(parts, (plan.a, plan.b))])
-        out = join(plan, o, s, came_back[-1], first, channels, out)
+        out, done = join(plan, o, s, came_back[-1], first, channels, out)
+        joined.append(done)
         first = end
     return mix, out
 

time: 124 us -> 119 us (0.960)
  the two profiles are of different devices: /device:TPU:8 before, /device:TPU:26 now
where the time goes in v4:
time: 119 us; the launch traced here: 117 us
  starting transfers between devices  45.1 us (38%)
  Pallas kernels  34.5 us (29%)
  waiting for transfers between devices  33.5 us (28%)
  local copies, waits for them, and re-layouts  2.79 us (2%)
    ppermute x21, starting transfers between devices, run_plan(): send = lambda x, pairs: lax.ppermute(x, 'ctx', pairs)  45.1 us
    ppermute x21, waiting for transfers between devices, run_plan(): send = lambda x, pairs: lax.ppermute(x, 'ctx', pairs)  33.5 us
    pallas_call x5, Pallas kernels, attend(): pl.pallas_call(partial(attend_kernel, starts.shape[0], plan), grid=(heads...  13.1 us
    pallas_call x1, Pallas kernels, hyena(): pl.pallas_call(partial(hyena_kernel, starts.shape[0], group), grid=(chann...  11 us
    pallas_call x5, Pallas kernels, join(): pl.pallas_call(partial(join_kernel, plan), grid=(wide // width,), in_spec...  8.28 us
    slice x8, local copies, waits for them, and re-layouts, run_plan(): columns = lambda x, first, end: x[:, first * HEAD_DIM:end * HEAD_DIM]  2.73 us
  transfers between devices with their start and end apart: 21, of which 9 were waited for; matrix products, arithmetic and copies ran while one was open for 2% of the time, Pallas kernels for 27%

profile of v4, /device:TPU:26, one launch (start us, length us, event | category | flops | bytes accessed | tf_op | source)
XLA Modules:
  0.0 117.1 jit_solution(1028112806654697493)
XLA Ops:
  0.6 2.1 %halo_product.1 = bf16[128,2048]{1,0:T(8,128)(2,1)} custom-call(bf16[384,2048]{1,0:T(8,128)(2,1)} %hk.3, bf16[384,2048]{1,0:T(8,128)(2,1)} %hv.3), custom_call_target="tpu_custom_call" | custom-call | flops 1024 | bytes 1024 | tf_op jit(solution)/shard_map/halo_product/pallas_call | solution.py:44
  2.7 1.4 %collective-permute-start = (bf16[128,2048]{1,0:T(8,128)(2,1)}, bf16[128,2048]{1,0:T(8,128)(2,1)S(1)}, u32[]{:S(2)}, u32[]{:S(2)}) collective-permute-start(bf16[128,2048]{1,0:T(8,128)(2,1)} %halo_product.1), channel_id=1, source_target_pairs={{0,4},{4,8},{8,12},{1,5},{5,9},{9,13},{2,6},{6,10},{10,14},{3,7},{... | collective-permute-start | bytes 1572872 | tf_op jit(solution)/shard_map/ppermute | solution.py:379
  4.2 0.0 copy-start.6
  4.2 0.1 fusion.4
  4.3 0.0 copy-start.4
  4.3 0.0 copy-start.5
  4.3 0.0 copy-start.7
  4.3 0.0 copy-start.8
  4.4 0.0 copy-start.9
  4.4 4.9 %collective-permute-start.1 = (bf16[384,1024]{1,0:T(8,128)(2,1)S(1)}, bf16[384,1024]{1,0:T(8,128)(2,1)S(1)}, u32[]{:S(2)}, u32[]{:S(2)}) collective-permute-start(bf16[384,1024]{1,0:T(8,128)(2,1)S(1)} %get-tuple-element.82), channel_id=1, source_target_pairs={{8,4},{12,8},{9,5},{13,9},{10,6},{14,10},{11,7},{15,11},{24,20},{2... | collective-permute-start | bytes 2359304 | tf_op jit(solution)/shard_map/ppermute | solution.py:379
  9.2 0.1 slice.45
  9.3 9.3 %collective-permute-done.halo = bf16[128,2048]{1,0:T(8,128)(2,1)S(1)} collective-permute-done((bf16[128,2048]{1,0:T(8,128)(2,1)}, bf16[128,2048]{1,0:T(8,128)(2,1)S(1)}, u32[]{:S(2)}, u32[]{:S(2)}) %collective-permute-start) | collective-permute-done | bytes 524320 | tf_op jit(solution)/shard_map/ppermute | solution.py:379
  18.6 0.7 collective-permute-start.3
  19.3 0.1 fusion.3
  19.4 2.9 %collective-permute-start.2 = (bf16[256,1024]{1,0:T(8,128)(2,1)S(1)}, bf16[256,1024]{1,0:T(8,128)(2,1)S(1)}, u32[]{:S(2)}, u32[]{:S(2)}) collective-permute-start(bf16[256,1024]{1,0:T(8,128)(2,1)S(1)} %get-tuple-element.80), channel_id=1, source_target_pairs={{12,4},{13,5},{14,6},{15,7},{28,20},{29,21},{30,22},{31,23}} | collective-permute-start | bytes 1572872 | tf_op jit(solution)/shard_map/ppermute | solution.py:379
  22.3 11.0 %hyena_mix.1.v = bf16[384,2048]{1,0:T(8,128)(2,1)} custom-call(s32[4]{0:T(128)S(1)} %copy-done.8, bf16[384,2048]{1,0:T(8,128)(2,1)S(1)} %copy-done.6, bf16[384,2048]{1,0:T(8,128)(2,1)S(1)} %copy-done.4, bf16[384,2048]{1,0:T(8,128)(2,1)S(1)} %copy-done.5, bf16[128,2048]{1,0:T(8,128)(2,1)S(1)} %collective-permute-done.halo, bf16[128,128]{1,0:T(8,128)(2,1)S(1)} %copy-done.7, ...), custom_call_target="tpu_custom_call" | custom-call | flops 1024 | bytes 1024 | tf_op jit(solution)/shard_map/hyena_mix/pallas_call | solution.py:115
  33.3 1.4 %fusion.2 = (bf16[384,512]{1,0:T(8,128)(2,1)S(1)}, bf16[384,512]{1,0:T(8,128)(2,1)S(1)}, bf16[384,512]{1,0:T(8,128)(2,1)S(1)}) fusion(bf16[384,2048]{1,0:T(8,128)(2,1)} %hyena_mix.1.v), kind=kLoop, calls=%fused_computation.5 | loop fusion | bytes 2359296 | tf_op jit(solution)/shard_map/slice | solution.py:381
  34.7 0.7 collective-permute-start.4
  35.4 0.7 collective-permute-start.12
  36.1 0.1 pad_maximum_fusion
  36.1 0.0 copy-start.2
  36.1 0.8 collective-permute-done.2.rest_1_
  36.9 1.3 %collective-permute-start.7 = (bf16[384,1024]{1,0:T(8,128)(2,1)S(1)}, bf16[384,1024]{1,0:T(8,128)(2,1)S(1)}, u32[]{:S(2)}, u32[]{:S(2)}) collective-permute-start(bf16[384,1024]{1,0:T(8,128)(2,1)S(1)} %get-tuple-element.41), channel_id=1, source_target_pairs={{8,4},{12,8},{9,5},{13,9},{10,6},{14,10},{11,7},{15,11},{24,20},{2... | collective-permute-start | bytes 2359304 | tf_op jit(solution)/shard_map/ppermute | solution.py:379
  38.3 0.0 collective-permute-done.1.rest_0_
  38.3 0.0 collective-permute-done.4.rest_3_
  38.3 0.0 collective-permute-done.3.rest_2_
  38.3 3.0 %attend_parts.5 = (bf16[384,512]{1,0:T(8,128)(2,1)S(1)}, f32[32,128]{1,0:T(8,128)S(1)}, bf16[400,512]{1,0:T(8,128)(2,1)S(1)}, bf16[272,512]{1,0:T(8,128)(2,1)S(1)}) custom-call(s32[4]{0:T(128)S(1)} %copy-done.8, bf16[384,2048]{1,0:T(8,128)(2,1)S(1)} %copy-done, bf16[384,2048]{1,0:T(8,128)(2,1)} %k.9, bf16[384,2048]{1,0:T(8,128)(2,1)} %hyena_mix.1.v, ...), custom_call_target="tpu_custom_call" | custom-call | flops 1024 | bytes 1024 | tf_op jit(solution)/shard_map/attend_parts/pallas_call | solution.py:283
  41.3 0.7 collective-permute-start.9
  42.0 1.3 %collective-permute-start.6 = (bf16[272,512]{1,0:T(8,128)(2,1)S(1)}, bf16[272,512]{1,0:T(8,128)(2,1)S(1)}, u32[]{:S(2)}, u32[]{:S(2)}) collective-permute-start(bf16[272,512]{1,0:T(8,128)(2,1)S(1)} %get-tuple-element.39), channel_id=1, source_target_pairs={{4,12},{5,13},{6,14},{7,15},{20,28},{21,29},{22,30},{23,31}} | collective-permute-start | bytes 835592 | tf_op jit(solution)/shard_map/ppermute | solution.py:379
  43.3 1.3 %collective-permute-start.5 = (bf16[400,512]{1,0:T(8,128)(2,1)S(1)}, bf16[400,512]{1,0:T(8,128)(2,1)S(1)}, u32[]{:S(2)}, u32[]{:S(2)}) collective-permute-start(bf16[400,512]{1,0:T(8,128)(2,1)S(1)} %get-tuple-element.38), channel_id=1, source_target_pairs={{4,8},{8,12},{5,9},{9,13},{6,10},{10,14},{7,11},{11,15},{20,24},{2... | collective-permute-start | bytes 1228808 | tf_op jit(solution)/shard_map/ppermute | solution.py:379
  44.6 0.0 collective-permute-done.12.rest_3_
  44.7 17.5 %collective-permute-start.8 = (bf16[256,1024]{1,0:T(8,128)(2,1)S(1)}, bf16[256,1024]{1,0:T(8,128)(2,1)S(1)}, u32[]{:S(2)}, u32[]{:S(2)}) collective-permute-start(bf16[256,1024]{1,0:T(8,128)(2,1)S(1)} %get-tuple-element.43), channel_id=1, source_target_pairs={{12,4},{13,5},{14,6},{15,7},{28,20},{29,21},{30,22},{31,23}} | collective-permute-start | bytes 1572872 | tf_op jit(solution)/shard_map/ppermute | solution.py:379
  62.2 1.1 fusion.1
  63.2 3.1 %attend_parts.7 = (bf16[384,512]{1,0:T(8,128)(2,1)S(1)}, f32[32,128]{1,0:T(8,128)S(1)}, bf16[400,512]{1,0:T(8,128)(2,1)S(1)}, bf16[272,512]{1,0:T(8,128)(2,1)S(1)}) custom-call(s32[4]{0:T(128)S(1)} %copy-done.8, bf16[384,2048]{1,0:T(8,128)(2,1)S(1)} %copy-done, bf16[384,2048]{1,0:T(8,128)(2,1)} %k.9, bf16[384,2048]{1,0:T(8,128)(2,1)} %hyena_mix.1.v, ...), custom_call_target="tpu_custom_call" | custom-call | flops 1024 | bytes 1024 | tf_op jit(solution)/shard_map/attend_parts/pallas_call | solution.py:283
  66.3 0.0 collective-permute-done.6.rest_1_
  66.3 1.3 %collective-permute-start.17 = (bf16[272,512]{1,0:T(8,128)(2,1)S(1)}, bf16[272,512]{1,0:T(8,128)(2,1)S(1)}, u32[]{:S(2)}, u32[]{:S(2)}) collective-permute-start(bf16[272,512]{1,0:T(8,128)(2,1)S(1)} %get-tuple-element.57), channel_id=1, source_target_pairs={{4,12},{5,13},{6,14},{7,15},{20,28},{21,29},{22,30},{23,31}} | collective-permute-start | bytes 835592 | tf_op jit(solution)/shard_map/ppermute | solution.py:379
  67.7 0.0 collective-permute-done.5.rest_0_
  67.7 0.7 collective-permute-start.18
  68.4 1.3 %collective-permute-start.16 = (bf16[400,512]{1,0:T(8,128)(2,1)S(1)}, bf16[400,512]{1,0:T(8,128)(2,1)S(1)}, u32[]{:S(2)}, u32[]{:S(2)}) collective-permute-start(bf16[400,512]{1,0:T(8,128)(2,1)S(1)} %get-tuple-element.56), channel_id=1, source_target_pairs={{4,8},{8,12},{5,9},{9,13},{6,10},{10,14},{7,11},{11,15},{20,24},{2... | collective-permute-start | bytes 1228808 | tf_op jit(solution)/shard_map/ppermute | solution.py:379
  69.7 0.3 collective-permute-done.8.rest_1_
  70.0 3.0 %attend_parts.6 = (bf16[384,512]{1,0:T(8,128)(2,1)S(1)}, f32[32,128]{1,0:T(8,128)S(1)}, bf16[400,512]{1,0:T(8,128)(2,1)S(1)}, bf16[272,512]{1,0:T(8,128)(2,1)S(1)}) custom-call(s32[4]{0:T(128)S(1)} %copy-done.8, bf16[384,2048]{1,0:T(8,128)(2,1)S(1)} %copy-done, bf16[384,2048]{1,0:T(8,128)(2,1)} %k.9, bf16[384,2048]{1,0:T(8,128)(2,1)} %hyena_mix.1.v, ...), custom_call_target="tpu_custom_call" | custom-call | flops 1024 | bytes 1024 | tf_op jit(solution)/shard_map/attend_parts/pallas_call | solution.py:283
  73.1 0.0 copy-start.3
  73.1 1.4 %collective-permute-start.10 = (bf16[400,512]{1,0:T(8,128)(2,1)S(1)}, bf16[400,512]{1,0:T(8,128)(2,1)S(1)}, u32[]{:S(2)}, u32[]{:S(2)}) collective-permute-start(bf16[400,512]{1,0:T(8,128)(2,1)S(1)} %get-tuple-element.45), channel_id=1, source_target_pairs={{4,8},{8,12},{5,9},{9,13},{6,10},{10,14},{7,11},{11,15},{20,24},{2... | collective-permute-start | bytes 1228808 | tf_op jit(solution)/shard_map/ppermute | solution.py:379
  74.5 0.7 collective-permute-start.13
  75.2 4.5 %collective-permute-done.17.rest_1_ = bf16[272,512]{1,0:T(8,128)(2,1)S(1)} collective-permute-done((bf16[272,512]{1,0:T(8,128)(2,1)S(1)}, bf16[272,512]{1,0:T(8,128)(2,1)S(1)}, u32[]{:S(2)}, u32[]{:S(2)}) %collective-permute-start.17) | collective-permute-done | bytes 278560 | tf_op jit(solution)/shard_map/ppermute | solution.py:379
  79.7 1.3 %collective-permute-start.11 = (bf16[272,512]{1,0:T(8,128)(2,1)S(1)}, bf16[272,512]{1,0:T(8,128)(2,1)S(1)}, u32[]{:S(2)}, u32[]{:S(2)}) collective-permute-start(bf16[272,512]{1,0:T(8,128)(2,1)S(1)} %get-tuple-element.46), channel_id=1, source_target_pairs={{4,12},{5,13},{6,14},{7,15},{20,28},{21,29},{22,30},{23,31}} | collective-permute-start | bytes 835592 | tf_op jit(solution)/shard_map/ppermute | solution.py:379
  81.0 1.9 %join_parts.5 = (bf16[384,2048]{1,0:T(8,128)(2,1)}, f32[8,128]{1,0:T(8,128)}) custom-call(bf16[384,512]{1,0:T(8,128)(2,1)S(1)} %get-tuple-element.47.o, f32[32,128]{1,0:T(8,128)S(1)} %get-tuple-element.42.s, bf16[400,512]{1,0:T(8,128)(2,1)S(1)} %collective-permute-done.5.rest_0_, bf16[272,512]{1,0:T(8,128)(2,1)S(1)} %collective-permute-done.6.rest_1_), custom_call_target="tpu_custom_call" | custom-call | flops 1024 | bytes 1024 | tf_op jit(solution)/shard_map/join_parts/pallas_call | solution.py:342
  82.9 5.0 %collective-permute-done.16.rest_0_ = bf16[400,512]{1,0:T(8,128)(2,1)S(1)} collective-permute-done((bf16[400,512]{1,0:T(8,128)(2,1)S(1)}, bf16[400,512]{1,0:T(8,128)(2,1)S(1)}, u32[]{:S(2)}, u32[]{:S(2)}) %collective-permute-start.16) | collective-permute-done | bytes 409632 | tf_op jit(solution)/shard_map/ppermute | solution.py:379
  87.9 2.1 %attend_parts.9 = (bf16[384,256]{1,0:T(8,128)(2,1)S(1)}, f32[16,128]{1,0:T(8,128)S(1)}, bf16[400,256]{1,0:T(8,128)(2,1)S(1)}, bf16[272,256]{1,0:T(8,128)(2,1)S(1)}) custom-call(s32[4]{0:T(128)S(1)} %copy-done.8, bf16[384,2048]{1,0:T(8,128)(2,1)S(1)} %copy-done, bf16[384,2048]{1,0:T(8,128)(2,1)S(1)} %copy-done.3, bf16[384,2048]{1,0:T(8,128)(2,1)} %hyena_mix.1.v, ...), custom_call_target="tpu_custom_call" | custom-call | flops 1024 | bytes 1024 | tf_op jit(solution)/shard_map/attend_parts/pallas_call | solution.py:283
  90.0 1.3 %collective-permute-start.19 = (bf16[400,256]{1,0:T(8,128)(2,1)S(1)}, bf16[400,256]{1,0:T(8,128)(2,1)S(1)}, u32[]{:S(2)}, u32[]{:S(2)}) collective-permute-start(bf16[400,256]{1,0:T(8,128)(2,1)S(1)} %get-tuple-element.62), channel_id=1, source_target_pairs={{4,8},{8,12},{5,9},{9,13},{6,10},{10,14},{7,11},{11,15},{20,24},{2... | collective-permute-start | bytes 614408 | tf_op jit(solution)/shard_map/ppermute | solution.py:379
  91.3 11.4 %collective-permute-done.11.rest_1_ = bf16[272,512]{1,0:T(8,128)(2,1)S(1)} collective-permute-done((bf16[272,512]{1,0:T(8,128)(2,1)S(1)}, bf16[272,512]{1,0:T(8,128)(2,1)S(1)}, u32[]{:S(2)}, u32[]{:S(2)}) %collective-permute-start.11) | collective-permute-done | bytes 278560 | tf_op jit(solution)/shard_map/ppermute | solution.py:379
  102.8 0.0 collective-permute-done.10.rest_0_
  102.8 0.0 collective-permute-done.13.rest_2_.rest_3_
  102.8 1.9 %attend_parts.8 = (bf16[384,256]{1,0:T(8,128)(2,1)S(1)}, f32[16,128]{1,0:T(8,128)S(1)}, bf16[400,256]{1,0:T(8,128)(2,1)S(1)}, bf16[272,256]{1,0:T(8,128)(2,1)S(1)}) custom-call(s32[4]{0:T(128)S(1)} %copy-done.8, bf16[384,2048]{1,0:T(8,128)(2,1)S(1)} %copy-done, bf16[384,2048]{1,0:T(8,128)(2,1)S(1)} %copy-done.3, bf16[384,2048]{1,0:T(8,128)(2,1)} %hyena_mix.1.v, ...), custom_call_target="tpu_custom_call" | custom-call | flops 1024 | bytes 1024 | tf_op jit(solution)/shard_map/attend_parts/pallas_call | solution.py:283
  104.7 1.3 %collective-permute-start.14 = (bf16[400,256]{1,0:T(8,128)(2,1)S(1)}, bf16[400,256]{1,0:T(8,128)(2,1)S(1)}, u32[]{:S(2)}, u32[]{:S(2)}) collective-permute-start(bf16[400,256]{1,0:T(8,128)(2,1)S(1)} %get-tuple-element.54), channel_id=1, source_target_pairs={{4,8},{8,12},{5,9},{9,13},{6,10},{10,14},{7,11},{11,15},{20,24},{2... | collective-permute-start | bytes 614408 | tf_op jit(solution)/shard_map/ppermute | solution.py:379
  106.0 1.3 %collective-permute-start.20 = (bf16[272,256]{1,0:T(8,128)(2,1)S(1)}, bf16[272,256]{1,0:T(8,128)(2,1)S(1)}, u32[]{:S(2)}, u32[]{:S(2)}) collective-permute-start(bf16[272,256]{1,0:T(8,128)(2,1)S(1)} %get-tuple-element.63), channel_id=1, source_target_pairs={{4,12},{5,13},{6,14},{7,15},{20,28},{21,29},{22,30},{23,31}} | collective-permute-start | bytes 417800 | tf_op jit(solution)/shard_map/ppermute | solution.py:379
  107.3 1.3 %collective-permute-start.15 = (bf16[272,256]{1,0:T(8,128)(2,1)S(1)}, bf16[272,256]{1,0:T(8,128)(2,1)S(1)}, u32[]{:S(2)}, u32[]{:S(2)}) collective-permute-start(bf16[272,256]{1,0:T(8,128)(2,1)S(1)} %get-tuple-element.55), channel_id=1, source_target_pairs={{4,12},{5,13},{6,14},{7,15},{20,28},{21,29},{22,30},{23,31}} | collective-permute-start | bytes 417800 | tf_op jit(solution)/shard_map/ppermute | solution.py:379
  108.6 1.9 %join_parts.6 = (bf16[384,2048]{1,0:T(8,128)(2,1)}, f32[8,128]{1,0:T(8,128)}) custom-call(bf16[384,512]{1,0:T(8,128)(2,1)S(1)} %get-tuple-element.66.o, f32[32,128]{1,0:T(8,128)S(1)} %get-tuple-element.50.s, bf16[400,512]{1,0:T(8,128)(2,1)S(1)} %collective-permute-done.16.rest_0_, ...), custom_call_target="tpu_custom_call", output_to_operand_aliasing={{0}: (4, {})} | custom-call | flops 1024 | bytes 1024 | tf_op jit(solution)/shard_map/join_parts/pallas_call | solution.py:342
  110.5 1.9 %join_parts.7 = (bf16[384,2048]{1,0:T(8,128)(2,1)}, f32[8,128]{1,0:T(8,128)}) custom-call(bf16[384,512]{1,0:T(8,128)(2,1)S(1)} %get-tuple-element.64.o, f32[32,128]{1,0:T(8,128)S(1)} %get-tuple-element.65.s, bf16[400,512]{1,0:T(8,128)(2,1)S(1)} %collective-permute-done.10.rest_0_, ...), custom_call_target="tpu_custom_call", output_to_operand_aliasing={{0}: (4, {})} | custom-call | flops 1024 | bytes 1024 | tf_op jit(solution)/shard_map/join_parts/pallas_call | solution.py:342
  112.4 1.5 %collective-permute-done.20.rest_1_ = bf16[272,256]{1,0:T(8,128)(2,1)S(1)} collective-permute-done((bf16[272,256]{1,0:T(8,128)(2,1)S(1)}, bf16[272,256]{1,0:T(8,128)(2,1)S(1)}, u32[]{:S(2)}, u32[]{:S(2)}) %collective-permute-start.20) | collective-permute-done | bytes 139296 | tf_op jit(solution)/shard_map/ppermute | solution.py:379
  113.9 1.2 %join_parts.8 = (bf16[384,2048]{1,0:T(8,128)(2,1)}, f32[8,128]{1,0:T(8,128)}) custom-call(bf16[384,256]{1,0:T(8,128)(2,1)S(1)} %get-tuple-element.60.o, f32[16,128]{1,0:T(8,128)S(1)} %get-tuple-element.61.s, bf16[400,256]{1,0:T(8,128)(2,1)S(1)} %collective-permute-done.19.rest_0_, ...), custom_call_target="tpu_custom_call", output_to_operand_aliasing={{0}: (4, {})} | custom-call | flops 1024 | bytes 1024 | tf_op jit(solution)/shard_map/join_parts/pallas_call | solution.py:342
  115.2 0.2 collective-permute-done.15.rest_1_
  115.4 0.5 collective-permute-done.14.rest_0_
  115.9 1.2 %join_parts.9 = (bf16[384,2048]{1,0:T(8,128)(2,1)}, f32[8,128]{1,0:T(8,128)}) custom-call(bf16[384,256]{1,0:T(8,128)(2,1)S(1)} %get-tuple-element.52.o, f32[16,128]{1,0:T(8,128)S(1)} %get-tuple-element.53.s, bf16[400,256]{1,0:T(8,128)(2,1)S(1)} %collective-permute-done.14.rest_0_, ...), custom_call_target="tpu_custom_call", output_to_operand_aliasing={{0}: (4, {})} | custom-call | flops 1024 | bytes 1024 | tf_op jit(solution)/shard_map/join_parts/pallas_call | solution.py:342
  (21 shorter events, 0.1 us)
Async XLA Ops:
  0.6 3.5 %copy-start = (bf16[384,2048]{1,0:T(8,128)(2,1)S(1)}, bf16[384,2048]{1,0:T(8,128)(2,1)}, u32[]{:S(2)}) copy-start(bf16[384,2048]{1,0:T(8,128)(2,1)} %q.9) | copy-start | bytes 4718596
  2.7 6.5 %copy-start.1 = (bf16[384,2048]{1,0:T(8,128)(2,1)S(1)}, bf16[384,2048]{1,0:T(8,128)(2,1)}, u32[]{:S(2)}) copy-start(bf16[384,2048]{1,0:T(8,128)(2,1)} %k.9) | copy-start | bytes 4718596
  2.7 15.9 %collective-permute-start = (bf16[128,2048]{1,0:T(8,128)(2,1)}, bf16[128,2048]{1,0:T(8,128)(2,1)S(1)}, u32[]{:S(2)}, u32[]{:S(2)}) collective-permute-start(bf16[128,2048]{1,0:T(8,128)(2,1)} %halo_product.1), channel_id=1, source_target_pairs={{0,4},{4,8},{8,12},{1,5},{5,9},{9,13},{2,6},{6,10},{10,14},{3,7},{... | collective-permute-start | bytes 1572872 | tf_op jit(solution)/shard_map/ppermute | solution.py:379
  4.2 18.1 %copy-start.6 = (bf16[384,2048]{1,0:T(8,128)(2,1)S(1)}, bf16[384,2048]{1,0:T(8,128)(2,1)}, u32[]{:S(2)}) copy-start(bf16[384,2048]{1,0:T(8,128)(2,1)} %hq.1) | copy-start | bytes 4718596
  4.3 18.0 %copy-start.4 = (bf16[384,2048]{1,0:T(8,128)(2,1)S(1)}, bf16[384,2048]{1,0:T(8,128)(2,1)}, u32[]{:S(2)}) copy-start(bf16[384,2048]{1,0:T(8,128)(2,1)} %hk.3) | copy-start | bytes 4718596
  4.3 18.0 %copy-start.5 = (bf16[384,2048]{1,0:T(8,128)(2,1)S(1)}, bf16[384,2048]{1,0:T(8,128)(2,1)}, u32[]{:S(2)}) copy-start(bf16[384,2048]{1,0:T(8,128)(2,1)} %hv.3) | copy-start | bytes 4718596
  4.3 18.0 %copy-start.7 = (bf16[128,128]{1,0:T(8,128)(2,1)S(1)}, bf16[128,128]{1,0:T(8,128)(2,1)}, u32[]{:S(2)}) copy-start(bf16[128,128]{1,0:T(8,128)(2,1)} %filters.1) | copy-start | bytes 98308
  4.3 18.0 %copy-start.8 = (s32[4]{0:T(128)S(1)}, s32[4]{0:T(128)}, u32[]{:S(2)}) copy-start(s32[4]{0:T(128)} %info.8) | copy-start | bytes 52
  4.4 18.0 %copy-start.9 = (f32[2048]{0:T(1024)S(1)}, f32[2048]{0:T(1024)}, u32[]{:S(2)}) copy-start(f32[2048]{0:T(1024)} %param.12) | copy-start | bytes 24580
  4.4 33.9 %collective-permute-start.1 = (bf16[384,1024]{1,0:T(8,128)(2,1)S(1)}, bf16[384,1024]{1,0:T(8,128)(2,1)S(1)}, u32[]{:S(2)}, u32[]{:S(2)}) collective-permute-start(bf16[384,1024]{1,0:T(8,128)(2,1)S(1)} %get-tuple-element.82), channel_id=1, source_target_pairs={{8,4},{12,8},{9,5},{13,9},{10,6},{14,10},{11,7},{15,11},{24,20},{2... | collective-permute-start | bytes 2359304 | tf_op jit(solution)/shard_map/ppermute | solution.py:379
  18.6 19.7 %collective-permute-start.3 = (bf16[384,1024]{1,0:T(8,128)(2,1)S(1)}, bf16[384,1024]{1,0:T(8,128)(2,1)S(1)}, u32[]{:S(2)}, u32[]{:S(2)}) collective-permute-start(bf16[384,1024]{1,0:T(8,128)(2,1)S(1)} %slice.45), channel_id=1, source_target_pairs={{0,4},{1,5},{2,6},{3,7},{16,20},{17,21},{18,22},{19,23}} | collective-permute-start | bytes 2359304 | tf_op jit(solution)/shard_map/ppermute | solution.py:379
  19.4 17.5 %collective-permute-start.2 = (bf16[256,1024]{1,0:T(8,128)(2,1)S(1)}, bf16[256,1024]{1,0:T(8,128)(2,1)S(1)}, u32[]{:S(2)}, u32[]{:S(2)}) collective-permute-start(bf16[256,1024]{1,0:T(8,128)(2,1)S(1)} %get-tuple-element.80), channel_id=1, source_target_pairs={{12,4},{13,5},{14,6},{15,7},{28,20},{29,21},{30,22},{31,23}} | collective-permute-start | bytes 1572872 | tf_op jit(solution)/shard_map/ppermute | solution.py:379
  33.3 2.8 %slice-start = ((bf16[384,2048]{1,0:T(8,128)(2,1)}), bf16[384,512]{1,0:T(8,128)(2,1)S(1)}, s32[]{:S(2)}) async-start(bf16[384,2048]{1,0:T(8,128)(2,1)} %k.9), calls=%async_computation | async-start | bytes 786432 | tf_op jit(solution)/shard_map/slice | solution.py:381
  34.7 3.6 %collective-permute-start.4 = (bf16[384,512]{1,0:T(8,128)(2,1)S(1)}, bf16[384,512]{1,0:T(8,128)(2,1)S(1)}, u32[]{:S(2)}, u32[]{:S(2)}) collective-permute-start(bf16[384,512]{1,0:T(8,128)(2,1)S(1)} %get-tuple-element.78), channel_id=1, source_target_pairs={{0,4},{1,5},{2,6},{3,7},{16,20},{17,21},{18,22},{19,23}} | collective-permute-start | bytes 1179656 | tf_op jit(solution)/shard_map/ppermute | solution.py:379
  35.4 9.3 %collective-permute-start.12 = (bf16[384,512]{1,0:T(8,128)(2,1)S(1)}, bf16[384,512]{1,0:T(8,128)(2,1)S(1)}, u32[]{:S(2)}, u32[]{:S(2)}) collective-permute-start(bf16[384,512]{1,0:T(8,128)(2,1)S(1)} %get-tuple-element.76), channel_id=1, source_target_pairs={{0,4},{1,5},{2,6},{3,7},{16,20},{17,21},{18,22},{19,23}} | collective-permute-start | bytes 1179656 | tf_op jit(solution)/shard_map/ppermute | solution.py:379
  36.1 26.0 %copy-start.2 = (bf16[384,2048]{1,0:T(8,128)(2,1)S(1)}, bf16[384,2048]{1,0:T(8,128)(2,1)}, u32[]{:S(2)}) copy-start(bf16[384,2048]{1,0:T(8,128)(2,1)} %k.9) | copy-start | bytes 4718596
  36.9 31.4 %collective-permute-start.7 = (bf16[384,1024]{1,0:T(8,128)(2,1)S(1)}, bf16[384,1024]{1,0:T(8,128)(2,1)S(1)}, u32[]{:S(2)}, u32[]{:S(2)}) collective-permute-start(bf16[384,1024]{1,0:T(8,128)(2,1)S(1)} %get-tuple-element.41), channel_id=1, source_target_pairs={{8,4},{12,8},{9,5},{13,9},{10,6},{14,10},{11,7},{15,11},{24,20},{2... | collective-permute-start | bytes 2359304 | tf_op jit(solution)/shard_map/ppermute | solution.py:379
  41.3 28.7 %collective-permute-start.9 = (bf16[768,512]{1,0:T(8,128)(2,1)S(1)}, bf16[768,512]{1,0:T(8,128)(2,1)S(1)}, u32[]{:S(2)}, u32[]{:S(2)}) collective-permute-start(bf16[768,512]{1,0:T(8,128)(2,1)S(1)} %pad_maximum_fusion), channel_id=1, source_target_pairs={{0,4},{1,5},{2,6},{3,7},{16,20},{17,21},{18,22},{19,23}} | collective-permute-start | bytes 2359304 | tf_op jit(solution)/shard_map/ppermute | solution.py:379
  42.0 24.3 %collective-permute-start.6 = (bf16[272,512]{1,0:T(8,128)(2,1)S(1)}, bf16[272,512]{1,0:T(8,128)(2,1)S(1)}, u32[]{:S(2)}, u32[]{:S(2)}) collective-permute-start(bf16[272,512]{1,0:T(8,128)(2,1)S(1)} %get-tuple-element.39), channel_id=1, source_target_pairs={{4,12},{5,13},{6,14},{7,15},{20,28},{21,29},{22,30},{23,31}} | collective-permute-start | bytes 835592 | tf_op jit(solution)/shard_map/ppermute | solution.py:379
  43.3 24.3 %collective-permute-start.5 = (bf16[400,512]{1,0:T(8,128)(2,1)S(1)}, bf16[400,512]{1,0:T(8,128)(2,1)S(1)}, u32[]{:S(2)}, u32[]{:S(2)}) collective-permute-start(bf16[400,512]{1,0:T(8,128)(2,1)S(1)} %get-tuple-element.38), channel_id=1, source_target_pairs={{4,8},{8,12},{5,9},{9,13},{6,10},{10,14},{7,11},{11,15},{20,24},{2... | collective-permute-start | bytes 1228808 | tf_op jit(solution)/shard_map/ppermute | solution.py:379
  44.7 25.3 %collective-permute-start.8 = (bf16[256,1024]{1,0:T(8,128)(2,1)S(1)}, bf16[256,1024]{1,0:T(8,128)(2,1)S(1)}, u32[]{:S(2)}, u32[]{:S(2)}) collective-permute-start(bf16[256,1024]{1,0:T(8,128)(2,1)S(1)} %get-tuple-element.43), channel_id=1, source_target_pairs={{12,4},{13,5},{14,6},{15,7},{28,20},{29,21},{30,22},{31,23}} | collective-permute-start | bytes 1572872 | tf_op jit(solution)/shard_map/ppermute | solution.py:379
  66.3 13.4 %collective-permute-start.17 = (bf16[272,512]{1,0:T(8,128)(2,1)S(1)}, bf16[272,512]{1,0:T(8,128)(2,1)S(1)}, u32[]{:S(2)}, u32[]{:S(2)}) collective-permute-start(bf16[272,512]{1,0:T(8,128)(2,1)S(1)} %get-tuple-element.57), channel_id=1, source_target_pairs={{4,12},{5,13},{6,14},{7,15},{20,28},{21,29},{22,30},{23,31}} | collective-permute-start | bytes 835592 | tf_op jit(solution)/shard_map/ppermute | solution.py:379
  67.7 20.3 %collective-permute-start.18 = (bf16[768,256]{1,0:T(8,128)(2,1)S(1)}, bf16[768,256]{1,0:T(8,128)(2,1)S(1)}, u32[]{:S(2)}, u32[]{:S(2)}) collective-permute-start(bf16[768,256]{1,0:T(8,128)(2,1)S(1)} %pad_maximum_fusion.2), channel_id=1, source_target_pairs={{0,4},{1,5},{2,6},{3,7},{16,20},{17,21},{18,22},{19,23}} | collective-permute-start | bytes 1179656 | tf_op jit(solution)/shard_map/ppermute | solution.py:379
  68.4 19.5 %collective-permute-start.16 = (bf16[400,512]{1,0:T(8,128)(2,1)S(1)}, bf16[400,512]{1,0:T(8,128)(2,1)S(1)}, u32[]{:S(2)}, u32[]{:S(2)}) collective-permute-start(bf16[400,512]{1,0:T(8,128)(2,1)S(1)} %get-tuple-element.56), channel_id=1, source_target_pairs={{4,8},{8,12},{5,9},{9,13},{6,10},{10,14},{7,11},{11,15},{20,24},{2... | collective-permute-start | bytes 1228808 | tf_op jit(solution)/shard_map/ppermute | solution.py:379
  73.1 14.9 %copy-start.3 = (bf16[384,2048]{1,0:T(8,128)(2,1)S(1)}, bf16[384,2048]{1,0:T(8,128)(2,1)}, u32[]{:S(2)}) copy-start(bf16[384,2048]{1,0:T(8,128)(2,1)} %k.9) | copy-start | bytes 4718596
  73.1 29.7 %collective-permute-start.10 = (bf16[400,512]{1,0:T(8,128)(2,1)S(1)}, bf16[400,512]{1,0:T(8,128)(2,1)S(1)}, u32[]{:S(2)}, u32[]{:S(2)}) collective-permute-start(bf16[400,512]{1,0:T(8,128)(2,1)S(1)} %get-tuple-element.45), channel_id=1, source_target_pairs={{4,8},{8,12},{5,9},{9,13},{6,10},{10,14},{7,11},{11,15},{20,24},{2... | collective-permute-start | bytes 1228808 | tf_op jit(solution)/shard_map/ppermute | solution.py:379
  74.5 28.3 %collective-permute-start.13 = (bf16[768,256]{1,0:T(8,128)(2,1)S(1)}, bf16[768,256]{1,0:T(8,128)(2,1)S(1)}, u32[]{:S(2)}, u32[]{:S(2)}) collective-permute-start(bf16[768,256]{1,0:T(8,128)(2,1)S(1)} %pad_maximum_fusion.1), channel_id=1, source_target_pairs={{0,4},{1,5},{2,6},{3,7},{16,20},{17,21},{18,22},{19,23}} | collective-permute-start | bytes 1179656 | tf_op jit(solution)/shard_map/ppermute | solution.py:379
  79.7 23.1 %collective-permute-start.11 = (bf16[272,512]{1,0:T(8,128)(2,1)S(1)}, bf16[272,512]{1,0:T(8,128)(2,1)S(1)}, u32[]{:S(2)}, u32[]{:S(2)}) collective-permute-start(bf16[272,512]{1,0:T(8,128)(2,1)S(1)} %get-tuple-element.46), channel_id=1, source_target_pairs={{4,12},{5,13},{6,14},{7,15},{20,28},{21,29},{22,30},{23,31}} | collective-permute-start | bytes 835592 | tf_op jit(solution)/shard_map/ppermute | solution.py:379
  90.0 23.9 %collective-permute-start.19 = (bf16[400,256]{1,0:T(8,128)(2,1)S(1)}, bf16[400,256]{1,0:T(8,128)(2,1)S(1)}, u32[]{:S(2)}, u32[]{:S(2)}) collective-permute-start(bf16[400,256]{1,0:T(8,128)(2,1)S(1)} %get-tuple-element.62), channel_id=1, source_target_pairs={{4,8},{8,12},{5,9},{9,13},{6,10},{10,14},{7,11},{11,15},{20,24},{2... | collective-permute-start | bytes 614408 | tf_op jit(solution)/shard_map/ppermute | solution.py:379
  104.7 11.2 %collective-permute-start.14 = (bf16[400,256]{1,0:T(8,128)(2,1)S(1)}, bf16[400,256]{1,0:T(8,128)(2,1)S(1)}, u32[]{:S(2)}, u32[]{:S(2)}) collective-permute-start(bf16[400,256]{1,0:T(8,128)(2,1)S(1)} %get-tuple-element.54), channel_id=1, source_target_pairs={{4,8},{8,12},{5,9},{9,13},{6,10},{10,14},{7,11},{11,15},{20,24},{2... | collective-permute-start | bytes 614408 | tf_op jit(solution)/shard_map/ppermute | solution.py:379
  106.0 7.9 %collective-permute-start.20 = (bf16[272,256]{1,0:T(8,128)(2,1)S(1)}, bf16[272,256]{1,0:T(8,128)(2,1)S(1)}, u32[]{:S(2)}, u32[]{:S(2)}) collective-permute-start(bf16[272,256]{1,0:T(8,128)(2,1)S(1)} %get-tuple-element.63), channel_id=1, source_target_pairs={{4,12},{5,13},{6,14},{7,15},{20,28},{21,29},{22,30},{23,31}} | collective-permute-start | bytes 417800 | tf_op jit(solution)/shard_map/ppermute | solution.py:379
  107.3 8.1 %collective-permute-start.15 = (bf16[272,256]{1,0:T(8,128)(2,1)S(1)}, bf16[272,256]{1,0:T(8,128)(2,1)S(1)}, u32[]{:S(2)}, u32[]{:S(2)}) collective-permute-start(bf16[272,256]{1,0:T(8,128)(2,1)S(1)} %get-tuple-element.55), channel_id=1, source_target_pairs={{4,12},{5,13},{6,14},{7,15},{20,28},{21,29},{22,30},{23,31}} | collective-permute-start | bytes 417800 | tf_op jit(solution)/shard_map/ppermute | solution.py:379

commit v5 on v4

--- a/solution.py
+++ b/solution.py
@@ -384,7 +384,8 @@
     mix = hyena(starts, hq, hk, hv, halo, filters, gain)
     heads, total = plan.heads, channels // HEAD_DIM
     early = sum(heads[:2])
-    rk = send(after(columns(k, 0, early), halo), plan.k)
+    rk = [send(columns(k, 0, heads[0]), plan.k)]
+    rk.append(send(after(columns(k, heads[0], early), halo), plan.k))
     qa = send(columns(q, 0, early), plan.a)
     qb = send(columns(q[: plan.nb], 0, early), plan.b)
     later_a = send(after(columns(q, early, total), halo), plan.a)
@@ -397,7 +398,7 @@
             q_at, qa = first, later_a
             qb = send(after(columns(q[: plan.nb], early, total), told[0]), plan.b)
         if end <= early:
-            keys = (rk, first)
+            keys = (rk[c], 0)
             values = (send(columns(mix, first, end), plan.k), 0, 0)
             go = values[0] if go is None else go
         else:

time: 119 us -> 119 us (level)
  waiting for transfers between devices: 33.5 us -> 28.9 us
  starting transfers between devices: 45.1 us -> 48.7 us
    ppermute x21 -> x22, waiting for transfers between devices: 33.5 us -> 28.9 us  [run_plan(): send = lambda x, pairs: lax.ppermute(x, 'ctx', pairs)]
    ppermute x21 -> x22, starting transfers between devices: 45.1 us -> 48.7 us  [run_plan(): send = lambda x, pairs: lax.ppermute(x, 'ctx', pairs)]
    slice x8 -> x6, local copies, waits for them, and re-layouts: 2.73 us -> 3.72 us  [run_plan(): columns = lambda x, first, end: x[:, first * HEAD_DIM:end * HEAD_DIM]]
  transfers between devices with their start and end apart: 21 -> 22, of which waited for: 9 -> 7; matrix products, arithmetic and copies ran while one was open for 2% -> 3% of each run, Pallas kernels for 27% -> 27%
where the time goes in v5:
time: 119 us; the launch traced here: 117 us
  starting transfers between devices  48.7 us (41%)
  Pallas kernels  34.5 us (29%)
  waiting for transfers between devices  28.9 us (24%)
  local copies, waits for them, and re-layouts  3.78 us (3%)
    ppermute x22, starting transfers between devices, run_plan(): send = lambda x, pairs: lax.ppermute(x, 'ctx', pairs)  48.7 us
    ppermute x22, waiting for transfers between devices, run_plan(): send = lambda x, pairs: lax.ppermute(x, 'ctx', pairs)  28.9 us
    pallas_call x5, Pallas kernels, attend(): pl.pallas_call(partial(attend_kernel, starts.shape[0], plan), grid=(heads...  13.1 us
    pallas_call x1, Pallas kernels, hyena(): pl.pallas_call(partial(hyena_kernel, starts.shape[0], group), grid=(chann...  11 us
    pallas_call x5, Pallas kernels, join(): pl.pallas_call(partial(join_kernel, plan), grid=(wide // width,), in_spec...  8.28 us
    slice x6, local copies, waits for them, and re-layouts, run_plan(): columns = lambda x, first, end: x[:, first * HEAD_DIM:end * HEAD_DIM]  3.72 us
  transfers between devices with their start and end apart: 22, of which 7 were waited for; matrix products, arithmetic and copies ran while one was open for 3% of the time, Pallas kernels for 27%

profile of v5, /device:TPU:26, one launch (start us, length us, event | category | flops | bytes accessed | tf_op | source)
XLA Modules:
  0.0 117.0 jit_solution(136762924214818582)
XLA Ops:
  0.6 2.1 %halo_product.1 = bf16[128,2048]{1,0:T(8,128)(2,1)} custom-call(bf16[384,2048]{1,0:T(8,128)(2,1)} %hk.3, bf16[384,2048]{1,0:T(8,128)(2,1)} %hv.3), custom_call_target="tpu_custom_call" | custom-call | flops 1024 | bytes 1024 | tf_op jit(solution)/shard_map/halo_product/pallas_call | solution.py:44
  2.7 1.3 %collective-permute-start = (bf16[128,2048]{1,0:T(8,128)(2,1)}, bf16[128,2048]{1,0:T(8,128)(2,1)S(1)}, u32[]{:S(2)}, u32[]{:S(2)}) collective-permute-start(bf16[128,2048]{1,0:T(8,128)(2,1)} %halo_product.1), channel_id=1, source_target_pairs={{0,4},{4,8},{8,12},{1,5},{5,9},{9,13},{2,6},{6,10},{10,14},{3,7},{... | collective-permute-start | bytes 1572872 | tf_op jit(solution)/shard_map/ppermute | solution.py:379
  4.0 0.0 copy-start.5
  4.0 0.1 fusion.4
  4.1 0.0 copy-start.1
  4.1 4.7 %collective-permute-start.2 = (bf16[256,1024]{1,0:T(8,128)(2,1)S(1)}, bf16[256,1024]{1,0:T(8,128)(2,1)S(1)}, u32[]{:S(2)}, u32[]{:S(2)}) collective-permute-start(bf16[256,1024]{1,0:T(8,128)(2,1)S(1)} %get-tuple-element.83), channel_id=1, source_target_pairs={{12,4},{13,5},{14,6},{15,7},{28,20},{29,21},{30,22},{31,23}} | collective-permute-start | bytes 1572872 | tf_op jit(solution)/shard_map/ppermute | solution.py:379
  8.9 0.0 copy-start.4
  8.9 0.1 fusion.5
  9.0 0.0 copy-start.3
  9.0 0.0 copy-start.6
  9.0 0.0 copy-start.7
  9.1 0.0 copy-start.8
  9.1 1.6 %collective-permute-start.1 = (bf16[384,1024]{1,0:T(8,128)(2,1)S(1)}, bf16[384,1024]{1,0:T(8,128)(2,1)S(1)}, u32[]{:S(2)}, u32[]{:S(2)}) collective-permute-start(bf16[384,1024]{1,0:T(8,128)(2,1)S(1)} %get-tuple-element.85), channel_id=1, source_target_pairs={{8,4},{12,8},{9,5},{13,9},{10,6},{14,10},{11,7},{15,11},{24,20},{2... | collective-permute-start | bytes 2359304 | tf_op jit(solution)/shard_map/ppermute | solution.py:379
  10.7 0.1 fusion.3
  10.8 0.7 collective-permute-start.3
  11.5 7.0 %collective-permute-done.halo = bf16[128,2048]{1,0:T(8,128)(2,1)S(1)} collective-permute-done((bf16[128,2048]{1,0:T(8,128)(2,1)}, bf16[128,2048]{1,0:T(8,128)(2,1)S(1)}, u32[]{:S(2)}, u32[]{:S(2)}) %collective-permute-start) | collective-permute-done | bytes 524320 | tf_op jit(solution)/shard_map/ppermute | solution.py:379
  18.5 11.0 %hyena_mix.1.v = bf16[384,2048]{1,0:T(8,128)(2,1)} custom-call(s32[4]{0:T(128)S(1)} %copy-done.7, bf16[384,2048]{1,0:T(8,128)(2,1)S(1)} %copy-done.5, bf16[384,2048]{1,0:T(8,128)(2,1)S(1)} %copy-done.3, bf16[384,2048]{1,0:T(8,128)(2,1)S(1)} %copy-done.4, bf16[128,2048]{1,0:T(8,128)(2,1)S(1)} %collective-permute-done.halo, bf16[128,128]{1,0:T(8,128)(2,1)S(1)} %copy-done.6, ...), custom_call_target="tpu_custom_call" | custom-call | flops 1024 | bytes 1024 | tf_op jit(solution)/shard_map/hyena_mix/pallas_call | solution.py:115
  29.5 1.3 %fusion.2 = (bf16[384,512]{1,0:T(8,128)(2,1)S(1)}, bf16[384,512]{1,0:T(8,128)(2,1)S(1)}, bf16[384,512]{1,0:T(8,128)(2,1)S(1)}) fusion(bf16[384,2048]{1,0:T(8,128)(2,1)} %hyena_mix.1.v), kind=kLoop, calls=%fused_computation.5 | loop fusion | bytes 2359296 | tf_op jit(solution)/shard_map/slice | solution.py:381
  30.8 0.7 collective-permute-start.4
  31.5 0.7 collective-permute-start.12
  32.2 0.0 collective-permute-done.3.rest_2_
  32.2 0.7 collective-permute-start.13
  32.9 0.1 pad_maximum_fusion
  33.0 0.0 collective-permute-done.2.rest_1_
  33.0 2.4 %collective-permute-start.7 = (bf16[384,1024]{1,0:T(8,128)(2,1)S(1)}, bf16[384,1024]{1,0:T(8,128)(2,1)S(1)}, u32[]{:S(2)}, u32[]{:S(2)}) collective-permute-start(bf16[384,1024]{1,0:T(8,128)(2,1)S(1)} %get-tuple-element.40), channel_id=1, source_target_pairs={{8,4},{12,8},{9,5},{13,9},{10,6},{14,10},{11,7},{15,11},{24,20},{2... | collective-permute-start | bytes 2359304 | tf_op jit(solution)/shard_map/ppermute | solution.py:379
  35.4 2.7 %collective-permute-done.1.rest_0_ = bf16[384,1024]{1,0:T(8,128)(2,1)S(1)} collective-permute-done((bf16[384,1024]{1,0:T(8,128)(2,1)S(1)}, bf16[384,1024]{1,0:T(8,128)(2,1)S(1)}, u32[]{:S(2)}, u32[]{:S(2)}) %collective-permute-start.1) | collective-permute-done | bytes 786464 | tf_op jit(solution)/shard_map/ppermute | solution.py:379
  38.1 0.0 collective-permute-done.4.rest_3_
  38.1 3.0 %attend_parts.5 = (bf16[384,512]{1,0:T(8,128)(2,1)S(1)}, f32[32,128]{1,0:T(8,128)S(1)}, bf16[400,512]{1,0:T(8,128)(2,1)S(1)}, bf16[272,512]{1,0:T(8,128)(2,1)S(1)}) custom-call(s32[4]{0:T(128)S(1)} %copy-done.7, bf16[384,2048]{1,0:T(8,128)(2,1)S(1)} %copy-done, bf16[384,2048]{1,0:T(8,128)(2,1)} %k.9, bf16[384,2048]{1,0:T(8,128)(2,1)} %hyena_mix.1.v, ...), custom_call_target="tpu_custom_call" | custom-call | flops 1024 | bytes 1024 | tf_op jit(solution)/shard_map/attend_parts/pallas_call | solution.py:283
  41.1 0.7 collective-permute-start.9
  41.8 1.3 %collective-permute-start.6 = (bf16[272,512]{1,0:T(8,128)(2,1)S(1)}, bf16[272,512]{1,0:T(8,128)(2,1)S(1)}, u32[]{:S(2)}, u32[]{:S(2)}) collective-permute-start(bf16[272,512]{1,0:T(8,128)(2,1)S(1)} %get-tuple-element.38), channel_id=1, source_target_pairs={{4,12},{5,13},{6,14},{7,15},{20,28},{21,29},{22,30},{23,31}} | collective-permute-start | bytes 835592 | tf_op jit(solution)/shard_map/ppermute | solution.py:379
  43.1 0.0 collective-permute-done.12.rest_2_
  43.1 1.3 %collective-permute-start.5 = (bf16[400,512]{1,0:T(8,128)(2,1)S(1)}, bf16[400,512]{1,0:T(8,128)(2,1)S(1)}, u32[]{:S(2)}, u32[]{:S(2)}) collective-permute-start(bf16[400,512]{1,0:T(8,128)(2,1)S(1)} %get-tuple-element.37), channel_id=1, source_target_pairs={{4,8},{8,12},{5,9},{9,13},{6,10},{10,14},{7,11},{11,15},{20,24},{2... | collective-permute-start | bytes 1228808 | tf_op jit(solution)/shard_map/ppermute | solution.py:379
  44.4 20.8 %collective-permute-start.8 = (bf16[256,1024]{1,0:T(8,128)(2,1)S(1)}, bf16[256,1024]{1,0:T(8,128)(2,1)S(1)}, u32[]{:S(2)}, u32[]{:S(2)}) collective-permute-start(bf16[256,1024]{1,0:T(8,128)(2,1)S(1)} %get-tuple-element.42), channel_id=1, source_target_pairs={{12,4},{13,5},{14,6},{15,7},{28,20},{29,21},{30,22},{31,23}} | collective-permute-start | bytes 1572872 | tf_op jit(solution)/shard_map/ppermute | solution.py:379
  65.2 1.1 fusion
  66.3 1.1 fusion.1
  67.3 3.1 %attend_parts.7 = (bf16[384,512]{1,0:T(8,128)(2,1)S(1)}, f32[32,128]{1,0:T(8,128)S(1)}, bf16[400,512]{1,0:T(8,128)(2,1)S(1)}, bf16[272,512]{1,0:T(8,128)(2,1)S(1)}) custom-call(s32[4]{0:T(128)S(1)} %copy-done.7, bf16[384,2048]{1,0:T(8,128)(2,1)S(1)} %copy-done, bf16[384,2048]{1,0:T(8,128)(2,1)} %k.9, bf16[384,2048]{1,0:T(8,128)(2,1)} %hyena_mix.1.v, ...), custom_call_target="tpu_custom_call" | custom-call | flops 1024 | bytes 1024 | tf_op jit(solution)/shard_map/attend_parts/pallas_call | solution.py:283
  70.4 1.3 %collective-permute-start.18 = (bf16[272,512]{1,0:T(8,128)(2,1)S(1)}, bf16[272,512]{1,0:T(8,128)(2,1)S(1)}, u32[]{:S(2)}, u32[]{:S(2)}) collective-permute-start(bf16[272,512]{1,0:T(8,128)(2,1)S(1)} %get-tuple-element.57), channel_id=1, source_target_pairs={{4,12},{5,13},{6,14},{7,15},{20,28},{21,29},{22,30},{23,31}} | collective-permute-start | bytes 835592 | tf_op jit(solution)/shard_map/ppermute | solution.py:379
  71.8 0.0 collective-permute-done.5.rest_0_
  71.8 0.7 collective-permute-start.19
  72.5 0.0 collective-permute-done.7.rest_0_
  72.5 1.3 %collective-permute-start.17 = (bf16[400,512]{1,0:T(8,128)(2,1)S(1)}, bf16[400,512]{1,0:T(8,128)(2,1)S(1)}, u32[]{:S(2)}, u32[]{:S(2)}) collective-permute-start(bf16[400,512]{1,0:T(8,128)(2,1)S(1)} %get-tuple-element.56), channel_id=1, source_target_pairs={{4,8},{8,12},{5,9},{9,13},{6,10},{10,14},{7,11},{11,15},{20,24},{2... | collective-permute-start | bytes 1228808 | tf_op jit(solution)/shard_map/ppermute | solution.py:379
  73.8 0.0 collective-permute-done.8.rest_1_
  73.8 3.1 %attend_parts.6 = (bf16[384,512]{1,0:T(8,128)(2,1)S(1)}, f32[32,128]{1,0:T(8,128)S(1)}, bf16[400,512]{1,0:T(8,128)(2,1)S(1)}, bf16[272,512]{1,0:T(8,128)(2,1)S(1)}) custom-call(s32[4]{0:T(128)S(1)} %copy-done.7, bf16[384,2048]{1,0:T(8,128)(2,1)S(1)} %copy-done, bf16[384,2048]{1,0:T(8,128)(2,1)} %k.9, bf16[384,2048]{1,0:T(8,128)(2,1)} %hyena_mix.1.v, ...), custom_call_target="tpu_custom_call" | custom-call | flops 1024 | bytes 1024 | tf_op jit(solution)/shard_map/attend_parts/pallas_call | solution.py:283
  76.9 0.0 copy-start.2
  76.9 1.4 %collective-permute-start.10 = (bf16[400,512]{1,0:T(8,128)(2,1)S(1)}, bf16[400,512]{1,0:T(8,128)(2,1)S(1)}, u32[]{:S(2)}, u32[]{:S(2)}) collective-permute-start(bf16[400,512]{1,0:T(8,128)(2,1)S(1)} %get-tuple-element.44), channel_id=1, source_target_pairs={{4,8},{8,12},{5,9},{9,13},{6,10},{10,14},{7,11},{11,15},{20,24},{2... | collective-permute-start | bytes 1228808 | tf_op jit(solution)/shard_map/ppermute | solution.py:379
  78.4 0.7 collective-permute-start.14
  79.1 0.8 collective-permute-done.18.rest_1_
  79.9 1.3 %collective-permute-start.11 = (bf16[272,512]{1,0:T(8,128)(2,1)S(1)}, bf16[272,512]{1,0:T(8,128)(2,1)S(1)}, u32[]{:S(2)}, u32[]{:S(2)}) collective-permute-start(bf16[272,512]{1,0:T(8,128)(2,1)S(1)} %get-tuple-element.45), channel_id=1, source_target_pairs={{4,12},{5,13},{6,14},{7,15},{20,28},{21,29},{22,30},{23,31}} | collective-permute-start | bytes 835592 | tf_op jit(solution)/shard_map/ppermute | solution.py:379
  81.2 1.9 %join_parts.5 = (bf16[384,2048]{1,0:T(8,128)(2,1)}, f32[8,128]{1,0:T(8,128)}) custom-call(bf16[384,512]{1,0:T(8,128)(2,1)S(1)} %get-tuple-element.46.o, f32[32,128]{1,0:T(8,128)S(1)} %get-tuple-element.41.s, bf16[400,512]{1,0:T(8,128)(2,1)S(1)} %collective-permute-done.5.rest_0_, bf16[272,512]{1,0:T(8,128)(2,1)S(1)} %collective-permute-done.6.rest_1_), custom_call_target="tpu_custom_call" | custom-call | flops 1024 | bytes 1024 | tf_op jit(solution)/shard_map/join_parts/pallas_call | solution.py:342
  83.1 5.5 %collective-permute-done.17.rest_0_ = bf16[400,512]{1,0:T(8,128)(2,1)S(1)} collective-permute-done((bf16[400,512]{1,0:T(8,128)(2,1)S(1)}, bf16[400,512]{1,0:T(8,128)(2,1)S(1)}, u32[]{:S(2)}, u32[]{:S(2)}) %collective-permute-start.17) | collective-permute-done | bytes 409632 | tf_op jit(solution)/shard_map/ppermute | solution.py:379
  88.6 2.1 %attend_parts.9 = (bf16[384,256]{1,0:T(8,128)(2,1)S(1)}, f32[16,128]{1,0:T(8,128)S(1)}, bf16[400,256]{1,0:T(8,128)(2,1)S(1)}, bf16[272,256]{1,0:T(8,128)(2,1)S(1)}) custom-call(s32[4]{0:T(128)S(1)} %copy-done.7, bf16[384,2048]{1,0:T(8,128)(2,1)S(1)} %copy-done, bf16[384,2048]{1,0:T(8,128)(2,1)S(1)} %copy-done.2, bf16[384,2048]{1,0:T(8,128)(2,1)} %hyena_mix.1.v, ...), custom_call_target="tpu_custom_call" | custom-call | flops 1024 | bytes 1024 | tf_op jit(solution)/shard_map/attend_parts/pallas_call | solution.py:283
  90.7 1.3 %collective-permute-start.20 = (bf16[400,256]{1,0:T(8,128)(2,1)S(1)}, bf16[400,256]{1,0:T(8,128)(2,1)S(1)}, u32[]{:S(2)}, u32[]{:S(2)}) collective-permute-start(bf16[400,256]{1,0:T(8,128)(2,1)S(1)} %get-tuple-element.62), channel_id=1, source_target_pairs={{4,8},{8,12},{5,9},{9,13},{6,10},{10,14},{7,11},{11,15},{20,24},{2... | collective-permute-start | bytes 614408 | tf_op jit(solution)/shard_map/ppermute | solution.py:379
  92.0 11.2 %collective-permute-done.11.rest_1_ = bf16[272,512]{1,0:T(8,128)(2,1)S(1)} collective-permute-done((bf16[272,512]{1,0:T(8,128)(2,1)S(1)}, bf16[272,512]{1,0:T(8,128)(2,1)S(1)}, u32[]{:S(2)}, u32[]{:S(2)}) %collective-permute-start.11) | collective-permute-done | bytes 278560 | tf_op jit(solution)/shard_map/ppermute | solution.py:379
  103.3 0.0 collective-permute-done.14.rest_2_.rest_3_
  103.3 1.9 %attend_parts.8 = (bf16[384,256]{1,0:T(8,128)(2,1)S(1)}, f32[16,128]{1,0:T(8,128)S(1)}, bf16[400,256]{1,0:T(8,128)(2,1)S(1)}, bf16[272,256]{1,0:T(8,128)(2,1)S(1)}) custom-call(s32[4]{0:T(128)S(1)} %copy-done.7, bf16[384,2048]{1,0:T(8,128)(2,1)S(1)} %copy-done, bf16[384,2048]{1,0:T(8,128)(2,1)S(1)} %copy-done.2, bf16[384,2048]{1,0:T(8,128)(2,1)} %hyena_mix.1.v, ...), custom_call_target="tpu_custom_call" | custom-call | flops 1024 | bytes 1024 | tf_op jit(solution)/shard_map/attend_parts/pallas_call | solution.py:283
  105.1 1.3 %collective-permute-start.15 = (bf16[400,256]{1,0:T(8,128)(2,1)S(1)}, bf16[400,256]{1,0:T(8,128)(2,1)S(1)}, u32[]{:S(2)}, u32[]{:S(2)}) collective-permute-start(bf16[400,256]{1,0:T(8,128)(2,1)S(1)} %get-tuple-element.54), channel_id=1, source_target_pairs={{4,8},{8,12},{5,9},{9,13},{6,10},{10,14},{7,11},{11,15},{20,24},{2... | collective-permute-start | bytes 614408 | tf_op jit(solution)/shard_map/ppermute | solution.py:379
  106.4 1.3 %collective-permute-start.21 = (bf16[272,256]{1,0:T(8,128)(2,1)S(1)}, bf16[272,256]{1,0:T(8,128)(2,1)S(1)}, u32[]{:S(2)}, u32[]{:S(2)}) collective-permute-start(bf16[272,256]{1,0:T(8,128)(2,1)S(1)} %get-tuple-element.63), channel_id=1, source_target_pairs={{4,12},{5,13},{6,14},{7,15},{20,28},{21,29},{22,30},{23,31}} | collective-permute-start | bytes 417800 | tf_op jit(solution)/shard_map/ppermute | solution.py:379
  107.7 1.3 %collective-permute-start.16 = (bf16[272,256]{1,0:T(8,128)(2,1)S(1)}, bf16[272,256]{1,0:T(8,128)(2,1)S(1)}, u32[]{:S(2)}, u32[]{:S(2)}) collective-permute-start(bf16[272,256]{1,0:T(8,128)(2,1)S(1)} %get-tuple-element.55), channel_id=1, source_target_pairs={{4,12},{5,13},{6,14},{7,15},{20,28},{21,29},{22,30},{23,31}} | collective-permute-start | bytes 417800 | tf_op jit(solution)/shard_map/ppermute | solution.py:379
  109.0 1.9 %join_parts.6 = (bf16[384,2048]{1,0:T(8,128)(2,1)}, f32[8,128]{1,0:T(8,128)}) custom-call(bf16[384,512]{1,0:T(8,128)(2,1)S(1)} %get-tuple-element.66.o, f32[32,128]{1,0:T(8,128)S(1)} %get-tuple-element.50.s, bf16[400,512]{1,0:T(8,128)(2,1)S(1)} %collective-permute-done.17.rest_0_, ...), custom_call_target="tpu_custom_call", output_to_operand_aliasing={{0}: (4, {})} | custom-call | flops 1024 | bytes 1024 | tf_op jit(solution)/shard_map/join_parts/pallas_call | solution.py:342
  111.0 1.9 %join_parts.7 = (bf16[384,2048]{1,0:T(8,128)(2,1)}, f32[8,128]{1,0:T(8,128)}) custom-call(bf16[384,512]{1,0:T(8,128)(2,1)S(1)} %get-tuple-element.64.o, f32[32,128]{1,0:T(8,128)S(1)} %get-tuple-element.65.s, bf16[400,512]{1,0:T(8,128)(2,1)S(1)} %collective-permute-done.10.rest_0_, ...), custom_call_target="tpu_custom_call", output_to_operand_aliasing={{0}: (4, {})} | custom-call | flops 1024 | bytes 1024 | tf_op jit(solution)/shard_map/join_parts/pallas_call | solution.py:342
  112.9 1.4 %collective-permute-done.21.rest_1_ = bf16[272,256]{1,0:T(8,128)(2,1)S(1)} collective-permute-done((bf16[272,256]{1,0:T(8,128)(2,1)S(1)}, bf16[272,256]{1,0:T(8,128)(2,1)S(1)}, u32[]{:S(2)}, u32[]{:S(2)}) %collective-permute-start.21) | collective-permute-done | bytes 139296 | tf_op jit(solution)/shard_map/ppermute | solution.py:379
  114.3 1.2 %join_parts.8 = (bf16[384,2048]{1,0:T(8,128)(2,1)}, f32[8,128]{1,0:T(8,128)}) custom-call(bf16[384,256]{1,0:T(8,128)(2,1)S(1)} %get-tuple-element.60.o, f32[16,128]{1,0:T(8,128)S(1)} %get-tuple-element.61.s, bf16[400,256]{1,0:T(8,128)(2,1)S(1)} %collective-permute-done.20.rest_0_, ...), custom_call_target="tpu_custom_call", output_to_operand_aliasing={{0}: (4, {})} | custom-call | flops 1024 | bytes 1024 | tf_op jit(solution)/shard_map/join_parts/pallas_call | solution.py:342
  115.5 0.2 collective-permute-done.16.rest_1_
  115.8 1.2 %join_parts.9 = (bf16[384,2048]{1,0:T(8,128)(2,1)}, f32[8,128]{1,0:T(8,128)}) custom-call(bf16[384,256]{1,0:T(8,128)(2,1)S(1)} %get-tuple-element.52.o, f32[16,128]{1,0:T(8,128)S(1)} %get-tuple-element.53.s, bf16[400,256]{1,0:T(8,128)(2,1)S(1)} %collective-permute-done.15.rest_0_, ...), custom_call_target="tpu_custom_call", output_to_operand_aliasing={{0}: (4, {})} | custom-call | flops 1024 | bytes 1024 | tf_op jit(solution)/shard_map/join_parts/pallas_call | solution.py:342
  (19 shorter events, 0.1 us)
Async XLA Ops:
  0.6 3.4 %copy-start = (bf16[384,2048]{1,0:T(8,128)(2,1)S(1)}, bf16[384,2048]{1,0:T(8,128)(2,1)}, u32[]{:S(2)}) copy-start(bf16[384,2048]{1,0:T(8,128)(2,1)} %q.9) | copy-start | bytes 4718596
  2.7 15.8 %collective-permute-start = (bf16[128,2048]{1,0:T(8,128)(2,1)}, bf16[128,2048]{1,0:T(8,128)(2,1)S(1)}, u32[]{:S(2)}, u32[]{:S(2)}) collective-permute-start(bf16[128,2048]{1,0:T(8,128)(2,1)} %halo_product.1), channel_id=1, source_target_pairs={{0,4},{4,8},{8,12},{1,5},{5,9},{9,13},{2,6},{6,10},{10,14},{3,7},{... | collective-permute-start | bytes 1572872 | tf_op jit(solution)/shard_map/ppermute | solution.py:379
  4.0 14.5 %copy-start.5 = (bf16[384,2048]{1,0:T(8,128)(2,1)S(1)}, bf16[384,2048]{1,0:T(8,128)(2,1)}, u32[]{:S(2)}) copy-start(bf16[384,2048]{1,0:T(8,128)(2,1)} %hq.1) | copy-start | bytes 4718596
  4.1 6.6 %copy-start.1 = (bf16[384,2048]{1,0:T(8,128)(2,1)S(1)}, bf16[384,2048]{1,0:T(8,128)(2,1)}, u32[]{:S(2)}) copy-start(bf16[384,2048]{1,0:T(8,128)(2,1)} %k.9) | copy-start | bytes 4718596
  4.1 28.8 %collective-permute-start.2 = (bf16[256,1024]{1,0:T(8,128)(2,1)S(1)}, bf16[256,1024]{1,0:T(8,128)(2,1)S(1)}, u32[]{:S(2)}, u32[]{:S(2)}) collective-permute-start(bf16[256,1024]{1,0:T(8,128)(2,1)S(1)} %get-tuple-element.83), channel_id=1, source_target_pairs={{12,4},{13,5},{14,6},{15,7},{28,20},{29,21},{30,22},{31,23}} | collective-permute-start | bytes 1572872 | tf_op jit(solution)/shard_map/ppermute | solution.py:379
  8.9 9.6 %copy-start.4 = (bf16[384,2048]{1,0:T(8,128)(2,1)S(1)}, bf16[384,2048]{1,0:T(8,128)(2,1)}, u32[]{:S(2)}) copy-start(bf16[384,2048]{1,0:T(8,128)(2,1)} %hv.3) | copy-start | bytes 4718596
  9.0 9.5 %copy-start.3 = (bf16[384,2048]{1,0:T(8,128)(2,1)S(1)}, bf16[384,2048]{1,0:T(8,128)(2,1)}, u32[]{:S(2)}) copy-start(bf16[384,2048]{1,0:T(8,128)(2,1)} %hk.3) | copy-start | bytes 4718596
  9.0 9.5 %copy-start.6 = (bf16[128,128]{1,0:T(8,128)(2,1)S(1)}, bf16[128,128]{1,0:T(8,128)(2,1)}, u32[]{:S(2)}) copy-start(bf16[128,128]{1,0:T(8,128)(2,1)} %filters.1) | copy-start | bytes 98308
  9.0 9.5 %copy-start.7 = (s32[4]{0:T(128)S(1)}, s32[4]{0:T(128)}, u32[]{:S(2)}) copy-start(s32[4]{0:T(128)} %info.8) | copy-start | bytes 52
  9.1 9.5 %copy-start.8 = (f32[2048]{0:T(1024)S(1)}, f32[2048]{0:T(1024)}, u32[]{:S(2)}) copy-start(f32[2048]{0:T(1024)} %param.12) | copy-start | bytes 24580
  9.1 29.0 %collective-permute-start.1 = (bf16[384,1024]{1,0:T(8,128)(2,1)S(1)}, bf16[384,1024]{1,0:T(8,128)(2,1)S(1)}, u32[]{:S(2)}, u32[]{:S(2)}) collective-permute-start(bf16[384,1024]{1,0:T(8,128)(2,1)S(1)} %get-tuple-element.85), channel_id=1, source_target_pairs={{8,4},{12,8},{9,5},{13,9},{10,6},{14,10},{11,7},{15,11},{24,20},{2... | collective-permute-start | bytes 2359304 | tf_op jit(solution)/shard_map/ppermute | solution.py:379
  10.8 21.4 %collective-permute-start.3 = (bf16[384,512]{1,0:T(8,128)(2,1)S(1)}, bf16[384,512]{1,0:T(8,128)(2,1)S(1)}, u32[]{:S(2)}, u32[]{:S(2)}) collective-permute-start(bf16[384,512]{1,0:T(8,128)(2,1)S(1)} %get-tuple-element.81), channel_id=1, source_target_pairs={{0,4},{1,5},{2,6},{3,7},{16,20},{17,21},{18,22},{19,23}} | collective-permute-start | bytes 1179656 | tf_op jit(solution)/shard_map/ppermute | solution.py:379
  30.8 7.3 %collective-permute-start.4 = (bf16[384,512]{1,0:T(8,128)(2,1)S(1)}, bf16[384,512]{1,0:T(8,128)(2,1)S(1)}, u32[]{:S(2)}, u32[]{:S(2)}) collective-permute-start(bf16[384,512]{1,0:T(8,128)(2,1)S(1)} %get-tuple-element.78), channel_id=1, source_target_pairs={{0,4},{1,5},{2,6},{3,7},{16,20},{17,21},{18,22},{19,23}} | collective-permute-start | bytes 1179656 | tf_op jit(solution)/shard_map/ppermute | solution.py:379
  31.5 11.6 %collective-permute-start.12 = (bf16[384,512]{1,0:T(8,128)(2,1)S(1)}, bf16[384,512]{1,0:T(8,128)(2,1)S(1)}, u32[]{:S(2)}, u32[]{:S(2)}) collective-permute-start(bf16[384,512]{1,0:T(8,128)(2,1)S(1)} %get-tuple-element.49), channel_id=1, source_target_pairs={{0,4},{1,5},{2,6},{3,7},{16,20},{17,21},{18,22},{19,23}} | collective-permute-start | bytes 1179656 | tf_op jit(solution)/shard_map/ppermute | solution.py:379
  32.2 12.2 %collective-permute-start.13 = (bf16[384,512]{1,0:T(8,128)(2,1)S(1)}, bf16[384,512]{1,0:T(8,128)(2,1)S(1)}, u32[]{:S(2)}, u32[]{:S(2)}) collective-permute-start(bf16[384,512]{1,0:T(8,128)(2,1)S(1)} %get-tuple-element.76), channel_id=1, source_target_pairs={{0,4},{1,5},{2,6},{3,7},{16,20},{17,21},{18,22},{19,23}} | collective-permute-start | bytes 1179656 | tf_op jit(solution)/shard_map/ppermute | solution.py:379
  33.0 39.5 %collective-permute-start.7 = (bf16[384,1024]{1,0:T(8,128)(2,1)S(1)}, bf16[384,1024]{1,0:T(8,128)(2,1)S(1)}, u32[]{:S(2)}, u32[]{:S(2)}) collective-permute-start(bf16[384,1024]{1,0:T(8,128)(2,1)S(1)} %get-tuple-element.40), channel_id=1, source_target_pairs={{8,4},{12,8},{9,5},{13,9},{10,6},{14,10},{11,7},{15,11},{24,20},{2... | collective-permute-start | bytes 2359304 | tf_op jit(solution)/shard_map/ppermute | solution.py:379
  41.1 32.7 %collective-permute-start.9 = (bf16[768,512]{1,0:T(8,128)(2,1)S(1)}, bf16[768,512]{1,0:T(8,128)(2,1)S(1)}, u32[]{:S(2)}, u32[]{:S(2)}) collective-permute-start(bf16[768,512]{1,0:T(8,128)(2,1)S(1)} %pad_maximum_fusion), channel_id=1, source_target_pairs={{0,4},{1,5},{2,6},{3,7},{16,20},{17,21},{18,22},{19,23}} | collective-permute-start | bytes 2359304 | tf_op jit(solution)/shard_map/ppermute | solution.py:379
  41.8 28.6 %collective-permute-start.6 = (bf16[272,512]{1,0:T(8,128)(2,1)S(1)}, bf16[272,512]{1,0:T(8,128)(2,1)S(1)}, u32[]{:S(2)}, u32[]{:S(2)}) collective-permute-start(bf16[272,512]{1,0:T(8,128)(2,1)S(1)} %get-tuple-element.38), channel_id=1, source_target_pairs={{4,12},{5,13},{6,14},{7,15},{20,28},{21,29},{22,30},{23,31}} | collective-permute-start | bytes 835592 | tf_op jit(solution)/shard_map/ppermute | solution.py:379
  43.1 28.6 %collective-permute-start.5 = (bf16[400,512]{1,0:T(8,128)(2,1)S(1)}, bf16[400,512]{1,0:T(8,128)(2,1)S(1)}, u32[]{:S(2)}, u32[]{:S(2)}) collective-permute-start(bf16[400,512]{1,0:T(8,128)(2,1)S(1)} %get-tuple-element.37), channel_id=1, source_target_pairs={{4,8},{8,12},{5,9},{9,13},{6,10},{10,14},{7,11},{11,15},{20,24},{2... | collective-permute-start | bytes 1228808 | tf_op jit(solution)/shard_map/ppermute | solution.py:379
  44.4 29.4 %collective-permute-start.8 = (bf16[256,1024]{1,0:T(8,128)(2,1)S(1)}, bf16[256,1024]{1,0:T(8,128)(2,1)S(1)}, u32[]{:S(2)}, u32[]{:S(2)}) collective-permute-start(bf16[256,1024]{1,0:T(8,128)(2,1)S(1)} %get-tuple-element.42), channel_id=1, source_target_pairs={{12,4},{13,5},{14,6},{15,7},{28,20},{29,21},{30,22},{31,23}} | collective-permute-start | bytes 1572872 | tf_op jit(solution)/shard_map/ppermute | solution.py:379
  70.4 9.4 %collective-permute-start.18 = (bf16[272,512]{1,0:T(8,128)(2,1)S(1)}, bf16[272,512]{1,0:T(8,128)(2,1)S(1)}, u32[]{:S(2)}, u32[]{:S(2)}) collective-permute-start(bf16[272,512]{1,0:T(8,128)(2,1)S(1)} %get-tuple-element.57), channel_id=1, source_target_pairs={{4,12},{5,13},{6,14},{7,15},{20,28},{21,29},{22,30},{23,31}} | collective-permute-start | bytes 835592 | tf_op jit(solution)/shard_map/ppermute | solution.py:379
  71.8 16.9 %collective-permute-start.19 = (bf16[768,256]{1,0:T(8,128)(2,1)S(1)}, bf16[768,256]{1,0:T(8,128)(2,1)S(1)}, u32[]{:S(2)}, u32[]{:S(2)}) collective-permute-start(bf16[768,256]{1,0:T(8,128)(2,1)S(1)} %pad_maximum_fusion.2), channel_id=1, source_target_pairs={{0,4},{1,5},{2,6},{3,7},{16,20},{17,21},{18,22},{19,23}} | collective-permute-start | bytes 1179656 | tf_op jit(solution)/shard_map/ppermute | solution.py:379
  72.5 16.1 %collective-permute-start.17 = (bf16[400,512]{1,0:T(8,128)(2,1)S(1)}, bf16[400,512]{1,0:T(8,128)(2,1)S(1)}, u32[]{:S(2)}, u32[]{:S(2)}) collective-permute-start(bf16[400,512]{1,0:T(8,128)(2,1)S(1)} %get-tuple-element.56), channel_id=1, source_target_pairs={{4,8},{8,12},{5,9},{9,13},{6,10},{10,14},{7,11},{11,15},{20,24},{2... | collective-permute-start | bytes 1228808 | tf_op jit(solution)/shard_map/ppermute | solution.py:379
  76.9 11.7 %copy-start.2 = (bf16[384,2048]{1,0:T(8,128)(2,1)S(1)}, bf16[384,2048]{1,0:T(8,128)(2,1)}, u32[]{:S(2)}) copy-start(bf16[384,2048]{1,0:T(8,128)(2,1)} %k.9) | copy-start | bytes 4718596
  76.9 26.4 %collective-permute-start.10 = (bf16[400,512]{1,0:T(8,128)(2,1)S(1)}, bf16[400,512]{1,0:T(8,128)(2,1)S(1)}, u32[]{:S(2)}, u32[]{:S(2)}) collective-permute-start(bf16[400,512]{1,0:T(8,128)(2,1)S(1)} %get-tuple-element.44), channel_id=1, source_target_pairs={{4,8},{8,12},{5,9},{9,13},{6,10},{10,14},{7,11},{11,15},{20,24},{2... | collective-permute-start | bytes 1228808 | tf_op jit(solution)/shard_map/ppermute | solution.py:379
  78.4 24.9 %collective-permute-start.14 = (bf16[768,256]{1,0:T(8,128)(2,1)S(1)}, bf16[768,256]{1,0:T(8,128)(2,1)S(1)}, u32[]{:S(2)}, u32[]{:S(2)}) collective-permute-start(bf16[768,256]{1,0:T(8,128)(2,1)S(1)} %pad_maximum_fusion.1), channel_id=1, source_target_pairs={{0,4},{1,5},{2,6},{3,7},{16,20},{17,21},{18,22},{19,23}} | collective-permute-start | bytes 1179656 | tf_op jit(solution)/shard_map/ppermute | solution.py:379
  79.9 23.4 %collective-permute-start.11 = (bf16[272,512]{1,0:T(8,128)(2,1)S(1)}, bf16[272,512]{1,0:T(8,128)(2,1)S(1)}, u32[]{:S(2)}, u32[]{:S(2)}) collective-permute-start(bf16[272,512]{1,0:T(8,128)(2,1)S(1)} %get-tuple-element.45), channel_id=1, source_target_pairs={{4,12},{5,13},{6,14},{7,15},{20,28},{21,29},{22,30},{23,31}} | collective-permute-start | bytes 835592 | tf_op jit(solution)/shard_map/ppermute | solution.py:379
  90.7 23.6 %collective-permute-start.20 = (bf16[400,256]{1,0:T(8,128)(2,1)S(1)}, bf16[400,256]{1,0:T(8,128)(2,1)S(1)}, u32[]{:S(2)}, u32[]{:S(2)}) collective-permute-start(bf16[400,256]{1,0:T(8,128)(2,1)S(1)} %get-tuple-element.62), channel_id=1, source_target_pairs={{4,8},{8,12},{5,9},{9,13},{6,10},{10,14},{7,11},{11,15},{20,24},{2... | collective-permute-start | bytes 614408 | tf_op jit(solution)/shard_map/ppermute | solution.py:379
  105.1 10.6 %collective-permute-start.15 = (bf16[400,256]{1,0:T(8,128)(2,1)S(1)}, bf16[400,256]{1,0:T(8,128)(2,1)S(1)}, u32[]{:S(2)}, u32[]{:S(2)}) collective-permute-start(bf16[400,256]{1,0:T(8,128)(2,1)S(1)} %get-tuple-element.54), channel_id=1, source_target_pairs={{4,8},{8,12},{5,9},{9,13},{6,10},{10,14},{7,11},{11,15},{20,24},{2... | collective-permute-start | bytes 614408 | tf_op jit(solution)/shard_map/ppermute | solution.py:379
  106.4 7.8 %collective-permute-start.21 = (bf16[272,256]{1,0:T(8,128)(2,1)S(1)}, bf16[272,256]{1,0:T(8,128)(2,1)S(1)}, u32[]{:S(2)}, u32[]{:S(2)}) collective-permute-start(bf16[272,256]{1,0:T(8,128)(2,1)S(1)} %get-tuple-element.63), channel_id=1, source_target_pairs={{4,12},{5,13},{6,14},{7,15},{20,28},{21,29},{22,30},{23,31}} | collective-permute-start | bytes 417800 | tf_op jit(solution)/shard_map/ppermute | solution.py:379
  107.7 8.0 %collective-permute-start.16 = (bf16[272,256]{1,0:T(8,128)(2,1)S(1)}, bf16[272,256]{1,0:T(8,128)(2,1)S(1)}, u32[]{:S(2)}, u32[]{:S(2)}) collective-permute-start(bf16[272,256]{1,0:T(8,128)(2,1)S(1)} %get-tuple-element.55), channel_id=1, source_target_pairs={{4,12},{5,13},{6,14},{7,15},{20,28},{21,29},{22,30},{23,31}} | collective-permute-start | bytes 417800 | tf_op jit(solution)/shard_map/ppermute | solution.py:379

commit v6 on v5

--- a/solution.py
+++ b/solution.py
@@ -405,7 +405,7 @@
             pair = jnp.concatenate([columns(k, first, end), columns(mix, first, end)])
             pair = send(after(pair, told[max(0, c - 3)]), plan.k)
             keys, values = (pair, 0), (pair, 0, 1)
-        ready = after(starts, *(came_back[c - 2] if c >= 2 else ()), *joined[: max(0, c - 2)])
+        ready = after(starts, *(came_back[c - 2] if c >= 2 else ()), *joined[: 2 if c >= 3 else 0])
         o, s, *parts = attend(
             plan, ready, q, k, mix, (qa, first - q_at), (qb, first - q_at), keys, values, first, many
         )

time: 119 us -> 117 us (0.983); the launches traced: 117 us -> 116 us
  no operation moved by 1% of the time
where the time goes in v6:
time: 117 us; the launch traced here: 116 us
  starting transfers between devices  48.7 us (42%)
  Pallas kernels  34.3 us (29%)
  waiting for transfers between devices  28.3 us (24%)
  local copies, waits for them, and re-layouts  3.77 us (3%)
    ppermute x22, starting transfers between devices, run_plan(): send = lambda x, pairs: lax.ppermute(x, 'ctx', pairs)  48.7 us
    ppermute x22, waiting for transfers between devices, run_plan(): send = lambda x, pairs: lax.ppermute(x, 'ctx', pairs)  28.3 us
    pallas_call x5, Pallas kernels, attend(): pl.pallas_call(partial(attend_kernel, starts.shape[0], plan), grid=(heads...  12.9 us
    pallas_call x1, Pallas kernels, hyena(): pl.pallas_call(partial(hyena_kernel, starts.shape[0], group), grid=(chann...  11 us
    pallas_call x5, Pallas kernels, join(): pl.pallas_call(partial(join_kernel, plan), grid=(wide // width,), in_spec...  8.28 us
    slice x6, local copies, waits for them, and re-layouts, run_plan(): columns = lambda x, first, end: x[:, first * HEAD_DIM:end * HEAD_DIM]  3.72 us
  transfers between devices with their start and end apart: 22, of which 7 were waited for; matrix products, arithmetic and copies ran while one was open for 3% of the time, Pallas kernels for 27%

profile of v6, /device:TPU:26, one launch (start us, length us, event | category | flops | bytes accessed | tf_op | source)
XLA Modules:
  0.0 116.2 jit_solution(12727961906437898509)
XLA Ops:
  0.6 2.1 %halo_product.1 = bf16[128,2048]{1,0:T(8,128)(2,1)} custom-call(bf16[384,2048]{1,0:T(8,128)(2,1)} %hk.3, bf16[384,2048]{1,0:T(8,128)(2,1)} %hv.3), custom_call_target="tpu_custom_call" | custom-call | flops 1024 | bytes 1024 | tf_op jit(solution)/shard_map/halo_product/pallas_call | solution.py:44
  2.7 1.3 %collective-permute-start = (bf16[128,2048]{1,0:T(8,128)(2,1)}, bf16[128,2048]{1,0:T(8,128)(2,1)S(1)}, u32[]{:S(2)}, u32[]{:S(2)}) collective-permute-start(bf16[128,2048]{1,0:T(8,128)(2,1)} %halo_product.1), channel_id=1, source_target_pairs={{0,4},{4,8},{8,12},{1,5},{5,9},{9,13},{2,6},{6,10},{10,14},{3,7},{... | collective-permute-start | bytes 1572872 | tf_op jit(solution)/shard_map/ppermute | solution.py:379
  4.0 0.0 copy-start.5
  4.0 0.1 fusion.4
  4.1 0.0 copy-start.1
  4.1 4.7 %collective-permute-start.2 = (bf16[256,1024]{1,0:T(8,128)(2,1)S(1)}, bf16[256,1024]{1,0:T(8,128)(2,1)S(1)}, u32[]{:S(2)}, u32[]{:S(2)}) collective-permute-start(bf16[256,1024]{1,0:T(8,128)(2,1)S(1)} %get-tuple-element.85), channel_id=1, source_target_pairs={{12,4},{13,5},{14,6},{15,7},{28,20},{29,21},{30,22},{31,23}} | collective-permute-start | bytes 1572872 | tf_op jit(solution)/shard_map/ppermute | solution.py:379
  8.9 0.0 copy-start.4
  8.9 0.1 fusion.5
  9.0 0.0 copy-start.3
  9.0 0.0 copy-start.6
  9.0 0.0 copy-start.7
  9.0 0.0 copy-start.8
  9.1 1.6 %collective-permute-start.1 = (bf16[384,1024]{1,0:T(8,128)(2,1)S(1)}, bf16[384,1024]{1,0:T(8,128)(2,1)S(1)}, u32[]{:S(2)}, u32[]{:S(2)}) collective-permute-start(bf16[384,1024]{1,0:T(8,128)(2,1)S(1)} %get-tuple-element.87), channel_id=1, source_target_pairs={{8,4},{12,8},{9,5},{13,9},{10,6},{14,10},{11,7},{15,11},{24,20},{2... | collective-permute-start | bytes 2359304 | tf_op jit(solution)/shard_map/ppermute | solution.py:379
  10.7 0.1 fusion.3
  10.8 0.7 collective-permute-start.3
  11.5 7.0 %collective-permute-done.halo = bf16[128,2048]{1,0:T(8,128)(2,1)S(1)} collective-permute-done((bf16[128,2048]{1,0:T(8,128)(2,1)}, bf16[128,2048]{1,0:T(8,128)(2,1)S(1)}, u32[]{:S(2)}, u32[]{:S(2)}) %collective-permute-start) | collective-permute-done | bytes 524320 | tf_op jit(solution)/shard_map/ppermute | solution.py:379
  18.5 11.0 %hyena_mix.1.v = bf16[384,2048]{1,0:T(8,128)(2,1)} custom-call(s32[4]{0:T(128)S(1)} %copy-done.7, bf16[384,2048]{1,0:T(8,128)(2,1)S(1)} %copy-done.5, bf16[384,2048]{1,0:T(8,128)(2,1)S(1)} %copy-done.3, bf16[384,2048]{1,0:T(8,128)(2,1)S(1)} %copy-done.4, bf16[128,2048]{1,0:T(8,128)(2,1)S(1)} %collective-permute-done.halo, bf16[128,128]{1,0:T(8,128)(2,1)S(1)} %copy-done.6, ...), custom_call_target="tpu_custom_call" | custom-call | flops 1024 | bytes 1024 | tf_op jit(solution)/shard_map/hyena_mix/pallas_call | solution.py:115
  29.5 1.3 %fusion.2 = (bf16[384,512]{1,0:T(8,128)(2,1)S(1)}, bf16[384,512]{1,0:T(8,128)(2,1)S(1)}, bf16[384,512]{1,0:T(8,128)(2,1)S(1)}) fusion(bf16[384,2048]{1,0:T(8,128)(2,1)} %hyena_mix.1.v), kind=kLoop, calls=%fused_computation.5 | loop fusion | bytes 2359296 | tf_op jit(solution)/shard_map/slice | solution.py:381
  30.8 0.7 collective-permute-start.4
  31.5 0.7 collective-permute-start.12
  32.2 0.7 collective-permute-start.13
  32.9 0.1 pad_maximum_fusion
  33.0 2.4 %collective-permute-start.7 = (bf16[384,1024]{1,0:T(8,128)(2,1)S(1)}, bf16[384,1024]{1,0:T(8,128)(2,1)S(1)}, u32[]{:S(2)}, u32[]{:S(2)}) collective-permute-start(bf16[384,1024]{1,0:T(8,128)(2,1)S(1)} %get-tuple-element.41), channel_id=1, source_target_pairs={{8,4},{12,8},{9,5},{13,9},{10,6},{14,10},{11,7},{15,11},{24,20},{2... | collective-permute-start | bytes 2359304 | tf_op jit(solution)/shard_map/ppermute | solution.py:379
  35.4 2.7 %collective-permute-done.1.rest_0_ = bf16[384,1024]{1,0:T(8,128)(2,1)S(1)} collective-permute-done((bf16[384,1024]{1,0:T(8,128)(2,1)S(1)}, bf16[384,1024]{1,0:T(8,128)(2,1)S(1)}, u32[]{:S(2)}, u32[]{:S(2)}) %collective-permute-start.1) | collective-permute-done | bytes 786464 | tf_op jit(solution)/shard_map/ppermute | solution.py:379
  38.1 3.0 %attend_parts.5 = (bf16[384,512]{1,0:T(8,128)(2,1)S(1)}, f32[32,128]{1,0:T(8,128)S(1)}, bf16[400,512]{1,0:T(8,128)(2,1)S(1)}, bf16[272,512]{1,0:T(8,128)(2,1)S(1)}) custom-call(s32[4]{0:T(128)S(1)} %copy-done.7, bf16[384,2048]{1,0:T(8,128)(2,1)S(1)} %copy-done, bf16[384,2048]{1,0:T(8,128)(2,1)} %k.9, bf16[384,2048]{1,0:T(8,128)(2,1)} %hyena_mix.1.v, ...), custom_call_target="tpu_custom_call" | custom-call | flops 1024 | bytes 1024 | tf_op jit(solution)/shard_map/attend_parts/pallas_call | solution.py:283
  41.1 0.7 collective-permute-start.9
  41.8 1.3 %collective-permute-start.6 = (bf16[272,512]{1,0:T(8,128)(2,1)S(1)}, bf16[272,512]{1,0:T(8,128)(2,1)S(1)}, u32[]{:S(2)}, u32[]{:S(2)}) collective-permute-start(bf16[272,512]{1,0:T(8,128)(2,1)S(1)} %get-tuple-element.39), channel_id=1, source_target_pairs={{4,12},{5,13},{6,14},{7,15},{20,28},{21,29},{22,30},{23,31}} | collective-permute-start | bytes 835592 | tf_op jit(solution)/shard_map/ppermute | solution.py:379
  43.1 0.0 collective-permute-done.12.rest_2_
  43.1 1.3 %collective-permute-start.5 = (bf16[400,512]{1,0:T(8,128)(2,1)S(1)}, bf16[400,512]{1,0:T(8,128)(2,1)S(1)}, u32[]{:S(2)}, u32[]{:S(2)}) collective-permute-start(bf16[400,512]{1,0:T(8,128)(2,1)S(1)} %get-tuple-element.38), channel_id=1, source_target_pairs={{4,8},{8,12},{5,9},{9,13},{6,10},{10,14},{7,11},{11,15},{20,24},{2... | collective-permute-start | bytes 1228808 | tf_op jit(solution)/shard_map/ppermute | solution.py:379
  44.4 0.0 collective-permute-done.13.rest_3_
  44.4 20.8 %collective-permute-start.8 = (bf16[256,1024]{1,0:T(8,128)(2,1)S(1)}, bf16[256,1024]{1,0:T(8,128)(2,1)S(1)}, u32[]{:S(2)}, u32[]{:S(2)}) collective-permute-start(bf16[256,1024]{1,0:T(8,128)(2,1)S(1)} %get-tuple-element.43), channel_id=1, source_target_pairs={{12,4},{13,5},{14,6},{15,7},{28,20},{29,21},{30,22},{31,23}} | collective-permute-start | bytes 1572872 | tf_op jit(solution)/shard_map/ppermute | solution.py:379
  65.2 1.1 fusion
  66.3 1.1 fusion.1
  67.3 3.1 %attend_parts.7 = (bf16[384,512]{1,0:T(8,128)(2,1)S(1)}, f32[32,128]{1,0:T(8,128)S(1)}, bf16[400,512]{1,0:T(8,128)(2,1)S(1)}, bf16[272,512]{1,0:T(8,128)(2,1)S(1)}) custom-call(s32[4]{0:T(128)S(1)} %copy-done.7, bf16[384,2048]{1,0:T(8,128)(2,1)S(1)} %copy-done, bf16[384,2048]{1,0:T(8,128)(2,1)} %k.9, bf16[384,2048]{1,0:T(8,128)(2,1)} %hyena_mix.1.v, ...), custom_call_target="tpu_custom_call" | custom-call | flops 1024 | bytes 1024 | tf_op jit(solution)/shard_map/attend_parts/pallas_call | solution.py:283
  70.4 0.0 collective-permute-done.6.rest_1_
  70.4 1.3 %collective-permute-start.15 = (bf16[272,512]{1,0:T(8,128)(2,1)S(1)}, bf16[272,512]{1,0:T(8,128)(2,1)S(1)}, u32[]{:S(2)}, u32[]{:S(2)}) collective-permute-start(bf16[272,512]{1,0:T(8,128)(2,1)S(1)} %get-tuple-element.53), channel_id=1, source_target_pairs={{4,12},{5,13},{6,14},{7,15},{20,28},{21,29},{22,30},{23,31}} | collective-permute-start | bytes 835592 | tf_op jit(solution)/shard_map/ppermute | solution.py:379
  71.8 0.0 collective-permute-done.5.rest_0_
  71.8 0.7 collective-permute-start.19
  72.5 1.3 %collective-permute-start.14 = (bf16[400,512]{1,0:T(8,128)(2,1)S(1)}, bf16[400,512]{1,0:T(8,128)(2,1)S(1)}, u32[]{:S(2)}, u32[]{:S(2)}) collective-permute-start(bf16[400,512]{1,0:T(8,128)(2,1)S(1)} %get-tuple-element.52), channel_id=1, source_target_pairs={{4,8},{8,12},{5,9},{9,13},{6,10},{10,14},{7,11},{11,15},{20,24},{2... | collective-permute-start | bytes 1228808 | tf_op jit(solution)/shard_map/ppermute | solution.py:379
  73.8 0.0 collective-permute-done.8.rest_1_
  73.8 0.0 collective-permute-done.9.rest_2_.rest_3_
  73.8 3.1 %attend_parts.6 = (bf16[384,512]{1,0:T(8,128)(2,1)S(1)}, f32[32,128]{1,0:T(8,128)S(1)}, bf16[400,512]{1,0:T(8,128)(2,1)S(1)}, bf16[272,512]{1,0:T(8,128)(2,1)S(1)}) custom-call(s32[4]{0:T(128)S(1)} %copy-done.7, bf16[384,2048]{1,0:T(8,128)(2,1)S(1)} %copy-done, bf16[384,2048]{1,0:T(8,128)(2,1)} %k.9, bf16[384,2048]{1,0:T(8,128)(2,1)} %hyena_mix.1.v, ...), custom_call_target="tpu_custom_call" | custom-call | flops 1024 | bytes 1024 | tf_op jit(solution)/shard_map/attend_parts/pallas_call | solution.py:283
  76.9 1.3 %collective-permute-start.10 = (bf16[400,512]{1,0:T(8,128)(2,1)S(1)}, bf16[400,512]{1,0:T(8,128)(2,1)S(1)}, u32[]{:S(2)}, u32[]{:S(2)}) collective-permute-start(bf16[400,512]{1,0:T(8,128)(2,1)S(1)} %get-tuple-element.45), channel_id=1, source_target_pairs={{4,8},{8,12},{5,9},{9,13},{6,10},{10,14},{7,11},{11,15},{20,24},{2... | collective-permute-start | bytes 1228808 | tf_op jit(solution)/shard_map/ppermute | solution.py:379
  78.2 0.7 collective-permute-start.16
  78.9 1.0 collective-permute-done.15.rest_1_
  79.9 1.5 %collective-permute-start.11 = (bf16[272,512]{1,0:T(8,128)(2,1)S(1)}, bf16[272,512]{1,0:T(8,128)(2,1)S(1)}, u32[]{:S(2)}, u32[]{:S(2)}) collective-permute-start(bf16[272,512]{1,0:T(8,128)(2,1)S(1)} %get-tuple-element.46), channel_id=1, source_target_pairs={{4,12},{5,13},{6,14},{7,15},{20,28},{21,29},{22,30},{23,31}} | collective-permute-start | bytes 835592 | tf_op jit(solution)/shard_map/ppermute | solution.py:379
  81.4 1.9 %join_parts.5 = (bf16[384,2048]{1,0:T(8,128)(2,1)}, f32[8,128]{1,0:T(8,128)}) custom-call(bf16[384,512]{1,0:T(8,128)(2,1)S(1)} %get-tuple-element.47.o, f32[32,128]{1,0:T(8,128)S(1)} %get-tuple-element.42.s, bf16[400,512]{1,0:T(8,128)(2,1)S(1)} %collective-permute-done.5.rest_0_, bf16[272,512]{1,0:T(8,128)(2,1)S(1)} %collective-permute-done.6.rest_1_), custom_call_target="tpu_custom_call" | custom-call | flops 1024 | bytes 1024 | tf_op jit(solution)/shard_map/join_parts/pallas_call | solution.py:342
  83.3 5.3 %collective-permute-done.14.rest_0_ = bf16[400,512]{1,0:T(8,128)(2,1)S(1)} collective-permute-done((bf16[400,512]{1,0:T(8,128)(2,1)S(1)}, bf16[400,512]{1,0:T(8,128)(2,1)S(1)}, u32[]{:S(2)}, u32[]{:S(2)}) %collective-permute-start.14) | collective-permute-done | bytes 409632 | tf_op jit(solution)/shard_map/ppermute | solution.py:379
  88.6 1.9 %join_parts.6 = (bf16[384,2048]{1,0:T(8,128)(2,1)}, f32[8,128]{1,0:T(8,128)}) custom-call(bf16[384,512]{1,0:T(8,128)(2,1)S(1)} %get-tuple-element.50.o, f32[32,128]{1,0:T(8,128)S(1)} %get-tuple-element.51.s, bf16[400,512]{1,0:T(8,128)(2,1)S(1)} %collective-permute-done.14.rest_0_, ...), custom_call_target="tpu_custom_call", output_to_operand_aliasing={{0}: (4, {})} | custom-call | flops 1024 | bytes 1024 | tf_op jit(solution)/shard_map/join_parts/pallas_call | solution.py:342
  90.6 1.9 %attend_parts.9 = (bf16[384,256]{1,0:T(8,128)(2,1)S(1)}, f32[16,128]{1,0:T(8,128)S(1)}, bf16[400,256]{1,0:T(8,128)(2,1)S(1)}, bf16[272,256]{1,0:T(8,128)(2,1)S(1)}) custom-call(s32[4]{0:T(128)S(1)} %copy-done.7, bf16[384,2048]{1,0:T(8,128)(2,1)S(1)} %copy-done, bf16[384,2048]{1,0:T(8,128)(2,1)S(1)} %copy-done.2, bf16[384,2048]{1,0:T(8,128)(2,1)} %hyena_mix.1.v, ...), custom_call_target="tpu_custom_call" | custom-call | flops 1024 | bytes 1024 | tf_op jit(solution)/shard_map/attend_parts/pallas_call | solution.py:283
  92.4 1.3 %collective-permute-start.20 = (bf16[400,256]{1,0:T(8,128)(2,1)S(1)}, bf16[400,256]{1,0:T(8,128)(2,1)S(1)}, u32[]{:S(2)}, u32[]{:S(2)}) collective-permute-start(bf16[400,256]{1,0:T(8,128)(2,1)S(1)} %get-tuple-element.66), channel_id=1, source_target_pairs={{4,8},{8,12},{5,9},{9,13},{6,10},{10,14},{7,11},{11,15},{20,24},{2... | collective-permute-start | bytes 614408 | tf_op jit(solution)/shard_map/ppermute | solution.py:379
  93.7 8.7 %collective-permute-done.11.rest_1_ = bf16[272,512]{1,0:T(8,128)(2,1)S(1)} collective-permute-done((bf16[272,512]{1,0:T(8,128)(2,1)S(1)}, bf16[272,512]{1,0:T(8,128)(2,1)S(1)}, u32[]{:S(2)}, u32[]{:S(2)}) %collective-permute-start.11) | collective-permute-done | bytes 278560 | tf_op jit(solution)/shard_map/ppermute | solution.py:379
  102.5 0.0 collective-permute-done.10.rest_0_
  102.5 0.0 collective-permute-done.16.rest_2_.rest_3_
  102.5 1.9 %attend_parts.8 = (bf16[384,256]{1,0:T(8,128)(2,1)S(1)}, f32[16,128]{1,0:T(8,128)S(1)}, bf16[400,256]{1,0:T(8,128)(2,1)S(1)}, bf16[272,256]{1,0:T(8,128)(2,1)S(1)}) custom-call(s32[4]{0:T(128)S(1)} %copy-done.7, bf16[384,2048]{1,0:T(8,128)(2,1)S(1)} %copy-done, bf16[384,2048]{1,0:T(8,128)(2,1)S(1)} %copy-done.2, bf16[384,2048]{1,0:T(8,128)(2,1)} %hyena_mix.1.v, ...), custom_call_target="tpu_custom_call" | custom-call | flops 1024 | bytes 1024 | tf_op jit(solution)/shard_map/attend_parts/pallas_call | solution.py:283
  104.3 1.3 %collective-permute-start.17 = (bf16[400,256]{1,0:T(8,128)(2,1)S(1)}, bf16[400,256]{1,0:T(8,128)(2,1)S(1)}, u32[]{:S(2)}, u32[]{:S(2)}) collective-permute-start(bf16[400,256]{1,0:T(8,128)(2,1)S(1)} %get-tuple-element.60), channel_id=1, source_target_pairs={{4,8},{8,12},{5,9},{9,13},{6,10},{10,14},{7,11},{11,15},{20,24},{2... | collective-permute-start | bytes 614408 | tf_op jit(solution)/shard_map/ppermute | solution.py:379
  105.6 1.3 %collective-permute-start.21 = (bf16[272,256]{1,0:T(8,128)(2,1)S(1)}, bf16[272,256]{1,0:T(8,128)(2,1)S(1)}, u32[]{:S(2)}, u32[]{:S(2)}) collective-permute-start(bf16[272,256]{1,0:T(8,128)(2,1)S(1)} %get-tuple-element.67), channel_id=1, source_target_pairs={{4,12},{5,13},{6,14},{7,15},{20,28},{21,29},{22,30},{23,31}} | collective-permute-start | bytes 417800 | tf_op jit(solution)/shard_map/ppermute | solution.py:379
  106.9 1.3 %collective-permute-start.18 = (bf16[272,256]{1,0:T(8,128)(2,1)S(1)}, bf16[272,256]{1,0:T(8,128)(2,1)S(1)}, u32[]{:S(2)}, u32[]{:S(2)}) collective-permute-start(bf16[272,256]{1,0:T(8,128)(2,1)S(1)} %get-tuple-element.61), channel_id=1, source_target_pairs={{4,12},{5,13},{6,14},{7,15},{20,28},{21,29},{22,30},{23,31}} | collective-permute-start | bytes 417800 | tf_op jit(solution)/shard_map/ppermute | solution.py:379
  108.2 1.9 %join_parts.7 = (bf16[384,2048]{1,0:T(8,128)(2,1)}, f32[8,128]{1,0:T(8,128)}) custom-call(bf16[384,512]{1,0:T(8,128)(2,1)S(1)} %get-tuple-element.68.o, f32[32,128]{1,0:T(8,128)S(1)} %get-tuple-element.69.s, bf16[400,512]{1,0:T(8,128)(2,1)S(1)} %collective-permute-done.10.rest_0_, ...), custom_call_target="tpu_custom_call", output_to_operand_aliasing={{0}: (4, {})} | custom-call | flops 1024 | bytes 1024 | tf_op jit(solution)/shard_map/join_parts/pallas_call | solution.py:342
  110.2 3.3 %collective-permute-done.21.rest_1_ = bf16[272,256]{1,0:T(8,128)(2,1)S(1)} collective-permute-done((bf16[272,256]{1,0:T(8,128)(2,1)S(1)}, bf16[272,256]{1,0:T(8,128)(2,1)S(1)}, u32[]{:S(2)}, u32[]{:S(2)}) %collective-permute-start.21) | collective-permute-done | bytes 139296 | tf_op jit(solution)/shard_map/ppermute | solution.py:379
  113.5 0.0 collective-permute-done.20.rest_0_
  113.5 1.2 %join_parts.8 = (bf16[384,2048]{1,0:T(8,128)(2,1)}, f32[8,128]{1,0:T(8,128)}) custom-call(bf16[384,256]{1,0:T(8,128)(2,1)S(1)} %get-tuple-element.64.o, f32[16,128]{1,0:T(8,128)S(1)} %get-tuple-element.65.s, bf16[400,256]{1,0:T(8,128)(2,1)S(1)} %collective-permute-done.20.rest_0_, ...), custom_call_target="tpu_custom_call", output_to_operand_aliasing={{0}: (4, {})} | custom-call | flops 1024 | bytes 1024 | tf_op jit(solution)/shard_map/join_parts/pallas_call | solution.py:342
  114.7 0.2 collective-permute-done.18.rest_1_
  115.0 1.2 %join_parts.9 = (bf16[384,2048]{1,0:T(8,128)(2,1)}, f32[8,128]{1,0:T(8,128)}) custom-call(bf16[384,256]{1,0:T(8,128)(2,1)S(1)} %get-tuple-element.58.o, f32[16,128]{1,0:T(8,128)S(1)} %get-tuple-element.59.s, bf16[400,256]{1,0:T(8,128)(2,1)S(1)} %collective-permute-done.17.rest_0_, ...), custom_call_target="tpu_custom_call", output_to_operand_aliasing={{0}: (4, {})} | custom-call | flops 1024 | bytes 1024 | tf_op jit(solution)/shard_map/join_parts/pallas_call | solution.py:342
  (19 shorter events, 0.1 us)
Async XLA Ops:
  0.6 3.4 %copy-start = (bf16[384,2048]{1,0:T(8,128)(2,1)S(1)}, bf16[384,2048]{1,0:T(8,128)(2,1)}, u32[]{:S(2)}) copy-start(bf16[384,2048]{1,0:T(8,128)(2,1)} %q.9) | copy-start | bytes 4718596
  2.7 15.8 %collective-permute-start = (bf16[128,2048]{1,0:T(8,128)(2,1)}, bf16[128,2048]{1,0:T(8,128)(2,1)S(1)}, u32[]{:S(2)}, u32[]{:S(2)}) collective-permute-start(bf16[128,2048]{1,0:T(8,128)(2,1)} %halo_product.1), channel_id=1, source_target_pairs={{0,4},{4,8},{8,12},{1,5},{5,9},{9,13},{2,6},{6,10},{10,14},{3,7},{... | collective-permute-start | bytes 1572872 | tf_op jit(solution)/shard_map/ppermute | solution.py:379
  4.0 14.5 %copy-start.5 = (bf16[384,2048]{1,0:T(8,128)(2,1)S(1)}, bf16[384,2048]{1,0:T(8,128)(2,1)}, u32[]{:S(2)}) copy-start(bf16[384,2048]{1,0:T(8,128)(2,1)} %hq.1) | copy-start | bytes 4718596
  4.1 6.6 %copy-start.1 = (bf16[384,2048]{1,0:T(8,128)(2,1)S(1)}, bf16[384,2048]{1,0:T(8,128)(2,1)}, u32[]{:S(2)}) copy-start(bf16[384,2048]{1,0:T(8,128)(2,1)} %k.9) | copy-start | bytes 4718596
  4.1 28.8 %collective-permute-start.2 = (bf16[256,1024]{1,0:T(8,128)(2,1)S(1)}, bf16[256,1024]{1,0:T(8,128)(2,1)S(1)}, u32[]{:S(2)}, u32[]{:S(2)}) collective-permute-start(bf16[256,1024]{1,0:T(8,128)(2,1)S(1)} %get-tuple-element.85), channel_id=1, source_target_pairs={{12,4},{13,5},{14,6},{15,7},{28,20},{29,21},{30,22},{31,23}} | collective-permute-start | bytes 1572872 | tf_op jit(solution)/shard_map/ppermute | solution.py:379
  8.9 9.6 %copy-start.4 = (bf16[384,2048]{1,0:T(8,128)(2,1)S(1)}, bf16[384,2048]{1,0:T(8,128)(2,1)}, u32[]{:S(2)}) copy-start(bf16[384,2048]{1,0:T(8,128)(2,1)} %hv.3) | copy-start | bytes 4718596
  9.0 9.5 %copy-start.3 = (bf16[384,2048]{1,0:T(8,128)(2,1)S(1)}, bf16[384,2048]{1,0:T(8,128)(2,1)}, u32[]{:S(2)}) copy-start(bf16[384,2048]{1,0:T(8,128)(2,1)} %hk.3) | copy-start | bytes 4718596
  9.0 9.5 %copy-start.6 = (bf16[128,128]{1,0:T(8,128)(2,1)S(1)}, bf16[128,128]{1,0:T(8,128)(2,1)}, u32[]{:S(2)}) copy-start(bf16[128,128]{1,0:T(8,128)(2,1)} %filters.1) | copy-start | bytes 98308
  9.0 9.5 %copy-start.7 = (s32[4]{0:T(128)S(1)}, s32[4]{0:T(128)}, u32[]{:S(2)}) copy-start(s32[4]{0:T(128)} %info.8) | copy-start | bytes 52
  9.0 9.5 %copy-start.8 = (f32[2048]{0:T(1024)S(1)}, f32[2048]{0:T(1024)}, u32[]{:S(2)}) copy-start(f32[2048]{0:T(1024)} %param.12) | copy-start | bytes 24580
  9.1 29.0 %collective-permute-start.1 = (bf16[384,1024]{1,0:T(8,128)(2,1)S(1)}, bf16[384,1024]{1,0:T(8,128)(2,1)S(1)}, u32[]{:S(2)}, u32[]{:S(2)}) collective-permute-start(bf16[384,1024]{1,0:T(8,128)(2,1)S(1)} %get-tuple-element.87), channel_id=1, source_target_pairs={{8,4},{12,8},{9,5},{13,9},{10,6},{14,10},{11,7},{15,11},{24,20},{2... | collective-permute-start | bytes 2359304 | tf_op jit(solution)/shard_map/ppermute | solution.py:379
  10.8 21.4 %collective-permute-start.3 = (bf16[384,512]{1,0:T(8,128)(2,1)S(1)}, bf16[384,512]{1,0:T(8,128)(2,1)S(1)}, u32[]{:S(2)}, u32[]{:S(2)}) collective-permute-start(bf16[384,512]{1,0:T(8,128)(2,1)S(1)} %get-tuple-element.83), channel_id=1, source_target_pairs={{0,4},{1,5},{2,6},{3,7},{16,20},{17,21},{18,22},{19,23}} | collective-permute-start | bytes 1179656 | tf_op jit(solution)/shard_map/ppermute | solution.py:379
  30.8 7.3 %collective-permute-start.4 = (bf16[384,512]{1,0:T(8,128)(2,1)S(1)}, bf16[384,512]{1,0:T(8,128)(2,1)S(1)}, u32[]{:S(2)}, u32[]{:S(2)}) collective-permute-start(bf16[384,512]{1,0:T(8,128)(2,1)S(1)} %get-tuple-element.80), channel_id=1, source_target_pairs={{0,4},{1,5},{2,6},{3,7},{16,20},{17,21},{18,22},{19,23}} | collective-permute-start | bytes 1179656 | tf_op jit(solution)/shard_map/ppermute | solution.py:379
  31.5 11.6 %collective-permute-start.12 = (bf16[384,512]{1,0:T(8,128)(2,1)S(1)}, bf16[384,512]{1,0:T(8,128)(2,1)S(1)}, u32[]{:S(2)}, u32[]{:S(2)}) collective-permute-start(bf16[384,512]{1,0:T(8,128)(2,1)S(1)} %get-tuple-element.49), channel_id=1, source_target_pairs={{0,4},{1,5},{2,6},{3,7},{16,20},{17,21},{18,22},{19,23}} | collective-permute-start | bytes 1179656 | tf_op jit(solution)/shard_map/ppermute | solution.py:379
  32.2 12.2 %collective-permute-start.13 = (bf16[384,512]{1,0:T(8,128)(2,1)S(1)}, bf16[384,512]{1,0:T(8,128)(2,1)S(1)}, u32[]{:S(2)}, u32[]{:S(2)}) collective-permute-start(bf16[384,512]{1,0:T(8,128)(2,1)S(1)} %get-tuple-element.78), channel_id=1, source_target_pairs={{0,4},{1,5},{2,6},{3,7},{16,20},{17,21},{18,22},{19,23}} | collective-permute-start | bytes 1179656 | tf_op jit(solution)/shard_map/ppermute | solution.py:379
  33.0 39.5 %collective-permute-start.7 = (bf16[384,1024]{1,0:T(8,128)(2,1)S(1)}, bf16[384,1024]{1,0:T(8,128)(2,1)S(1)}, u32[]{:S(2)}, u32[]{:S(2)}) collective-permute-start(bf16[384,1024]{1,0:T(8,128)(2,1)S(1)} %get-tuple-element.41), channel_id=1, source_target_pairs={{8,4},{12,8},{9,5},{13,9},{10,6},{14,10},{11,7},{15,11},{24,20},{2... | collective-permute-start | bytes 2359304 | tf_op jit(solution)/shard_map/ppermute | solution.py:379
  41.1 32.7 %collective-permute-start.9 = (bf16[768,512]{1,0:T(8,128)(2,1)S(1)}, bf16[768,512]{1,0:T(8,128)(2,1)S(1)}, u32[]{:S(2)}, u32[]{:S(2)}) collective-permute-start(bf16[768,512]{1,0:T(8,128)(2,1)S(1)} %pad_maximum_fusion), channel_id=1, source_target_pairs={{0,4},{1,5},{2,6},{3,7},{16,20},{17,21},{18,22},{19,23}} | collective-permute-start | bytes 2359304 | tf_op jit(solution)/shard_map/ppermute | solution.py:379
  41.8 28.6 %collective-permute-start.6 = (bf16[272,512]{1,0:T(8,128)(2,1)S(1)}, bf16[272,512]{1,0:T(8,128)(2,1)S(1)}, u32[]{:S(2)}, u32[]{:S(2)}) collective-permute-start(bf16[272,512]{1,0:T(8,128)(2,1)S(1)} %get-tuple-element.39), channel_id=1, source_target_pairs={{4,12},{5,13},{6,14},{7,15},{20,28},{21,29},{22,30},{23,31}} | collective-permute-start | bytes 835592 | tf_op jit(solution)/shard_map/ppermute | solution.py:379
  43.1 28.6 %collective-permute-start.5 = (bf16[400,512]{1,0:T(8,128)(2,1)S(1)}, bf16[400,512]{1,0:T(8,128)(2,1)S(1)}, u32[]{:S(2)}, u32[]{:S(2)}) collective-permute-start(bf16[400,512]{1,0:T(8,128)(2,1)S(1)} %get-tuple-element.38), channel_id=1, source_target_pairs={{4,8},{8,12},{5,9},{9,13},{6,10},{10,14},{7,11},{11,15},{20,24},{2... | collective-permute-start | bytes 1228808 | tf_op jit(solution)/shard_map/ppermute | solution.py:379
  44.4 29.4 %collective-permute-start.8 = (bf16[256,1024]{1,0:T(8,128)(2,1)S(1)}, bf16[256,1024]{1,0:T(8,128)(2,1)S(1)}, u32[]{:S(2)}, u32[]{:S(2)}) collective-permute-start(bf16[256,1024]{1,0:T(8,128)(2,1)S(1)} %get-tuple-element.43), channel_id=1, source_target_pairs={{12,4},{13,5},{14,6},{15,7},{28,20},{29,21},{30,22},{31,23}} | collective-permute-start | bytes 1572872 | tf_op jit(solution)/shard_map/ppermute | solution.py:379
  70.4 9.4 %collective-permute-start.15 = (bf16[272,512]{1,0:T(8,128)(2,1)S(1)}, bf16[272,512]{1,0:T(8,128)(2,1)S(1)}, u32[]{:S(2)}, u32[]{:S(2)}) collective-permute-start(bf16[272,512]{1,0:T(8,128)(2,1)S(1)} %get-tuple-element.53), channel_id=1, source_target_pairs={{4,12},{5,13},{6,14},{7,15},{20,28},{21,29},{22,30},{23,31}} | collective-permute-start | bytes 835592 | tf_op jit(solution)/shard_map/ppermute | solution.py:379
  71.8 18.8 %collective-permute-start.19 = (bf16[768,256]{1,0:T(8,128)(2,1)S(1)}, bf16[768,256]{1,0:T(8,128)(2,1)S(1)}, u32[]{:S(2)}, u32[]{:S(2)}) collective-permute-start(bf16[768,256]{1,0:T(8,128)(2,1)S(1)} %pad_maximum_fusion.2), channel_id=1, source_target_pairs={{0,4},{1,5},{2,6},{3,7},{16,20},{17,21},{18,22},{19,23}} | collective-permute-start | bytes 1179656 | tf_op jit(solution)/shard_map/ppermute | solution.py:379
  72.5 16.1 %collective-permute-start.14 = (bf16[400,512]{1,0:T(8,128)(2,1)S(1)}, bf16[400,512]{1,0:T(8,128)(2,1)S(1)}, u32[]{:S(2)}, u32[]{:S(2)}) collective-permute-start(bf16[400,512]{1,0:T(8,128)(2,1)S(1)} %get-tuple-element.52), channel_id=1, source_target_pairs={{4,8},{8,12},{5,9},{9,13},{6,10},{10,14},{7,11},{11,15},{20,24},{2... | collective-permute-start | bytes 1228808 | tf_op jit(solution)/shard_map/ppermute | solution.py:379
  76.9 25.6 %collective-permute-start.10 = (bf16[400,512]{1,0:T(8,128)(2,1)S(1)}, bf16[400,512]{1,0:T(8,128)(2,1)S(1)}, u32[]{:S(2)}, u32[]{:S(2)}) collective-permute-start(bf16[400,512]{1,0:T(8,128)(2,1)S(1)} %get-tuple-element.45), channel_id=1, source_target_pairs={{4,8},{8,12},{5,9},{9,13},{6,10},{10,14},{7,11},{11,15},{20,24},{2... | collective-permute-start | bytes 1228808 | tf_op jit(solution)/shard_map/ppermute | solution.py:379
  78.2 24.2 %collective-permute-start.16 = (bf16[768,256]{1,0:T(8,128)(2,1)S(1)}, bf16[768,256]{1,0:T(8,128)(2,1)S(1)}, u32[]{:S(2)}, u32[]{:S(2)}) collective-permute-start(bf16[768,256]{1,0:T(8,128)(2,1)S(1)} %pad_maximum_fusion.1), channel_id=1, source_target_pairs={{0,4},{1,5},{2,6},{3,7},{16,20},{17,21},{18,22},{19,23}} | collective-permute-start | bytes 1179656 | tf_op jit(solution)/shard_map/ppermute | solution.py:379
  79.9 22.6 %collective-permute-start.11 = (bf16[272,512]{1,0:T(8,128)(2,1)S(1)}, bf16[272,512]{1,0:T(8,128)(2,1)S(1)}, u32[]{:S(2)}, u32[]{:S(2)}) collective-permute-start(bf16[272,512]{1,0:T(8,128)(2,1)S(1)} %get-tuple-element.46), channel_id=1, source_target_pairs={{4,12},{5,13},{6,14},{7,15},{20,28},{21,29},{22,30},{23,31}} | collective-permute-start | bytes 835592 | tf_op jit(solution)/shard_map/ppermute | solution.py:379
  83.3 7.2 %copy-start.2 = (bf16[384,2048]{1,0:T(8,128)(2,1)S(1)}, bf16[384,2048]{1,0:T(8,128)(2,1)}, u32[]{:S(2)}) copy-start(bf16[384,2048]{1,0:T(8,128)(2,1)} %k.9) | copy-start | bytes 4718596
  92.4 21.1 %collective-permute-start.20 = (bf16[400,256]{1,0:T(8,128)(2,1)S(1)}, bf16[400,256]{1,0:T(8,128)(2,1)S(1)}, u32[]{:S(2)}, u32[]{:S(2)}) collective-permute-start(bf16[400,256]{1,0:T(8,128)(2,1)S(1)} %get-tuple-element.66), channel_id=1, source_target_pairs={{4,8},{8,12},{5,9},{9,13},{6,10},{10,14},{7,11},{11,15},{20,24},{2... | collective-permute-start | bytes 614408 | tf_op jit(solution)/shard_map/ppermute | solution.py:379
  104.3 10.6 %collective-permute-start.17 = (bf16[400,256]{1,0:T(8,128)(2,1)S(1)}, bf16[400,256]{1,0:T(8,128)(2,1)S(1)}, u32[]{:S(2)}, u32[]{:S(2)}) collective-permute-start(bf16[400,256]{1,0:T(8,128)(2,1)S(1)} %get-tuple-element.60), channel_id=1, source_target_pairs={{4,8},{8,12},{5,9},{9,13},{6,10},{10,14},{7,11},{11,15},{20,24},{2... | collective-permute-start | bytes 614408 | tf_op jit(solution)/shard_map/ppermute | solution.py:379
  105.6 7.8 %collective-permute-start.21 = (bf16[272,256]{1,0:T(8,128)(2,1)S(1)}, bf16[272,256]{1,0:T(8,128)(2,1)S(1)}, u32[]{:S(2)}, u32[]{:S(2)}) collective-permute-start(bf16[272,256]{1,0:T(8,128)(2,1)S(1)} %get-tuple-element.67), channel_id=1, source_target_pairs={{4,12},{5,13},{6,14},{7,15},{20,28},{21,29},{22,30},{23,31}} | collective-permute-start | bytes 417800 | tf_op jit(solution)/shard_map/ppermute | solution.py:379
  106.9 8.0 %collective-permute-start.18 = (bf16[272,256]{1,0:T(8,128)(2,1)S(1)}, bf16[272,256]{1,0:T(8,128)(2,1)S(1)}, u32[]{:S(2)}, u32[]{:S(2)}) collective-permute-start(bf16[272,256]{1,0:T(8,128)(2,1)S(1)} %get-tuple-element.61), channel_id=1, source_target_pairs={{4,12},{5,13},{6,14},{7,15},{20,28},{21,29},{22,30},{23,31}} | collective-permute-start | bytes 417800 | tf_op jit(solution)/shard_map/ppermute | solution.py:379
